TPU v7x, 128 devices: a whole 4x4x4 slice. The times are simulated.
128 devices in a mesh: blk: 16 (over y, z), sub: 8 (over x, core).
Axes of the slice: x: 4, y: 4, z: 4, core: 2. Of those that a mesh axis runs over, the one named last changes fastest.
Arguments:
- fields: float32 [4, 216, 32768], P(None, None, ('blk', 'sub')), may hold values from -6 to 6
- metric: float32 [32768], P(('blk', 'sub')), may hold values from 1 to 3
- neighbours: int32 [6, 32768], P(None, ('blk', 'sub')), may hold values from -2 to 32767, as said below
- mortar_sends: int32 [3, 65536], P(None, ('blk', 'sub')), may hold values from -1 to 127, as said below
- mortar_pairs: int32 [2, 32768], P(None, ('blk', 'sub')), may hold values from -1 to 511, as said below
Outputs:
- advanced: float32 [4, 216, 32768], P(None, None, ('blk', 'sub'))
Inputs may be any that keep to these rules, and one draw needn't show every extreme that they name: `neighbours`: element numbers run device by device, 256 to a device, devices blk-major. A neighbour across faces 0 and 1 lies on the same device or on the device before or after it along sub, across faces 2 and 3 on the same device or along blk, across faces 4 and 5 on the same device; an element named across face f names the first one back across face f xor 1. On each device and for each of faces 0 to 3, the elements whose neighbour lies on another device number 32, or zero where no device lies that way. Exactly 64 elements of each device have -2 on face 5 and 64 on face 4; -2 appears on no other face. `mortar_sends`: row 0 names one of the device's 2 * 64 interface faces, or -1 for an empty slot; rows 1 and 2 are 0 on empty slots and satisfy 0 <= lo < hi <= 16 on live ones. Device d's slots for owner o are the 4 columns from 2 * 256 d + 2 * 2 o on. Every interface face is named in exactly two live slots, whose intervals split [0, 16] in two. `mortar_pairs`: column 256 o + j is mortar slot j of owner o; both rows are -1 for an empty mortar slot. Every live send slot is named by exactly one mortar; the rotor entry names a slot carrying a rotor face, the stator entry one carrying a stator face, with intervals of equal length. Some owner has all 256 mortar slots live. The two slots of a mortar are partners; the live send slots of one device whose partners lie on one device (possibly itself) number at most 4, and some pair of devices has exactly 4.
All inputs are finite; a program needn't handle non-finite values.
Results may differ from a plain program's by a relative error of at most 0.00005.
Values sent between devices are 32-bit elements; how exact they have to be, the bound alone decides.
No kernel may reach another device: no remote copies, remote signals or barrier semaphores. Data moves between devices by JAX's collectives and lax.ppermute only.
A program may use at most 128 MiB of HBM per device.

v0:
```python
import jax
import jax.numpy as jnp
import numpy as np
from jax import lax
from jax.sharding import PartitionSpec as P

P_SIZE = 6
SUB = 16
IFD = 64
RIM = 32


DT_STEP = 0.01


def with_halo(cells, sides, width):
    for axis, dim in sides:
        count = lax.axis_size(axis)
        ends = count - 1
        head = lax.slice_in_dim(cells, 0, width, axis=dim)
        tail = lax.slice_in_dim(cells, cells.shape[dim] - width, cells.shape[dim], axis=dim)
        cells = jnp.concatenate(
            [
                lax.ppermute(tail, axis, [(i, (i + 1) % count) for i in range(ends)]),
                cells,
                lax.ppermute(head, axis, [((i + 1) % count, i) for i in range(ends)]),
            ],
            axis=dim,
        )
    return cells


def legendre_columns(points, npts):
    legendre = np.zeros((npts, npts))
    legendre[:, 0] = 1.0
    legendre[:, 1] = points
    for k in range(2, npts):
        legendre[:, k] = (
            (2 * k - 1) * points * legendre[:, k - 1] - (k - 1) * legendre[:, k - 2]
        ) / k
    return legendre


def basis_tables(npts):
    order = npts - 1
    points = -np.cos(np.pi * np.arange(npts) / order)
    for iteration in range(60):
        legendre = legendre_columns(points, npts)
        points = points - (points * legendre[:, order] - legendre[:, order - 1]) / (
            npts * legendre[:, order]
        )
    legendre = legendre_columns(points, npts)
    weights = 2.0 / (order * npts * legendre[:, order] ** 2)
    separation = points[:, None] - points[None, :] + np.eye(npts)
    derivative = legendre[:, order][:, None] / legendre[:, order][None, :] / separation
    derivative = derivative * (1.0 - np.eye(npts))
    derivative[0, 0] = -order * npts / 4.0
    derivative[order, order] = order * npts / 4.0
    return (points, weights, derivative)


def volume_operators(npts):
    points, weights, derivative = basis_tables(npts)
    single = np.eye(npts)
    square = np.eye(npts * npts)
    along_a = np.kron(derivative, square)
    along_b = np.kron(single, np.kron(derivative, single))
    along_c = np.kron(square, derivative)
    stacked = np.concatenate([along_a, along_b, along_c], axis=0)
    joined = np.concatenate([along_a, along_b, along_c], axis=1)
    return (stacked, joined)


def face_trace(field_cube, face_index):
    spot = 0 if face_index % 2 == 0 else field_cube.shape[1] - 1
    return lax.index_in_dim(field_cube, spot, 1 + face_index // 2, keepdims=False)


def place_face(surface, values, face_index):
    spot = 0 if face_index % 2 == 0 else surface.shape[1] - 1
    selector = [slice(None)] * 5
    selector[1 + face_index // 2] = spot
    return surface.at[tuple(selector)].add(values)


def normal_flux(trace, face_index):
    along = face_index // 2
    orient = 1.0 if face_index % 2 == 1 else -1.0
    blank = jnp.zeros_like(trace[0])
    parts = [blank, blank, blank, blank]
    parts[0] = orient * trace[1 + along]
    parts[1 + along] = orient * trace[0]
    return jnp.stack(parts)


def face_term(inside, outside, face_index):
    return 0.5 * (normal_flux(inside, face_index) - normal_flux(outside, face_index)) - 0.5 * (
        inside - outside
    )


def lagrange_rows(points, targets):
    rows_out = []
    for i in range(len(points)):
        product = jnp.ones_like(targets)
        for j in range(len(points)):
            if j != i:
                product = product * (targets - float(points[j])) / float(points[i] - points[j])
        rows_out.append(product)
    return jnp.stack(rows_out)


def mortar_points(points, lower, upper):
    unit = (jnp.asarray(points, jnp.float32)[:, None] + 1.0) * 0.5
    spots = lower[None, :] + (upper - lower)[None, :] * unit
    return spots * (2.0 / SUB) - 1.0


def to_mortar(flat, lower, upper, points):
    npts = len(points)
    slots = flat.shape[1]
    grid = flat.reshape(4, npts, npts, slots)
    basis = lagrange_rows(points, mortar_points(points, lower, upper))
    moved = jnp.einsum("ims,civs->cmvs", basis, grid, precision=lax.Precision.HIGHEST)
    return moved.reshape(4 * npts * npts, slots)


def from_mortar(flat, lower, upper, points, weights):
    npts = len(points)
    slots = flat.shape[1]
    grid = flat.reshape(4, npts, npts, slots)
    basis = lagrange_rows(points, mortar_points(points, lower, upper))
    scale = jnp.asarray(weights, jnp.float32)[:, None] * ((upper - lower) / SUB)[None, :]
    moved = jnp.einsum("ims,cmvs->civs", basis * scale[None], grid, precision=lax.Precision.HIGHEST)
    moved = moved / jnp.asarray(weights, jnp.float32)[None, :, None, None]
    return moved.reshape(4 * npts * npts, slots)


def mortar_flux(rotor_vals, stator_vals):
    cols = rotor_vals.shape[1]
    rotor_grid = rotor_vals.reshape(4, -1, cols)
    stator_grid = stator_vals.reshape(4, -1, cols)
    half_jump = 0.5 * (normal_flux(rotor_grid, 5) - normal_flux(stator_grid, 5))
    half_gap = 0.5 * (rotor_grid - stator_grid)
    return ((half_jump - half_gap).reshape(-1, cols), (half_jump + half_gap).reshape(-1, cols))


def route_out(payload):
    delivered = lax.all_to_all(payload, ("blk", "sub"), split_axis=1, concat_axis=1, tiled=True)
    return delivered


def route_back(payload):
    delivered = lax.all_to_all(payload, ("blk", "sub"), split_axis=1, concat_axis=1, tiled=True)
    return delivered


def per_device(fields, metric, neighbours, mortar_sends, mortar_pairs):
    node_count = fields.shape[1]
    elem_count = fields.shape[2]
    points, weights, derivative = basis_tables(P_SIZE)
    stacked_np, joined_np = volume_operators(P_SIZE)
    stacked = jnp.asarray(stacked_np, jnp.float32)
    joined = jnp.asarray(joined_np, jnp.float32)
    lift_scale = 1.0 / float(weights[0])
    row_count = 4 * P_SIZE * P_SIZE
    device = lax.axis_index(("blk", "sub"))
    local_ids = jnp.arange(elem_count, dtype=jnp.int32)
    first_id = device * elem_count
    lookups = []
    senders = []
    for face_index in range(6):
        target = neighbours[face_index]
        if face_index < 4:
            remote = (target >= 0) & (target // elem_count != device)
            far_local = jnp.where(remote, target % elem_count, 2 * elem_count)
            wanted = jnp.sort(far_local)[:RIM]
            position = jnp.minimum(jnp.searchsorted(wanted, target % elem_count), RIM - 1)
            senders.append(jnp.argsort(jnp.where(remote, local_ids, elem_count + local_ids))[:RIM])
            lookup = jnp.where(
                target < 0,
                elem_count + RIM,
                jnp.where(remote, elem_count + position, target - first_id),
            )
        else:
            lookup = jnp.where(target < 0, elem_count, target - first_id)
        lookups.append(lookup)
    rotor_elems = jnp.argsort(jnp.where(neighbours[5] == -2, local_ids, elem_count + local_ids))[
        :IFD
    ]
    stator_elems = jnp.argsort(jnp.where(neighbours[4] == -2, local_ids, elem_count + local_ids))[
        :IFD
    ]
    send_face = mortar_sends[0]
    send_live = (send_face >= 0).astype(jnp.float32)
    send_pick = jnp.maximum(send_face, 0)
    send_lo = mortar_sends[1].astype(jnp.float32)
    send_hi = mortar_sends[2].astype(jnp.float32)
    face_match = (send_face[:, None] == jnp.arange(2 * IFD, dtype=jnp.int32)[None, :]).astype(
        jnp.float32
    )
    slot_total = mortar_sends.shape[1]
    pair_live = mortar_pairs[0] >= 0
    rotor_pick = jnp.maximum(mortar_pairs[0], 0)
    stator_pick = jnp.maximum(mortar_pairs[1], 0)
    rotor_put = jnp.where(pair_live, mortar_pairs[0], slot_total)
    stator_put = jnp.where(pair_live, mortar_pairs[1], slot_total)

    def mortar_part(traces):
        both = jnp.concatenate(
            [jnp.take(traces[5], rotor_elems, axis=1), jnp.take(traces[4], stator_elems, axis=1)],
            axis=1,
        )
        sent = jnp.take(both, send_pick, axis=1) * send_live[None, :]
        outgoing = jnp.zeros((row_count, slot_total), jnp.float32)
        payload = jnp.concatenate([sent, send_lo[None, :], send_hi[None, :]], axis=0)
        arrived = route_out(payload)
        values = arrived[:row_count]
        rotor_lo = jnp.take(arrived[row_count], rotor_pick)
        rotor_hi = jnp.take(arrived[row_count + 1], rotor_pick)
        stator_lo = jnp.take(arrived[row_count], stator_pick)
        stator_hi = jnp.take(arrived[row_count + 1], stator_pick)
        rotor_in = to_mortar(jnp.take(values, rotor_pick, axis=1), rotor_lo, rotor_hi, points)
        stator_in = to_mortar(jnp.take(values, stator_pick, axis=1), stator_lo, stator_hi, points)
        rotor_flux, stator_flux = mortar_flux(rotor_in, stator_in)
        outgoing = outgoing.at[:, rotor_put].set(
            from_mortar(rotor_flux, rotor_lo, rotor_hi, points, weights), mode="drop"
        )
        outgoing = outgoing.at[:, stator_put].set(
            from_mortar(stator_flux, stator_lo, stator_hi, points, weights), mode="drop"
        )
        returned = route_back(outgoing)
        return jnp.dot(returned, face_match, precision=lax.Precision.HIGHEST)

    def time_rates(current):
        field_cube = current.reshape(4, P_SIZE, P_SIZE, P_SIZE, elem_count)
        traces = [face_trace(field_cube, f).reshape(row_count, elem_count) for f in range(6)]
        along_sub = jnp.stack(
            [jnp.take(traces[0], senders[0], axis=1), jnp.take(traces[1], senders[1], axis=1)]
        )
        along_blk = jnp.stack(
            [jnp.take(traces[2], senders[2], axis=1), jnp.take(traces[3], senders[3], axis=1)]
        )
        got_sub = with_halo(along_sub, (("sub", 0),), 1)
        got_blk = with_halo(along_blk, (("blk", 0),), 1)
        arrived_rims = [got_sub[0], got_sub[3], got_blk[0], got_blk[3]]
        interface = mortar_part(traces)
        gradient = jnp.dot(stacked, current[0], precision=lax.Precision.HIGHEST).reshape(
            3, node_count, elem_count
        )
        divergence = jnp.dot(
            joined, current[1:].reshape(3 * node_count, elem_count), precision=lax.Precision.HIGHEST
        )
        surface = jnp.zeros((4, P_SIZE, P_SIZE, P_SIZE, elem_count), jnp.float32)
        blank_col = jnp.zeros((row_count, 1), jnp.float32)
        for face_index in range(6):
            pieces = [traces[face_index ^ 1]]
            if face_index < 4:
                pieces.append(arrived_rims[face_index])
            pieces.append(blank_col)
            outside = jnp.take(jnp.concatenate(pieces, axis=1), lookups[face_index], axis=1)
            term = face_term(
                traces[face_index].reshape(4, P_SIZE, P_SIZE, elem_count),
                outside.reshape(4, P_SIZE, P_SIZE, elem_count),
                face_index,
            )
            if face_index >= 4:
                term = jnp.where(neighbours[face_index] == -2, 0.0, term)
            surface = place_face(surface, term, face_index)
        surface = surface.at[:, :, :, P_SIZE - 1, rotor_elems].add(
            interface[:, :IFD].reshape(4, P_SIZE, P_SIZE, IFD)
        )
        surface = surface.at[:, :, :, 0, stator_elems].add(
            interface[:, IFD:].reshape(4, P_SIZE, P_SIZE, IFD)
        )
        volume = jnp.concatenate([divergence[None], gradient], axis=0)
        return metric * (lift_scale * surface.reshape(4, node_count, elem_count) - volume)

    first_section = fields + DT_STEP * time_rates(fields)
    second_section = 0.75 * fields + 0.25 * (first_section + DT_STEP * time_rates(first_section))
    return fields / 3.0 + 2.0 / 3.0 * (second_section + DT_STEP * time_rates(second_section))


def solution(mesh):
    placed = (
        P(None, None, ("blk", "sub")),
        P(("blk", "sub")),
        P(None, ("blk", "sub")),
        P(None, ("blk", "sub")),
        P(None, ("blk", "sub")),
    )
    return jax.shard_map(
        per_device,
        mesh=mesh,
        in_specs=placed,
        out_specs=P(None, None, ("blk", "sub")),
        check_vma=False,
    )
```

profile of v0, /device:TPU:0, one launch (start us, length us, event | category | flops | bytes accessed | tf_op | source)
XLA Modules:
  0.0 1302.5 jit_solution(15710483024726471299)
XLA Ops:
  45.4 129.5 %while.81 = (s32[]{:T(128)}, u32[256]{0:T(256)S(1)}, u32[256]{0:T(256)S(1)}, s32[32]{0:T(128)S(1)}, s32[256]{0:T(256)S(1)}, /*index=5*/s32[]{:T(128)}, s32[]{:T(128)}) while((s32[]{:T(128)}, u32[256]{0:T(256)S(1)}, u32[256]{0:T(256)S(1)}, s32[32]{0:T(128)S(1)}, s32[256]{0:T(256)S(1)}, /*index=5*/s32[]{:T(128)}, s32[]{:T(128)}) %tuple.459), condition=%wide.region_3.5_spmd.clone, body=%wide.region_2.4_spmd.clone.sunk | while | flops 19203 | bytes 10200 | solution.py:178
  46.9 20.1 %fusion.323 = (u32[256]{0:T(256)S(1)}, pred[256]{0:T(512)(128)(4,1)S(1)}) fusion(u32[256]{0:T(256)S(1)} %get-tuple-element.1362, pred[]{:T(512)S(6)} %compare.4672, u32[256]{0:T(256)S(1)} %get-tuple-element.1361, s32[256]{0:T(256)S(1)} %get-tuple-element.1371, s32[]{:T(128)} %bitcast.582, s32[]{:T(128)} %bitcast.583, s32[]{:T(128)} %bitcast.584, ...), kind=kLoop, calls=%fused_computation.105.clone.1 | loop fusion | flops 17664 | bytes 4481 | tf_op jit(solution)/shard_map/jit(searchsorted)/jit(_searchsorted_scan_impl)/vmap(jit(_searchsorted_scan_impl))/while/body/eval_jaxpr/select_n | solution.py:178
  68.5 20.1 %fusion.323 = (u32[256]{0:T(256)S(1)}, pred[256]{0:T(512)(128)(4,1)S(1)}) fusion(u32[256]{0:T(256)S(1)} %get-tuple-element.1362, pred[]{:T(512)S(6)} %compare.4672, u32[256]{0:T(256)S(1)} %get-tuple-element.1361, s32[256]{0:T(256)S(1)} %get-tuple-element.1371, s32[]{:T(128)} %bitcast.582, s32[]{:T(128)} %bitcast.583, s32[]{:T(128)} %bitcast.584, ...), kind=kLoop, calls=%fused_computation.105.clone.1 | loop fusion | flops 17664 | bytes 4481 | tf_op jit(solution)/shard_map/jit(searchsorted)/jit(_searchsorted_scan_impl)/vmap(jit(_searchsorted_scan_impl))/while/body/eval_jaxpr/select_n | solution.py:178
  90.1 20.1 %fusion.323 = (u32[256]{0:T(256)S(1)}, pred[256]{0:T(512)(128)(4,1)S(1)}) fusion(u32[256]{0:T(256)S(1)} %get-tuple-element.1362, pred[]{:T(512)S(6)} %compare.4672, u32[256]{0:T(256)S(1)} %get-tuple-element.1361, s32[256]{0:T(256)S(1)} %get-tuple-element.1371, s32[]{:T(128)} %bitcast.582, s32[]{:T(128)} %bitcast.583, s32[]{:T(128)} %bitcast.584, ...), kind=kLoop, calls=%fused_computation.105.clone.1 | loop fusion | flops 17664 | bytes 4481 | tf_op jit(solution)/shard_map/jit(searchsorted)/jit(_searchsorted_scan_impl)/vmap(jit(_searchsorted_scan_impl))/while/body/eval_jaxpr/select_n | solution.py:178
  111.7 20.1 %fusion.323 = (u32[256]{0:T(256)S(1)}, pred[256]{0:T(512)(128)(4,1)S(1)}) fusion(u32[256]{0:T(256)S(1)} %get-tuple-element.1362, pred[]{:T(512)S(6)} %compare.4672, u32[256]{0:T(256)S(1)} %get-tuple-element.1361, s32[256]{0:T(256)S(1)} %get-tuple-element.1371, s32[]{:T(128)} %bitcast.582, s32[]{:T(128)} %bitcast.583, s32[]{:T(128)} %bitcast.584, ...), kind=kLoop, calls=%fused_computation.105.clone.1 | loop fusion | flops 17664 | bytes 4481 | tf_op jit(solution)/shard_map/jit(searchsorted)/jit(_searchsorted_scan_impl)/vmap(jit(_searchsorted_scan_impl))/while/body/eval_jaxpr/select_n | solution.py:178
  133.3 20.1 %fusion.323 = (u32[256]{0:T(256)S(1)}, pred[256]{0:T(512)(128)(4,1)S(1)}) fusion(u32[256]{0:T(256)S(1)} %get-tuple-element.1362, pred[]{:T(512)S(6)} %compare.4672, u32[256]{0:T(256)S(1)} %get-tuple-element.1361, s32[256]{0:T(256)S(1)} %get-tuple-element.1371, s32[]{:T(128)} %bitcast.582, s32[]{:T(128)} %bitcast.583, s32[]{:T(128)} %bitcast.584, ...), kind=kLoop, calls=%fused_computation.105.clone.1 | loop fusion | flops 17664 | bytes 4481 | tf_op jit(solution)/shard_map/jit(searchsorted)/jit(_searchsorted_scan_impl)/vmap(jit(_searchsorted_scan_impl))/while/body/eval_jaxpr/select_n | solution.py:178
  154.8 20.1 %fusion.323 = (u32[256]{0:T(256)S(1)}, pred[256]{0:T(512)(128)(4,1)S(1)}) fusion(u32[256]{0:T(256)S(1)} %get-tuple-element.1362, pred[]{:T(512)S(6)} %compare.4672, u32[256]{0:T(256)S(1)} %get-tuple-element.1361, s32[256]{0:T(256)S(1)} %get-tuple-element.1371, s32[]{:T(128)} %bitcast.582, s32[]{:T(128)} %bitcast.583, s32[]{:T(128)} %bitcast.584, ...), kind=kLoop, calls=%fused_computation.105.clone.1 | loop fusion | flops 17664 | bytes 4481 | tf_op jit(solution)/shard_map/jit(searchsorted)/jit(_searchsorted_scan_impl)/vmap(jit(_searchsorted_scan_impl))/while/body/eval_jaxpr/select_n | solution.py:178
  178.8 129.5 %while.83 = (s32[]{:T(128)}, u32[256]{0:T(256)S(1)}, u32[256]{0:T(256)S(1)}, s32[32]{0:T(128)S(1)}, s32[256]{0:T(256)S(1)}, /*index=5*/s32[]{:T(128)}, s32[]{:T(128)}) while((s32[]{:T(128)}, u32[256]{0:T(256)S(1)}, u32[256]{0:T(256)S(1)}, s32[32]{0:T(128)S(1)}, s32[256]{0:T(256)S(1)}, /*index=5*/s32[]{:T(128)}, ...), condition=%wide.region_11.14_spmd.clone, body=%wide.region_10.13_spmd.clone.sunk | while | flops 19203 | bytes 10200 | solution.py:178
  180.2 20.1 %fusion.331 = (u32[256]{0:T(256)S(1)}, pred[256]{0:T(512)(128)(4,1)S(1)}) fusion(u32[256]{0:T(256)S(1)} %get-tuple-element.1383, pred[]{:T(512)S(6)} %compare.4674, u32[256]{0:T(256)S(1)} %get-tuple-element.1382, s32[256]{0:T(256)S(1)} %get-tuple-element.1392, s32[]{:T(128)} %bitcast.646, s32[]{:T(128)} %bitcast.647, s32[]{:T(128)} %bitcast.648, ...), kind=kLoop, calls=%fused_computation.179.clone.1 | loop fusion | flops 17664 | bytes 4481 | tf_op jit(solution)/shard_map/jit(searchsorted)/jit(_searchsorted_scan_impl)/vmap(jit(_searchsorted_scan_impl))/while/body/eval_jaxpr/select_n | solution.py:178
  201.8 20.1 %fusion.331 = (u32[256]{0:T(256)S(1)}, pred[256]{0:T(512)(128)(4,1)S(1)}) fusion(u32[256]{0:T(256)S(1)} %get-tuple-element.1383, pred[]{:T(512)S(6)} %compare.4674, u32[256]{0:T(256)S(1)} %get-tuple-element.1382, s32[256]{0:T(256)S(1)} %get-tuple-element.1392, s32[]{:T(128)} %bitcast.646, s32[]{:T(128)} %bitcast.647, s32[]{:T(128)} %bitcast.648, ...), kind=kLoop, calls=%fused_computation.179.clone.1 | loop fusion | flops 17664 | bytes 4481 | tf_op jit(solution)/shard_map/jit(searchsorted)/jit(_searchsorted_scan_impl)/vmap(jit(_searchsorted_scan_impl))/while/body/eval_jaxpr/select_n | solution.py:178
  223.4 20.1 %fusion.331 = (u32[256]{0:T(256)S(1)}, pred[256]{0:T(512)(128)(4,1)S(1)}) fusion(u32[256]{0:T(256)S(1)} %get-tuple-element.1383, pred[]{:T(512)S(6)} %compare.4674, u32[256]{0:T(256)S(1)} %get-tuple-element.1382, s32[256]{0:T(256)S(1)} %get-tuple-element.1392, s32[]{:T(128)} %bitcast.646, s32[]{:T(128)} %bitcast.647, s32[]{:T(128)} %bitcast.648, ...), kind=kLoop, calls=%fused_computation.179.clone.1 | loop fusion | flops 17664 | bytes 4481 | tf_op jit(solution)/shard_map/jit(searchsorted)/jit(_searchsorted_scan_impl)/vmap(jit(_searchsorted_scan_impl))/while/body/eval_jaxpr/select_n | solution.py:178
  245.0 20.1 %fusion.331 = (u32[256]{0:T(256)S(1)}, pred[256]{0:T(512)(128)(4,1)S(1)}) fusion(u32[256]{0:T(256)S(1)} %get-tuple-element.1383, pred[]{:T(512)S(6)} %compare.4674, u32[256]{0:T(256)S(1)} %get-tuple-element.1382, s32[256]{0:T(256)S(1)} %get-tuple-element.1392, s32[]{:T(128)} %bitcast.646, s32[]{:T(128)} %bitcast.647, s32[]{:T(128)} %bitcast.648, ...), kind=kLoop, calls=%fused_computation.179.clone.1 | loop fusion | flops 17664 | bytes 4481 | tf_op jit(solution)/shard_map/jit(searchsorted)/jit(_searchsorted_scan_impl)/vmap(jit(_searchsorted_scan_impl))/while/body/eval_jaxpr/select_n | solution.py:178
  266.6 20.1 %fusion.331 = (u32[256]{0:T(256)S(1)}, pred[256]{0:T(512)(128)(4,1)S(1)}) fusion(u32[256]{0:T(256)S(1)} %get-tuple-element.1383, pred[]{:T(512)S(6)} %compare.4674, u32[256]{0:T(256)S(1)} %get-tuple-element.1382, s32[256]{0:T(256)S(1)} %get-tuple-element.1392, s32[]{:T(128)} %bitcast.646, s32[]{:T(128)} %bitcast.647, s32[]{:T(128)} %bitcast.648, ...), kind=kLoop, calls=%fused_computation.179.clone.1 | loop fusion | flops 17664 | bytes 4481 | tf_op jit(solution)/shard_map/jit(searchsorted)/jit(_searchsorted_scan_impl)/vmap(jit(_searchsorted_scan_impl))/while/body/eval_jaxpr/select_n | solution.py:178
  288.2 20.1 %fusion.331 = (u32[256]{0:T(256)S(1)}, pred[256]{0:T(512)(128)(4,1)S(1)}) fusion(u32[256]{0:T(256)S(1)} %get-tuple-element.1383, pred[]{:T(512)S(6)} %compare.4674, u32[256]{0:T(256)S(1)} %get-tuple-element.1382, s32[256]{0:T(256)S(1)} %get-tuple-element.1392, s32[]{:T(128)} %bitcast.646, s32[]{:T(128)} %bitcast.647, s32[]{:T(128)} %bitcast.648, ...), kind=kLoop, calls=%fused_computation.179.clone.1 | loop fusion | flops 17664 | bytes 4481 | tf_op jit(solution)/shard_map/jit(searchsorted)/jit(_searchsorted_scan_impl)/vmap(jit(_searchsorted_scan_impl))/while/body/eval_jaxpr/select_n | solution.py:178
  311.6 129.9 %while.82 = (s32[]{:T(128)}, u32[256]{0:T(256)S(1)}, u32[256]{0:T(256)S(1)}, s32[32]{0:T(128)S(1)}, s32[256]{0:T(256)S(1)}, /*index=5*/s32[]{:T(128)}, s32[]{:T(128)}) while((s32[]{:T(128)}, u32[256]{0:T(256)S(1)}, u32[256]{0:T(256)S(1)}, s32[32]{0:T(128)S(1)}, s32[256]{0:T(256)S(1)}, /*index=5*/s32[]{:T(128)}, s32[]{:T(128)}) %tuple.465), condition=%wide.region_7.10_spmd.clone, body=%wide.region_6.9_spmd.clone.sunk | while | flops 19203 | bytes 10200 | solution.py:178
  313.0 20.1 %fusion.327 = (u32[256]{0:T(256)S(1)}, pred[256]{0:T(512)(128)(4,1)S(1)}) fusion(u32[256]{0:T(256)S(1)} %get-tuple-element.1404, pred[]{:T(512)S(6)} %compare.4673, u32[256]{0:T(256)S(1)} %get-tuple-element.1403, s32[256]{0:T(256)S(1)} %get-tuple-element.1413, s32[]{:T(128)} %bitcast.614, s32[]{:T(128)} %bitcast.615, s32[]{:T(128)} %bitcast.616, ...), kind=kLoop, calls=%fused_computation.142.clone.1 | loop fusion | flops 17664 | bytes 4481 | tf_op jit(solution)/shard_map/jit(searchsorted)/jit(_searchsorted_scan_impl)/vmap(jit(_searchsorted_scan_impl))/while/body/eval_jaxpr/select_n | solution.py:178
  334.7 20.1 %fusion.327 = (u32[256]{0:T(256)S(1)}, pred[256]{0:T(512)(128)(4,1)S(1)}) fusion(u32[256]{0:T(256)S(1)} %get-tuple-element.1404, pred[]{:T(512)S(6)} %compare.4673, u32[256]{0:T(256)S(1)} %get-tuple-element.1403, s32[256]{0:T(256)S(1)} %get-tuple-element.1413, s32[]{:T(128)} %bitcast.614, s32[]{:T(128)} %bitcast.615, s32[]{:T(128)} %bitcast.616, ...), kind=kLoop, calls=%fused_computation.142.clone.1 | loop fusion | flops 17664 | bytes 4481 | tf_op jit(solution)/shard_map/jit(searchsorted)/jit(_searchsorted_scan_impl)/vmap(jit(_searchsorted_scan_impl))/while/body/eval_jaxpr/select_n | solution.py:178
  356.3 20.1 %fusion.327 = (u32[256]{0:T(256)S(1)}, pred[256]{0:T(512)(128)(4,1)S(1)}) fusion(u32[256]{0:T(256)S(1)} %get-tuple-element.1404, pred[]{:T(512)S(6)} %compare.4673, u32[256]{0:T(256)S(1)} %get-tuple-element.1403, s32[256]{0:T(256)S(1)} %get-tuple-element.1413, s32[]{:T(128)} %bitcast.614, s32[]{:T(128)} %bitcast.615, s32[]{:T(128)} %bitcast.616, ...), kind=kLoop, calls=%fused_computation.142.clone.1 | loop fusion | flops 17664 | bytes 4481 | tf_op jit(solution)/shard_map/jit(searchsorted)/jit(_searchsorted_scan_impl)/vmap(jit(_searchsorted_scan_impl))/while/body/eval_jaxpr/select_n | solution.py:178
  378.0 20.1 %fusion.327 = (u32[256]{0:T(256)S(1)}, pred[256]{0:T(512)(128)(4,1)S(1)}) fusion(u32[256]{0:T(256)S(1)} %get-tuple-element.1404, pred[]{:T(512)S(6)} %compare.4673, u32[256]{0:T(256)S(1)} %get-tuple-element.1403, s32[256]{0:T(256)S(1)} %get-tuple-element.1413, s32[]{:T(128)} %bitcast.614, s32[]{:T(128)} %bitcast.615, s32[]{:T(128)} %bitcast.616, ...), kind=kLoop, calls=%fused_computation.142.clone.1 | loop fusion | flops 17664 | bytes 4481 | tf_op jit(solution)/shard_map/jit(searchsorted)/jit(_searchsorted_scan_impl)/vmap(jit(_searchsorted_scan_impl))/while/body/eval_jaxpr/select_n | solution.py:178
  399.6 20.1 %fusion.327 = (u32[256]{0:T(256)S(1)}, pred[256]{0:T(512)(128)(4,1)S(1)}) fusion(u32[256]{0:T(256)S(1)} %get-tuple-element.1404, pred[]{:T(512)S(6)} %compare.4673, u32[256]{0:T(256)S(1)} %get-tuple-element.1403, s32[256]{0:T(256)S(1)} %get-tuple-element.1413, s32[]{:T(128)} %bitcast.614, s32[]{:T(128)} %bitcast.615, s32[]{:T(128)} %bitcast.616, ...), kind=kLoop, calls=%fused_computation.142.clone.1 | loop fusion | flops 17664 | bytes 4481 | tf_op jit(solution)/shard_map/jit(searchsorted)/jit(_searchsorted_scan_impl)/vmap(jit(_searchsorted_scan_impl))/while/body/eval_jaxpr/select_n | solution.py:178
  421.3 20.1 %fusion.327 = (u32[256]{0:T(256)S(1)}, pred[256]{0:T(512)(128)(4,1)S(1)}) fusion(u32[256]{0:T(256)S(1)} %get-tuple-element.1404, pred[]{:T(512)S(6)} %compare.4673, u32[256]{0:T(256)S(1)} %get-tuple-element.1403, s32[256]{0:T(256)S(1)} %get-tuple-element.1413, s32[]{:T(128)} %bitcast.614, s32[]{:T(128)} %bitcast.615, s32[]{:T(128)} %bitcast.616, ...), kind=kLoop, calls=%fused_computation.142.clone.1 | loop fusion | flops 17664 | bytes 4481 | tf_op jit(solution)/shard_map/jit(searchsorted)/jit(_searchsorted_scan_impl)/vmap(jit(_searchsorted_scan_impl))/while/body/eval_jaxpr/select_n | solution.py:178
  445.3 129.4 %while.84 = (s32[]{:T(128)}, u32[256]{0:T(256)S(1)}, u32[256]{0:T(256)S(1)}, s32[32]{0:T(128)S(1)}, s32[256]{0:T(256)S(1)}, /*index=5*/s32[]{:T(128)}, s32[]{:T(128)}) while((s32[]{:T(128)}, u32[256]{0:T(256)S(1)}, u32[256]{0:T(256)S(1)}, s32[32]{0:T(128)S(1)}, s32[256]{0:T(256)S(1)}, /*index=5*/s32[]{:T(128)}, ...), condition=%wide.region_15.18_spmd.clone, body=%wide.region_14.17_spmd.clone.sunk | while | flops 19203 | bytes 10200 | solution.py:178
  446.8 20.1 %fusion.335 = (u32[256]{0:T(256)S(1)}, pred[256]{0:T(512)(128)(4,1)S(1)}) fusion(u32[256]{0:T(256)S(1)} %copy.1606, pred[]{:T(512)S(6)} %compare.4675, u32[256]{0:T(256)S(1)} %get-tuple-element.1424, s32[256]{0:T(256)S(1)} %get-tuple-element.1434, s32[]{:T(128)} %bitcast.678, s32[]{:T(128)} %bitcast.679, s32[]{:T(128)} %bitcast.680, s32[]{:T(128)} %bitcast.681, ...), kind=kLoop, calls=%fused_computation.216.clone.1 | loop fusion | flops 17664 | bytes 4481 | tf_op jit(solution)/shard_map/jit(searchsorted)/jit(_searchsorted_scan_impl)/vmap(jit(_searchsorted_scan_impl))/while/body/eval_jaxpr/select_n | solution.py:178
  468.4 20.1 %fusion.335 = (u32[256]{0:T(256)S(1)}, pred[256]{0:T(512)(128)(4,1)S(1)}) fusion(u32[256]{0:T(256)S(1)} %copy.1606, pred[]{:T(512)S(6)} %compare.4675, u32[256]{0:T(256)S(1)} %get-tuple-element.1424, s32[256]{0:T(256)S(1)} %get-tuple-element.1434, s32[]{:T(128)} %bitcast.678, s32[]{:T(128)} %bitcast.679, s32[]{:T(128)} %bitcast.680, s32[]{:T(128)} %bitcast.681, ...), kind=kLoop, calls=%fused_computation.216.clone.1 | loop fusion | flops 17664 | bytes 4481 | tf_op jit(solution)/shard_map/jit(searchsorted)/jit(_searchsorted_scan_impl)/vmap(jit(_searchsorted_scan_impl))/while/body/eval_jaxpr/select_n | solution.py:178
  490.0 20.1 %fusion.335 = (u32[256]{0:T(256)S(1)}, pred[256]{0:T(512)(128)(4,1)S(1)}) fusion(u32[256]{0:T(256)S(1)} %copy.1606, pred[]{:T(512)S(6)} %compare.4675, u32[256]{0:T(256)S(1)} %get-tuple-element.1424, s32[256]{0:T(256)S(1)} %get-tuple-element.1434, s32[]{:T(128)} %bitcast.678, s32[]{:T(128)} %bitcast.679, s32[]{:T(128)} %bitcast.680, s32[]{:T(128)} %bitcast.681, ...), kind=kLoop, calls=%fused_computation.216.clone.1 | loop fusion | flops 17664 | bytes 4481 | tf_op jit(solution)/shard_map/jit(searchsorted)/jit(_searchsorted_scan_impl)/vmap(jit(_searchsorted_scan_impl))/while/body/eval_jaxpr/select_n | solution.py:178
  511.5 20.1 %fusion.335 = (u32[256]{0:T(256)S(1)}, pred[256]{0:T(512)(128)(4,1)S(1)}) fusion(u32[256]{0:T(256)S(1)} %copy.1606, pred[]{:T(512)S(6)} %compare.4675, u32[256]{0:T(256)S(1)} %get-tuple-element.1424, s32[256]{0:T(256)S(1)} %get-tuple-element.1434, s32[]{:T(128)} %bitcast.678, s32[]{:T(128)} %bitcast.679, s32[]{:T(128)} %bitcast.680, s32[]{:T(128)} %bitcast.681, ...), kind=kLoop, calls=%fused_computation.216.clone.1 | loop fusion | flops 17664 | bytes 4481 | tf_op jit(solution)/shard_map/jit(searchsorted)/jit(_searchsorted_scan_impl)/vmap(jit(_searchsorted_scan_impl))/while/body/eval_jaxpr/select_n | solution.py:178
  533.1 20.1 %fusion.335 = (u32[256]{0:T(256)S(1)}, pred[256]{0:T(512)(128)(4,1)S(1)}) fusion(u32[256]{0:T(256)S(1)} %copy.1606, pred[]{:T(512)S(6)} %compare.4675, u32[256]{0:T(256)S(1)} %get-tuple-element.1424, s32[256]{0:T(256)S(1)} %get-tuple-element.1434, s32[]{:T(128)} %bitcast.678, s32[]{:T(128)} %bitcast.679, s32[]{:T(128)} %bitcast.680, s32[]{:T(128)} %bitcast.681, ...), kind=kLoop, calls=%fused_computation.216.clone.1 | loop fusion | flops 17664 | bytes 4481 | tf_op jit(solution)/shard_map/jit(searchsorted)/jit(_searchsorted_scan_impl)/vmap(jit(_searchsorted_scan_impl))/while/body/eval_jaxpr/select_n | solution.py:178
  554.7 20.1 %fusion.335 = (u32[256]{0:T(256)S(1)}, pred[256]{0:T(512)(128)(4,1)S(1)}) fusion(u32[256]{0:T(256)S(1)} %copy.1606, pred[]{:T(512)S(6)} %compare.4675, u32[256]{0:T(256)S(1)} %get-tuple-element.1424, s32[256]{0:T(256)S(1)} %get-tuple-element.1434, s32[]{:T(128)} %bitcast.678, s32[]{:T(128)} %bitcast.679, s32[]{:T(128)} %bitcast.680, s32[]{:T(128)} %bitcast.681, ...), kind=kLoop, calls=%fused_computation.216.clone.1 | loop fusion | flops 17664 | bytes 4481 | tf_op jit(solution)/shard_map/jit(searchsorted)/jit(_searchsorted_scan_impl)/vmap(jit(_searchsorted_scan_impl))/while/body/eval_jaxpr/select_n | solution.py:178
  639.3 13.0 %all-to-all-start = ((f32[146,128,4]{0,2,1:T(4,128)}), f32[146,128,4]{0,2,1:T(4,128)S(1)}, u32[]{:S(2)}, u32[]{:S(2)}) async-start(f32[146,128,4]{0,2,1:T(4,128)} %pad_maximum_fusion.26), calls=%async_computation | async-start | bytes 1048576 | tf_op jit(solution)/shard_map/all_to_all | solution.py:149
  653.5 12.4 all-to-all-done
  728.2 14.2 %multiply_bitcast_fusion.5 = f32[4,6,6,256]{1,2,0,3:T(8,128)} fusion(f32[6,6,256,1]{1,0,3,2:T(8,128)} %copy.1445, f32[6]{0:T(128)S(1)} %copy-done.80, f32[4,6,6,256]{1,2,0,3:T(8,128)} %copy-done.7, f32[4,6,6,256]{1,2,0,3:T(8,128)} %copy-done.4, f32[1,6,6,256]{1,2,0,3:T(8,128)} %copy-done.20, f32[1,6,6,256]{1,2,0,3:T(8,128)} %copy-done.19, ...), kind=kOutput, calls=%fused_computation.228 | convolution fusion | flops 3022848 | bytes 626728 | tf_op jit(solution)/shard_map/ims,cmvs->civs/dot_general | solution.py:134
  758.1 12.7 copy.1302
  772.6 9.2 scatter_fusion.1
  781.8 9.2 scatter_fusion.2
  791.0 15.1 %copy.1305 = f32[4,6,6,6,256]{4,0,3,2,1:T(4,128)S(1)} copy(f32[4,6,6,6,256]{2,0,4,3,1:T(4,128)} %scatter_fusion.2) | data formatting | bytes 1769472 | tf_op jit(solution)/shard_map/scatter-add | solution.py:273
  885.5 13.1 %all-to-all-start.2 = ((f32[146,128,4]{0,2,1:T(4,128)}), f32[146,128,4]{0,2,1:T(4,128)S(1)}, u32[]{:S(2)}, u32[]{:S(2)}) async-start(f32[146,128,4]{0,2,1:T(4,128)} %pad_maximum_fusion.25), calls=%async_computation.2 | async-start | bytes 1048576 | tf_op jit(solution)/shard_map/all_to_all | solution.py:149
  901.3 10.8 all-to-all-done.2
  974.9 14.2 %multiply_bitcast_fusion.3 = f32[4,6,6,256]{1,2,0,3:T(8,128)} fusion(f32[6,6,256,1]{1,0,3,2:T(8,128)} %copy.1449, f32[6]{0:T(128)S(1)} %copy-done.81, f32[4,6,6,256]{1,2,0,3:T(8,128)} %copy-done.8, f32[4,6,6,256]{1,2,0,3:T(8,128)} %copy-done.2, f32[1,6,6,256]{1,2,0,3:T(8,128)} %copy-done.22, f32[1,6,6,256]{1,2,0,3:T(8,128)} %copy-done.21, ...), kind=kOutput, calls=%fused_computation.226 | convolution fusion | flops 3022848 | bytes 626728 | tf_op jit(solution)/shard_map/ims,cmvs->civs/dot_general | solution.py:134
  1005.0 12.7 copy.1370
  1019.5 9.2 scatter_fusion.4
  1028.7 9.2 scatter_fusion.5
  1037.9 15.2 %copy.1373 = f32[4,6,6,6,256]{4,0,3,2,1:T(4,128)S(1)} copy(f32[4,6,6,6,256]{2,0,4,3,1:T(4,128)} %scatter_fusion.5) | data formatting | bytes 1769472 | tf_op jit(solution)/shard_map/scatter-add | solution.py:273
  1132.6 13.1 %all-to-all-start.4 = ((f32[146,128,4]{0,2,1:T(4,128)}), f32[146,128,4]{0,2,1:T(4,128)S(1)}, u32[]{:S(2)}, u32[]{:S(2)}) async-start(f32[146,128,4]{0,2,1:T(4,128)} %pad_maximum_fusion.24), calls=%async_computation.4 | async-start | bytes 1048576 | tf_op jit(solution)/shard_map/all_to_all | solution.py:149
  1148.4 10.8 all-to-all-done.4
  1221.9 14.2 %multiply_bitcast_fusion.1 = f32[4,6,6,256]{1,2,0,3:T(8,128)} fusion(f32[6,6,256,1]{1,0,3,2:T(8,128)} %copy.1453, f32[6]{0:T(128)S(1)} %copy-done.82, f32[4,6,6,256]{1,2,0,3:T(8,128)} %copy-done.6, f32[4,6,6,256]{1,2,0,3:T(8,128)} %copy-done, f32[1,6,6,256]{1,2,0,3:T(8,128)} %copy-done.18, f32[1,6,6,256]{1,2,0,3:T(8,128)} %copy-done.17, ...), kind=kOutput, calls=%fused_computation.224 | convolution fusion | flops 3022848 | bytes 626728 | tf_op jit(solution)/shard_map/ims,cmvs->civs/dot_general | solution.py:134
  1251.8 12.7 copy.1438
  1266.3 9.2 scatter_fusion.7
  1284.6 15.2 %copy.1441 = f32[4,6,6,6,256]{4,0,3,2,1:T(4,128)S(1)} copy(f32[4,6,6,6,256]{2,0,4,3,1:T(4,128)} %scatter_fusion.8) | data formatting | bytes 1769472 | tf_op jit(solution)/shard_map/scatter-add | solution.py:273
  (1012 shorter events, 569.8 us)
Async XLA Ops:
  0.0 31.1 %copy-start.143 = (s32[3,512]{1,0:T(4,128)S(1)}, s32[3,512]{1,0:T(4,128)}, u32[]{:S(2)}) copy-start(s32[3,512]{1,0:T(4,128)} %param.92) | copy-start | bytes 18436
  0.0 33.5 %copy-start.144 = (s32[2,256]{1,0:T(2,128)S(1)}, s32[2,256]{1,0:T(2,128)}, u32[]{:S(2)}) copy-start(s32[2,256]{1,0:T(2,128)} %param.93) | copy-start | bytes 6148
  9.4 620.7 %copy-start.23 = (f32[4,216,256]{2,0,1:T(4,128)}, f32[4,216,256]{2,0,1:T(4,128)S(1)}, u32[]{:S(2)}) copy-start(f32[4,216,256]{2,0,1:T(4,128)S(1)} %copy.1239) | copy-start | bytes 2654212
  9.7 35.8 %copy-start.33 = (f32[144,256]{0,1:T(8,128)}, f32[144,256]{0,1:T(8,128)S(1)}, u32[]{:S(2)}) copy-start(f32[144,256]{0,1:T(8,128)S(1)} %copy.1242) | copy-start | bytes 442372
  11.0 582.9 %collective-permute-start = (f32[1,144,32]{1,2,0:T(8,128)}, f32[1,144,32]{1,2,0:T(8,128)}, u32[]{:S(2)}, u32[]{:S(2)}) collective-permute-start(f32[1,144,32]{1,2,0:T(8,128)} %select_bitcast_fusion.41), channel_id=1, source_target_pairs={{0,1},{1,2},{2,3},{3,4},{4,5},{5,6},{6,7},{8,9},{9,10},{10,11},{11... | collective-permute-start | bytes 55304 | tf_op jit(solution)/shard_map/ppermute | solution.py:24
  20.0 25.4 %copy-start.35 = (f32[144,256]{0,1:T(8,128)}, f32[144,256]{0,1:T(8,128)S(1)}, u32[]{:S(2)}) copy-start(f32[144,256]{0,1:T(8,128)S(1)} %copy.1258) | copy-start | bytes 442372
  21.3 578.7 %collective-permute-start.2 = (f32[1,144,32]{1,2,0:T(8,128)}, f32[1,144,32]{1,2,0:T(8,128)}, u32[]{:S(2)}, u32[]{:S(2)}) collective-permute-start(f32[1,144,32]{1,2,0:T(8,128)} %select_bitcast_fusion.39), channel_id=1, source_target_pairs={{0,8},{8,16},{16,24},{24,32},{32,40},{40,48},{48,56},{56,64},{64,7... | collective-permute-start | bytes 55304 | tf_op jit(solution)/shard_map/ppermute | solution.py:24
  33.5 558.1 %copy-start.94 = (s32[1,256]{1,0:T(1,128)}, s32[1,256]{1,0:T(1,128)S(1)}, u32[]{:S(2)}) copy-start(s32[1,256]{1,0:T(1,128)S(1)} %get-tuple-element.912) | copy-start | bytes 3076
  33.5 558.1 %copy-start.96 = (s32[1,256]{1,0:T(1,128)}, s32[1,256]{1,0:T(1,128)S(1)}, u32[]{:S(2)}) copy-start(s32[1,256]{1,0:T(1,128)S(1)} %get-tuple-element.913) | copy-start | bytes 3076
  175.0 412.7 %copy-start.142 = (s32[512]{0:T(512)S(1)}, s32[512]{0:T(512)}, u32[]{:S(2)}) copy-start(s32[512]{0:T(512)} %broadcast_maximum_fusion) | copy-start | bytes 6148
  175.0 413.3 %copy-start.9 = (f32[4,216,256]{2,1,0:T(8,128)S(1)}, f32[4,216,256]{2,1,0:T(8,128)}, u32[]{:S(2)}) copy-start(f32[4,216,256]{2,1,0:T(8,128)} %param.89) | copy-start | bytes 2654212
  175.0 420.8 %copy-start.106 = (pred[256]{0:T(512)(128)(4,1)}, pred[256]{0:T(512)(128)(4,1)S(1)}, u32[]{:S(2)}) copy-start(pred[256]{0:T(512)(128)(4,1)S(1)} %get-tuple-element.658) | copy-start | bytes 772
  175.0 419.7 %copy-start.89 = (s32[1024]{0:T(1024)}, s32[1024]{0:T(1024)S(1)}, u32[]{:S(2)}) copy-start(s32[1024]{0:T(1024)S(1)} %pad_clamp_fusion.13) | copy-start | bytes 12292
  308.4 282.5 %copy-start.103 = (pred[64]{0:T(512)(128)(4,1)S(1)}, pred[64]{0:T(512)(128)(4,1)}, u32[]{:S(2)}) copy-start(pred[64]{0:T(512)(128)(4,1)} %get-tuple-element.632) | copy-start | bytes 196
  311.6 280.7 %slice-start = ((f32[4,216,256]{2,1,0:T(8,128)}), f32[3,216,256]{2,1,0:T(8,128)S(1)}, s32[]{:S(2)}) async-start(f32[4,216,256]{2,1,0:T(8,128)} %param.89), calls=%async_computation.6 | async-start | bytes 1327104 | tf_op jit(solution)/shard_map/slice | solution.py:252
  311.6 280.7 %copy-start.30 = (f32[216,648]{1,0:T(8,128)S(1)}, f32[216,648]{1,0:T(8,128)}, u32[]{:S(2)}) copy-start(f32[216,648]{1,0:T(8,128)} %constant.1317.clone) | copy-start | bytes 1679620
  441.5 162.9 %copy-start.109 = (pred[256]{0:T(512)(128)(4,1)}, pred[256]{0:T(512)(128)(4,1)S(1)}, u32[]{:S(2)}) copy-start(pred[256]{0:T(512)(128)(4,1)S(1)} %get-tuple-element.953) | copy-start | bytes 772
  441.5 166.6 %copy-start.112 = (pred[256]{0:T(512)(128)(4,1)}, pred[256]{0:T(512)(128)(4,1)S(1)}, u32[]{:S(2)}) copy-start(pred[256]{0:T(512)(128)(4,1)S(1)} %get-tuple-element.643) | copy-start | bytes 772
  441.5 161.1 %copy-start.90 = (s32[1024]{0:T(1024)}, s32[1024]{0:T(1024)S(1)}, u32[]{:S(2)}) copy-start(s32[1024]{0:T(1024)S(1)} %pad_clamp_fusion.11) | copy-start | bytes 12292
  441.6 165.4 %copy-start.91 = (s32[1024]{0:T(1024)}, s32[1024]{0:T(1024)S(1)}, u32[]{:S(2)}) copy-start(s32[1024]{0:T(1024)S(1)} %pad_clamp_fusion.9) | copy-start | bytes 12292
  598.0 3.5 collective-permute-start.1
  615.2 7.7 collective-permute-start.3
  616.5 58.3 %copy-start.68 = (s32[1024]{0:T(1024)}, s32[1024]{0:T(1024)S(1)}, u32[]{:S(2)}) copy-start(s32[1024]{0:T(1024)S(1)} %pad_clamp_fusion) | copy-start | bytes 12292
  639.3 26.6 %all-to-all-start = ((f32[146,128,4]{0,2,1:T(4,128)}), f32[146,128,4]{0,2,1:T(4,128)S(1)}, u32[]{:S(2)}, u32[]{:S(2)}) async-start(f32[146,128,4]{0,2,1:T(4,128)} %pad_maximum_fusion.26), calls=%async_computation | async-start | bytes 1048576 | tf_op jit(solution)/shard_map/all_to_all | solution.py:149
  653.5 23.9 %copy-start.97 = (s32[1,256]{1,0:T(1,128)S(1)}, s32[1,256]{1,0:T(1,128)}, u32[]{:S(2)}) copy-start(s32[1,256]{1,0:T(1,128)} %copy-done.96) | copy-start | bytes 3076
  653.5 23.9 %copy-start.95 = (s32[1,256]{1,0:T(1,128)S(1)}, s32[1,256]{1,0:T(1,128)}, u32[]{:S(2)}) copy-start(s32[1,256]{1,0:T(1,128)} %copy-done.94) | copy-start | bytes 3076
  751.5 19.4 %all-to-all-start.1 = ((f32[144,128,4]{0,2,1:T(4,128)}), f32[144,128,4]{0,2,1:T(4,128)S(1)}, u32[]{:S(2)}, u32[]{:S(2)}) async-start(f32[144,128,4]{0,2,1:T(4,128)} %all_to_all.37), calls=%async_computation.1 | async-start | bytes 1048576 | tf_op jit(solution)/shard_map/all_to_all | solution.py:154
  807.6 61.0 %copy-start.12 = (f32[4,216,256]{2,1,0:T(8,128)}, f32[4,216,256]{2,1,0:T(8,128)S(1)}, u32[]{:S(2)}) copy-start(f32[4,216,256]{2,1,0:T(8,128)S(1)} %fusion.41) | copy-start | bytes 2654212
  807.9 66.3 %copy-start.25 = (f32[4,216,256]{2,0,1:T(4,128)}, f32[4,216,256]{2,0,1:T(4,128)S(1)}, u32[]{:S(2)}) copy-start(f32[4,216,256]{2,0,1:T(4,128)S(1)} %copy.1307) | copy-start | bytes 2654212
  817.7 22.9 %copy-start.107 = (pred[256]{0:T(512)(128)(4,1)S(1)}, pred[256]{0:T(512)(128)(4,1)}, u32[]{:S(2)}) copy-start(pred[256]{0:T(512)(128)(4,1)} %copy-done.106) | copy-start | bytes 772
  817.7 18.9 %collective-permute-start.4 = (f32[1,144,32]{1,2,0:T(8,128)S(1)}, f32[1,144,32]{1,2,0:T(8,128)S(1)}, u32[]{:S(2)}, u32[]{:S(2)}) collective-permute-start(f32[1,144,32]{1,2,0:T(8,128)S(1)} %select_bitcast_fusion.37), channel_id=1, source_target_pairs={{0,1},{1,2},{2,3},{3,4},{4,5},{5,6},{6,7},{8,9},{9,10},{10,11},{11... | collective-permute-start | bytes 55304 | tf_op jit(solution)/shard_map/ppermute | solution.py:24
  826.0 10.6 collective-permute-start.6
  845.1 8.2 collective-permute-start.5
  864.6 5.8 collective-permute-start.7
  883.4 31.5 %copy-start.69 = (s32[1024]{0:T(1024)S(1)}, s32[1024]{0:T(1024)}, u32[]{:S(2)}) copy-start(s32[1024]{0:T(1024)} %copy-done.68) | copy-start | bytes 12292
  885.5 26.7 %all-to-all-start.2 = ((f32[146,128,4]{0,2,1:T(4,128)}), f32[146,128,4]{0,2,1:T(4,128)S(1)}, u32[]{:S(2)}, u32[]{:S(2)}) async-start(f32[146,128,4]{0,2,1:T(4,128)} %pad_maximum_fusion.25), calls=%async_computation.2 | async-start | bytes 1048576 | tf_op jit(solution)/shard_map/all_to_all | solution.py:149
  998.2 19.6 %all-to-all-start.3 = ((f32[144,128,4]{0,2,1:T(4,128)}), f32[144,128,4]{0,2,1:T(4,128)S(1)}, u32[]{:S(2)}, u32[]{:S(2)}) async-start(f32[144,128,4]{0,2,1:T(4,128)} %all_to_all.41), calls=%async_computation.3 | async-start | bytes 1048576 | tf_op jit(solution)/shard_map/all_to_all | solution.py:154
  1054.6 61.0 %copy-start.10 = (f32[4,216,256]{2,1,0:T(8,128)}, f32[4,216,256]{2,1,0:T(8,128)S(1)}, u32[]{:S(2)}) copy-start(f32[4,216,256]{2,1,0:T(8,128)S(1)} %fusion.46) | copy-start | bytes 2654212
  1055.0 66.3 %copy-start.24 = (f32[4,216,256]{2,0,1:T(4,128)}, f32[4,216,256]{2,0,1:T(4,128)S(1)}, u32[]{:S(2)}) copy-start(f32[4,216,256]{2,0,1:T(4,128)S(1)} %copy.1375) | copy-start | bytes 2654212
  1059.4 22.9 %copy-start.141 = (pred[256]{0:T(512)(128)(4,1)S(1)}, pred[256]{0:T(512)(128)(4,1)}, u32[]{:S(2)}) copy-start(pred[256]{0:T(512)(128)(4,1)} %get-tuple-element.950) | copy-start | bytes 772
  1064.8 22.9 %copy-start.108 = (pred[256]{0:T(512)(128)(4,1)S(1)}, pred[256]{0:T(512)(128)(4,1)}, u32[]{:S(2)}) copy-start(pred[256]{0:T(512)(128)(4,1)} %copy-done.106) | copy-start | bytes 772
  1067.4 16.3 %collective-permute-start.8 = (f32[1,144,32]{1,2,0:T(8,128)S(1)}, f32[1,144,32]{1,2,0:T(8,128)S(1)}, u32[]{:S(2)}, u32[]{:S(2)}) collective-permute-start(f32[1,144,32]{1,2,0:T(8,128)S(1)} %select_bitcast_fusion.33), channel_id=1, source_target_pairs={{0,1},{1,2},{2,3},{3,4},{4,5},{5,6},{6,7},{8,9},{9,10},{10,11},{11... | collective-permute-start | bytes 55304 | tf_op jit(solution)/shard_map/ppermute | solution.py:24
  1075.6 8.1 collective-permute-start.10
  1092.2 8.2 collective-permute-start.9
  1111.7 5.8 collective-permute-start.11
  1130.4 31.6 %copy-start.70 = (s32[1024]{0:T(1024)S(1)}, s32[1024]{0:T(1024)}, u32[]{:S(2)}) copy-start(s32[1024]{0:T(1024)} %copy-done.68) | copy-start | bytes 12292
  1132.6 26.7 %all-to-all-start.4 = ((f32[146,128,4]{0,2,1:T(4,128)}), f32[146,128,4]{0,2,1:T(4,128)S(1)}, u32[]{:S(2)}, u32[]{:S(2)}) async-start(f32[146,128,4]{0,2,1:T(4,128)} %pad_maximum_fusion.24), calls=%async_computation.4 | async-start | bytes 1048576 | tf_op jit(solution)/shard_map/all_to_all | solution.py:149
  1245.2 19.4 %all-to-all-start.5 = ((f32[144,128,4]{0,2,1:T(4,128)}), f32[144,128,4]{0,2,1:T(4,128)S(1)}, u32[]{:S(2)}, u32[]{:S(2)}) async-start(f32[144,128,4]{0,2,1:T(4,128)} %all_to_all.45), calls=%async_computation.5 | async-start | bytes 1048576 | tf_op jit(solution)/shard_map/all_to_all | solution.py:154
  (125 other events, 1429.2 us)
where the time goes:
time: 1320 us; the launch traced here: 1300 us
  other arithmetic  658 us (50%)
  local copies, waits for them, and re-layouts  391 us (30%)
  matrix products  130 us (10%)
  starting transfers between devices  80.1 us (6%)
  waiting for transfers between devices  39.2 us (3%)
    select_n x48, other arithmetic, per_device(): jnp.searchsorted(wanted, target % elem_count)  483 us
    dot_general x6, matrix products, from_mortar(): jnp.einsum('ims,cmvs->civs', basis * scale[None], grid, precision=lax.Pre...  69.8 us
    dot_general x6, matrix products, to_mortar(): jnp.einsum('ims,civs->cmvs', basis, grid, precision=lax.Precision.HIGHEST)  46 us
    scatter-add x3, local copies, waits for them, and re-layouts, time_rates(): surface.at[:, :, :, 0, stator_elems]  45.5 us
    scatter-add x6, local copies, waits for them, and re-layouts, place_face(): return surface.at[tuple(selector)].add(values)  42.3 us
    all_to_all x3, starting transfers between devices, route_out(): lax.all_to_all(payload, ('blk', 'sub'), split_axis=1, concat_axis=1, tile...  39.3 us
    gather x27, local copies, waits for them, and re-layouts, time_rates(): jnp.take(jnp.concatenate(pieces, axis=1), lookups[face_index], axis=1)  35.5 us
    gather x48, local copies, waits for them, and re-layouts, per_device(): jnp.searchsorted(wanted, target % elem_count)  34.8 us
  transfers between devices with their start and end apart: 18, of which 6 were waited for; matrix products, arithmetic and copies ran while one was open for 52% of the time, Pallas kernels for 0%

commit v1 on v0

v1 whole, which is shorter than its diff:
```python
import jax
import jax.numpy as jnp
import numpy as np
from jax import lax
from jax.experimental import pallas as pl
from jax.experimental.pallas import tpu as pltpu
from jax.sharding import PartitionSpec as P

P_SIZE = 6
SUB = 16
IFD = 64
RIM = 32
NODES = 216
ELEMS = 256
FACES = 2 * IFD
SLOTS = 512
DEVICES = 128
TR = 40
FEAT = 128
DT_STEP = 0.01
F32 = jnp.float32
BF16 = jnp.bfloat16
VMEM_BYTES = 40 * 1024 * 1024


def legendre_columns(points, npts):
    legendre = np.zeros((npts, npts))
    legendre[:, 0] = 1.0
    legendre[:, 1] = points
    for k in range(2, npts):
        legendre[:, k] = (
            (2 * k - 1) * points * legendre[:, k - 1] - (k - 1) * legendre[:, k - 2]
        ) / k
    return legendre


def basis_tables(npts):
    order = npts - 1
    points = -np.cos(np.pi * np.arange(npts) / order)
    for iteration in range(60):
        legendre = legendre_columns(points, npts)
        points = points - (points * legendre[:, order] - legendre[:, order - 1]) / (
            npts * legendre[:, order]
        )
    legendre = legendre_columns(points, npts)
    weights = 2.0 / (order * npts * legendre[:, order] ** 2)
    separation = points[:, None] - points[None, :] + np.eye(npts)
    derivative = legendre[:, order][:, None] / legendre[:, order][None, :] / separation
    derivative = derivative * (1.0 - np.eye(npts))
    derivative[0, 0] = -order * npts / 4.0
    derivative[order, order] = order * npts / 4.0
    return (points, weights, derivative)


POINTS, WEIGHTS, DERIVATIVE = basis_tables(P_SIZE)
LIFT = float(1.0 / WEIGHTS[0])
SECTIONS = (
    (0.0, 1.0, DT_STEP),
    (0.75, 0.25, 0.25 * DT_STEP),
    (1.0 / 3.0, 2.0 / 3.0, 2.0 / 3.0 * DT_STEP),
)


def face_rows():
    picks = np.zeros((6 * TR, NODES))
    for face in range(6):
        fixed = 0 if face % 2 == 0 else P_SIZE - 1
        for a in range(P_SIZE):
            for b in range(P_SIZE):
                place = [a, b]
                place.insert(face // 2, fixed)
                node = (place[0] * P_SIZE + place[1]) * P_SIZE + place[2]
                picks[face * TR + a * P_SIZE + b, node] = 1.0
    return picks


def derivative_pieces():
    one = np.eye(P_SIZE)
    square = np.eye(P_SIZE * P_SIZE)
    whole = [
        np.kron(DERIVATIVE, square),
        np.kron(one, np.kron(DERIVATIVE, one)),
        np.kron(square, DERIVATIVE),
    ]
    pieces = []
    for matrix in whole:
        matrix = matrix.astype(np.float32)
        high = matrix.astype(jnp.bfloat16)
        pieces.append(high)
        pieces.append((matrix - high.astype(np.float32)).astype(jnp.bfloat16))
    return np.stack(pieces)


def nn(a, b):
    return lax.dot_general(a, b, (((1,), (0,)), ((), ())), preferred_element_type=F32)


def nt(a, b):
    return lax.dot_general(a, b, (((1,), (1,)), ((), ())), preferred_element_type=F32)


def tn(a, b):
    return lax.dot_general(a, b, (((0,), (0,)), ((), ())), preferred_element_type=F32)


def halves(x):
    high = x.astype(BF16)
    return high, (x - high.astype(F32)).astype(BF16)


def nn2(exact, x):
    high, low = halves(x)
    return nn(exact, high) + nn(exact, low)


def mark(cond):
    return jnp.where(cond, 1.0, 0.0)


def iota(shape, dim):
    return lax.broadcasted_iota(jnp.int32, shape, dim)


def my_device():
    return lax.axis_index("blk") * 8 + lax.axis_index("sub")


def call(body, outs, args, scratch=(), flops=1e8, moved=2e6):
    return pl.pallas_call(
        body,
        out_shape=[jax.ShapeDtypeStruct(s, d) for s, d in outs],
        in_specs=[pl.BlockSpec(memory_space=pltpu.VMEM)] * len(args),
        out_specs=[pl.BlockSpec(memory_space=pltpu.VMEM)] * len(outs),
        scratch_shapes=list(scratch),
        compiler_params=pltpu.CompilerParams(vmem_limit_bytes=VMEM_BYTES),
        cost_estimate=pl.CostEstimate(
            flops=int(flops), bytes_accessed=int(moved), transcendentals=0
        ),
    )(*args)


def spread(values, pad, width):
    for group in range(3 * P_SIZE):
        c, i = divmod(group, P_SIZE)
        start = c * TR + i * P_SIZE
        pad[group, 0:P_SIZE, 0:width] = values[start : start + P_SIZE, :]


def to_mortars(basis, pad, out, comps, add):
    for half in range(2):
        lanes = slice(half * FACES, (half + 1) * FACES)
        for c in comps:
            for m in range(P_SIZE):
                total = basis[0, m : m + 1, lanes] * pad[c * P_SIZE, :, 0:FACES]
                for i in range(1, P_SIZE):
                    total += basis[i, m : m + 1, lanes] * pad[c * P_SIZE + i, :, 0:FACES]
                start = c * TR + m * P_SIZE
                rows = slice(start, start + P_SIZE)
                if add:
                    out[rows, lanes] += total[0:P_SIZE, :]
                else:
                    out[rows, lanes] = total[0:P_SIZE, :]


def outgoing(traces4, traces5):
    blank = jnp.zeros((FEAT - 3 * TR, ELEMS), F32)
    out4 = jnp.concatenate([traces4[0] - traces4[3], traces4[1], traces4[2], blank], axis=0)
    out5 = jnp.concatenate([traces5[0] + traces5[3], traces5[1], traces5[2], blank], axis=0)
    return out4, out5


def at_faces(rows4, rows5, members):
    high5, low5 = halves(rows5)
    high4, low4 = halves(rows4)
    rotor = nt(high5, members) + nt(low5, members)
    stator = nt(high4, members) + nt(low4, members)
    return jnp.where(iota((FEAT, FACES), 1) < IFD, rotor, stator)


def at_elements(values, members):
    rotor_side = iota((FEAT, FACES), 1) < IFD
    to5 = nn2b(jnp.where(rotor_side, values, 0.0), members)
    to4 = nn2b(jnp.where(rotor_side, 0.0, values), members)
    return to4, to5


def nn2b(x, exact):
    high, low = halves(x)
    return nn(high, exact) + nn(low, exact)


def comp(rows, c):
    return rows[c * TR : (c + 1) * TR, :]


def partner_body(pairs, out):
    row = iota((DEVICES, ELEMS), 0)
    total = None
    for mine, other in ((0, 1), (1, 0)):
        entry = pairs[mine : mine + 1, :]
        partner = pairs[other : other + 1, :]
        owner_row = mark(row == (entry >> 2)).astype(BF16)
        spot = entry & 3
        facts = jnp.where(row == spot, (partner >> 2) + 1, 0) + jnp.where(
            row == spot + 4, partner & 3, 0
        )
        term = nt(owner_row, facts.astype(F32).astype(BF16))
        total = term if total is None else total + term
    out[...] = total


def tables_body(
    neighbours, sends, metric, fields, sel45,
    local, rim_out, rim_in, members, basis, project, own, info, face_metric, mortars,
    rows, pad,
):
    me = my_device()
    nb = neighbours[...]
    face_id = iota(nb.shape, 0)
    remote = (nb >= 0) & ((nb >> 8) != me)
    here = (nb >= 0) & ((nb >> 8) == me)
    spot = nb & 255
    flags = jnp.where(face_id < 4, mark(remote), mark(nb == -2))
    rows[...] = jnp.zeros(rows.shape, F32)
    rows[0, 0:6, :] = flags
    rows[1, 0:6, :] = spot.astype(F32)
    flag_rows = rows[0].astype(BF16)
    spot_rows = rows[1].astype(BF16)
    down = iota((ELEMS, ELEMS), 0)
    across = iota((ELEMS, ELEMS), 1)
    before = mark(down < across).astype(BF16)
    same = mark(down == across).astype(BF16)
    rank = nn(flag_rows, before)
    spot_down = jnp.where(nt(same, flag_rows) > 0.5, nt(same, spot_rows), 1e4)
    key = jnp.where(here, spot, -1)
    for face in range(6):
        local[face] = mark(down == key[face : face + 1, :]).astype(BF16)
    slot = iota((RIM, ELEMS), 0).astype(F32)
    for face in range(4):
        live = flags[face : face + 1, :] > 0.5
        order = jnp.sum(
            mark(spot_down[:, face : face + 1] < rows[1, face : face + 1, :]),
            axis=0,
            keepdims=True,
        )
        lines = slice(face * RIM, (face + 1) * RIM)
        rim_out[lines, :] = mark((slot == rank[face : face + 1, :]) & live).astype(BF16)
        rim_in[lines, :] = mark((slot == order) & live).astype(BF16)
    number = iota((FACES, ELEMS), 0)
    wanted = number.astype(F32)
    rotor = (wanted == rank[5:6, :]) & (flags[5:6, :] > 0.5)
    stator = (wanted - IFD == rank[4:5, :]) & (flags[4:5, :] > 0.5)
    member = jnp.where(number < IFD, mark(rotor), mark(stator)).astype(BF16)
    members[...] = member
    face_of = sends[0:1, :]
    lo_of = sends[1:2, :]
    lane_of = jnp.where(face_of >= 0, face_of + jnp.where(lo_of > 0, FACES, 0), -1)
    slot_lane = mark(iota((2 * FACES, SLOTS), 0) == lane_of).astype(BF16)
    kind = iota((16, SLOTS), 0)
    number = iota((16, SLOTS), 1)
    facts = jnp.where(kind == 0, number >> 2, 0) + jnp.where(kind == 1, number & 3, 0)
    facts += jnp.where(kind == 2, lo_of, 0) + jnp.where(kind == 3, sends[2:3, :], 0)
    found = nt(facts.astype(F32).astype(BF16), slot_lane)
    info[...] = found
    lo = found[2:3, :]
    width = found[3:4, :] - lo
    point = iota((8, 2 * FACES), 0)
    unit = jnp.zeros((8, 2 * FACES), F32)
    weight = jnp.zeros((8, 2 * FACES), F32)
    for m in range(P_SIZE):
        unit = jnp.where(point == m, float((POINTS[m] + 1.0) * 0.5), unit)
        weight = jnp.where(point == m, float(0.5 * WEIGHTS[m] / SUB), weight)
    spots = (lo + width * unit) * (2.0 / SUB) - 1.0
    for i in range(P_SIZE):
        product = None
        for j in range(P_SIZE):
            if j != i:
                term = (spots - float(POINTS[j])) * float(1.0 / (POINTS[i] - POINTS[j]))
                product = term if product is None else product * term
        basis[i] = product
        project[i] = product * weight * width * float(1.0 / WEIGHTS[i])
    for i in range(P_SIZE):
        for k in range(P_SIZE):
            term = jnp.sum(project[i] * basis[k], axis=0, keepdims=True)
            own[i, k : k + 1, :] = term[:, 0:FACES] + term[:, FACES:]
    scale = jnp.broadcast_to(metric[...], (16, ELEMS))
    high, rest = scale.astype(BF16), scale - scale.astype(BF16).astype(F32)
    middle, low = halves(rest)
    face_metric[...] = nt(high, member) + nt(middle, member) + nt(low, member)
    traces = [nn2(sel45[...], fields[c]) for c in range(4)]
    out4, out5 = outgoing([t[:TR] for t in traces], [t[TR:] for t in traces])
    spread(at_faces(out4, out5, member), pad, FACES)
    mortars[...] = jnp.zeros(mortars.shape, F32)
    to_mortars(basis, pad, mortars, (0, 1, 2), False)


def send_rows(exact, values):
    high, low = halves(values)
    return nt(exact, high) + nt(exact, low)


def route_body(facts, info, mortars, send, receive, payload):
    owner = info[0:1, :]
    turn = info[1:2, :]
    owner_pick = mark(iota((DEVICES, 2 * FACES), 0).astype(F32) == owner).astype(BF16)
    found = tn(facts[...].astype(BF16), owner_pick)
    partner = jnp.zeros((1, 2 * FACES), F32)
    other = jnp.zeros((1, 2 * FACES), F32)
    for t in range(4):
        partner = jnp.where(turn == t, found[t : t + 1, :], partner)
        other = jnp.where(turn == t, found[4 + t : 5 + t, :], other)
    partner = partner - 1.0
    kind = iota((16, 2 * FACES), 0)
    lines = jnp.where(kind == 0, partner, 0.0) + jnp.where(kind == 1, owner, 0.0)
    lines += jnp.where(kind == 2, turn, 0.0) + jnp.where(kind == 3, other, 0.0)
    same = mark(iota((2 * FACES, 2 * FACES), 0) == iota((2 * FACES, 2 * FACES), 1)).astype(BF16)
    down = nt(same, lines.astype(BF16))
    partner_down = down[:, 0:1]
    together = partner_down == partner
    mine_down = down[:, 1:2] * 4.0 + down[:, 2:3]
    theirs_down = down[:, 1:2] * 4.0 + down[:, 3:4]
    mine = owner * 4.0 + turn
    theirs = owner * 4.0 + other
    ahead = jnp.sum(mark(together & (mine_down < mine)), axis=0, keepdims=True)
    behind = jnp.sum(mark(together & (theirs_down < theirs)), axis=0, keepdims=True)
    place = iota((SLOTS, 2 * FACES), 0).astype(F32)
    sending = mark(place == partner * 4.0 + ahead).astype(BF16)
    send[...] = sending
    receive[...] = mark(place == partner * 4.0 + behind).astype(BF16)
    payload[...] = send_rows(sending, mortars[...])


def place_interface(part, arrived, members, place45):
    to4, to5 = at_elements(arrived[...], members[...])
    result = []
    for c in range(4):
        source = (0, 1, 2, 0)[c]
        sign5 = -1.0 if c == 3 else 1.0
        stack = jnp.concatenate([comp(to4, source), sign5 * comp(to5, source)], axis=0)
        result.append(part[c] + nn2(place45[...], stack))
    return result


def inner_body(section, *refs):
    if section == 0:
        part, refs = refs[0], refs[1:]
        first = part
        arrived = None
    else:
        part, first, arrived, place45 = refs[:4]
        refs = refs[4:]
    (members, local, rim_out, own, metric, neighbours, derive, select, place) = refs[:9]
    rims = refs[9:13]
    after, pad, mixed = refs[13:]
    keep, stay, rate = SECTIONS[section]
    if section == 0:
        fields = [part[c] for c in range(4)]
    else:
        fields = place_interface(part, arrived, members, place45)
    high, low = zip(*[halves(x) for x in fields])
    sel = select[...]
    traces = [nn(sel, high[c]) + nn(sel, low[c]) for c in range(4)]
    blank = jnp.zeros((FEAT - 3 * TR, ELEMS), F32)
    leaving, inside = [], []
    for face in range(6):
        sign = 1.0 if face % 2 else -1.0
        cut = [t[face * TR : (face + 1) * TR, :] for t in traces]
        along = face // 2
        tangent = [cut[1 + c] for c in range(3) if c != along]
        normal = sign * cut[1 + along]
        leaving.append(jnp.concatenate([cut[0] + normal] + tangent + [blank], axis=0))
        inside.append(jnp.concatenate([cut[0] - normal] + tangent + [blank], axis=0))
    leaving = [halves(x) for x in leaving]
    for face in range(4):
        pick = rim_out[face * RIM : (face + 1) * RIM, :]
        rims[face][...] = nt(pick, leaving[face][0]) + nt(pick, leaving[face][1])
    spread(at_faces(inside[4], inside[5], members[...]), pad, FACES)
    mixed[...] = jnp.zeros(mixed.shape, F32)
    for c in range(3):
        for i in range(P_SIZE):
            total = own[i, 0:1, :] * pad[c * P_SIZE]
            for k in range(1, P_SIZE):
                total += own[i, k : k + 1, :] * pad[c * P_SIZE + k]
            start = c * TR + i * P_SIZE
            mixed[start : start + P_SIZE, :] = -total[0:P_SIZE, :]
    to4, to5 = at_elements(mixed[...], members[...])
    terms = []
    for face in range(6):
        pick = local[face]
        arriving = nn(leaving[face ^ 1][0], pick) + nn(leaving[face ^ 1][1], pick)
        term = 0.5 * (arriving - inside[face])
        if face >= 4:
            term = jnp.where(neighbours[face : face + 1, :] == -2, 0.0, term)
            term = term + (to4, to5)[face - 4]
        terms.append(term)
    scale = metric[...] * rate
    for c in range(4):
        pieces = []
        for face in range(6):
            along = face // 2
            if c == 0:
                pieces.append(comp(terms[face], 0))
            elif c == 1 + along:
                pieces.append((-1.0 if face % 2 else 1.0) * comp(terms[face], 0))
            else:
                tangents = [k for k in range(3) if k != along]
                pieces.append(comp(terms[face], 1 + tangents.index(c - 1)))
        surface = nn2(place[...], jnp.concatenate(pieces, axis=0))
        if c == 0:
            pairs = ((0, 1), (1, 2), (2, 3))
        else:
            pairs = ((c - 1, 0),)
        volume = None
        for direction, source in pairs:
            big, small = derive[2 * direction], derive[2 * direction + 1]
            term = nn(big, high[source]) + nn(big, low[source]) + nn(small, high[source])
            volume = term if volume is None else volume + term
        base = stay * fields[c]
        if keep:
            base = base + keep * first[c]
        after[c] = base + scale * (LIFT * surface - volume)


def rim_body(section, *refs):
    before, r0, r1, r2, r3, rim_in, metric, place03 = refs[:8]
    last = section == 2
    if last:
        (after,) = refs[8:]
    else:
        members, basis, sel45, after, mortars, pad = refs[8:]
    scale = metric[...] * (SECTIONS[section][2] * LIFT)
    terms = []
    for face, ref in enumerate((r0, r1, r2, r3)):
        high, low = halves(ref[...])
        pick = rim_in[face * RIM : (face + 1) * RIM, :]
        terms.append(0.5 * (tn(high, pick) + tn(low, pick)))
    fields = []
    for c in range(4):
        pieces = []
        for face in range(4):
            along = face // 2
            if c == 0:
                pieces.append(comp(terms[face], 0))
            elif c == 1 + along:
                pieces.append((-1.0 if face % 2 else 1.0) * comp(terms[face], 0))
            else:
                tangents = [k for k in range(3) if k != along]
                pieces.append(comp(terms[face], 1 + tangents.index(c - 1)))
        value = before[c] + scale * nn2(place03[...], jnp.concatenate(pieces, axis=0))
        after[c] = value
        fields.append(value)
    if not last:
        traces = [nn2(sel45[...], x) for x in fields]
        out4, out5 = outgoing([t[:TR] for t in traces], [t[TR:] for t in traces])
        spread(at_faces(out4, out5, members[...]), pad, FACES)
        mortars[...] = jnp.zeros(mortars.shape, F32)
        to_mortars(basis, pad, mortars, (0, 1, 2), False)


def arrive(section, arrivals, receive, project, face_metric, pad, wide, out):
    high, low = halves(arrivals[...])
    pick = receive[...]
    spread(tn(high, pick) + tn(low, pick), wide, 2 * FACES)
    scale = face_metric[0:1, :] * (SECTIONS[section][2] * LIFT)
    out[...] = jnp.zeros(out.shape, F32)
    for c in range(3):
        for i in range(P_SIZE):
            total = None
            for half in range(2):
                lanes = slice(half * FACES, (half + 1) * FACES)
                for m in range(P_SIZE):
                    term = project[i, m : m + 1, lanes] * wide[c * P_SIZE + m, :, lanes]
                    total = term if total is None else total + term
            total = total * scale
            pad[c * P_SIZE + i] = total
            start = c * TR + i * P_SIZE
            out[start : start + P_SIZE, :] = total[0:P_SIZE, :]


def flux_body(
    section, arrivals, receive, send, project, basis, face_metric, mortars,
    arrived, payload, pad, wide, mixed,
):
    arrive(section, arrivals, receive, project, face_metric, pad, wide, arrived)
    mixed[...] = mortars[...]
    to_mortars(basis, pad, mixed, (1, 2), True)
    payload[...] = send_rows(send[...], mixed[...])


def last_body(
    arrivals, receive, project, face_metric, part, members, place45, after, pad, wide, arrived
):
    arrive(2, arrivals, receive, project, face_metric, pad, wide, arrived)
    result = place_interface(part, arrived, members, place45)
    for c in range(4):
        after[c] = result[c]


def exchange(rows, width):
    whole = rows.reshape(DEVICES, width, FEAT)
    moved = lax.all_to_all(whole, ("blk", "sub"), split_axis=0, concat_axis=0, tiled=True)
    return moved.reshape(DEVICES * width, FEAT)


def pass_rims(rims):
    arrived = []
    for face in range(4):
        axis = ("sub", "blk")[face // 2]
        count = lax.axis_size(axis)
        step = -1 if face % 2 else 1
        pairs = [(i, i + step) for i in range(count) if 0 <= i + step < count]
        arrived.append(lax.ppermute(rims[face ^ 1], axis, pairs))
    return arrived


def bind(body, section):
    def bound(*refs):
        body(section, *refs)

    return bound


def per_device(fields, metric, neighbours, mortar_sends, mortar_pairs):
    picks = face_rows()
    select = jnp.asarray(picks, BF16)
    sel45 = jnp.asarray(picks[4 * TR :], BF16)
    place = jnp.asarray(picks.T, BF16)
    place03 = jnp.asarray(picks[: 4 * TR].T, BF16)
    place45 = jnp.asarray(picks[4 * TR :].T, BF16)
    derive = jnp.asarray(derivative_pieces())
    metric = metric.reshape(1, ELEMS)
    whole = ((4, NODES, ELEMS), F32)
    rim = ((RIM, FEAT), F32)
    pad = pltpu.VMEM((3 * P_SIZE, 8, FACES), F32)
    wide = pltpu.VMEM((3 * P_SIZE, 8, 2 * FACES), F32)
    narrow = pltpu.VMEM((FEAT, FACES), F32)
    broad = pltpu.VMEM((FEAT, 2 * FACES), F32)

    (facts,) = call(partner_body, [((DEVICES, FEAT), F32)], (mortar_pairs,))
    facts = exchange(facts, 1)
    local, rim_out, rim_in, members, basis, project, own, info, face_metric, mortars = call(
        tables_body,
        [
            ((6, ELEMS, ELEMS), BF16),
            ((4 * RIM, ELEMS), BF16),
            ((4 * RIM, ELEMS), BF16),
            ((FACES, ELEMS), BF16),
            ((P_SIZE, 8, 2 * FACES), F32),
            ((P_SIZE, 8, 2 * FACES), F32),
            ((P_SIZE, 8, FACES), F32),
            ((16, 2 * FACES), F32),
            ((16, FACES), F32),
            ((FEAT, 2 * FACES), F32),
        ],
        (neighbours, mortar_sends, metric, fields, sel45),
        scratch=[pltpu.VMEM((2, 16, ELEMS), F32), pad],
    )
    send, receive, payload = call(
        route_body,
        [((SLOTS, 2 * FACES), BF16), ((SLOTS, 2 * FACES), BF16), ((SLOTS, FEAT), F32)],
        (facts, info, mortars),
    )
    part, arrived = fields, None
    for section in range(3):
        arrivals = exchange(payload, 4)
        lead = (part,) if section == 0 else (part, fields, arrived, place45)
        fixed = (members, local, rim_out, own, metric, neighbours, derive, select, place)
        *rims, after = call(
            bind(inner_body, section), [rim] * 4 + [whole], lead + fixed, scratch=[pad, narrow]
        )
        rims = pass_rims(rims)
        held = (after, *rims, rim_in, metric, place03)
        if section == 2:
            (part,) = call(bind(rim_body, section), [whole], held)
        else:
            part, mortars = call(
                bind(rim_body, section),
                [whole, ((FEAT, 2 * FACES), F32)],
                held + (members, basis, sel45),
                scratch=[pad],
            )
            arrived, payload = call(
                bind(flux_body, section),
                [((FEAT, FACES), F32), ((SLOTS, FEAT), F32)],
                (arrivals, receive, send, project, basis, face_metric, mortars),
                scratch=[pad, wide, broad],
            )
    (result,) = call(
        last_body,
        [whole],
        (arrivals, receive, project, face_metric, part, members, place45),
        scratch=[pad, wide, narrow],
    )
    return result


def solution(mesh):
    placed = (
        P(None, None, ("blk", "sub")),
        P(("blk", "sub")),
        P(None, ("blk", "sub")),
        P(None, ("blk", "sub")),
        P(None, ("blk", "sub")),
    )
    return jax.shard_map(
        per_device,
        mesh=mesh,
        in_specs=placed,
        out_specs=P(None, None, ("blk", "sub")),
        check_vma=False,
    )
```

time: 1320 us -> 133 us (0.10)
  the two profiles are of different devices: /device:TPU:0 before, /device:TPU:98 now
where the time goes in v1:
time: 133 us; the launch traced here: 131 us
  starting transfers between devices  72.4 us (54%)
  local copies, waits for them, and re-layouts  27.5 us (21%)
  Pallas kernels  16.7 us (13%)
  waiting for transfers between devices  13.9 us (10%)
    all_to_all x4, starting transfers between devices, exchange(): lax.all_to_all(whole, ('blk', 'sub'), split_axis=0, concat_axis=0, tiled=...  38.2 us
    ppermute x12, starting transfers between devices, pass_rims(): arrived.append(lax.ppermute(rims[face ^ 1], axis, pairs))  34.2 us
    unnamed x114, local copies, waits for them, and re-layouts  27.5 us
    pallas_call x12, Pallas kernels, call(): pl.pallas_call(body, out_shape=[jax.ShapeDtypeStruct(s, d) for s, d in ou...  16.7 us
    ppermute x12, waiting for transfers between devices, pass_rims(): arrived.append(lax.ppermute(rims[face ^ 1], axis, pairs))  13.7 us
  transfers between devices with their start and end apart: 16, of which 4 were waited for; matrix products, arithmetic and copies ran while one was open for 0% of the time, Pallas kernels for 9%

profile of v1, /device:TPU:98, one launch (start us, length us, event | category | flops | bytes accessed | tf_op | source)
XLA Modules:
  0.0 131.0 jit_solution(6425373606862462821)
XLA Ops:
  0.7 0.9 shard_map.109
  1.5 9.8 %all-to-all-start = ((f32[128,1,128]{2,1,0:T(1,128)}), f32[128,1,128]{2,1,0:T(1,128)S(1)}, u32[]{:S(2)}, u32[]{:S(2)}) async-start(f32[128,1,128]{2,1,0:T(1,128)} %bitcast.1), calls=%async_computation | async-start | bytes 131072 | tf_op jit(solution)/shard_map/all_to_all | solution.py:501
  12.1 1.2 copy-done
  13.2 1.2 shard_map.110
  17.7 0.8 shard_map.111
  18.5 0.7 copy-done.34
  19.3 9.6 %all-to-all-start.1 = ((f32[128,4,128]{2,1,0:T(4,128)}), f32[128,4,128]{2,1,0:T(4,128)S(1)}, u32[]{:S(2)}, u32[]{:S(2)}) async-start(f32[128,4,128]{2,1,0:T(4,128)} %bitcast.16), calls=%async_computation.1 | async-start | bytes 524288 | tf_op jit(solution)/shard_map/all_to_all | solution.py:501
  29.5 0.8 copy-done.16
  31.1 2.1 %shard_map.112 = (f32[32,128]{1,0:T(8,128)S(1)}, f32[32,128]{1,0:T(8,128)S(1)}, f32[32,128]{1,0:T(8,128)S(1)}, f32[32,128]{1,0:T(8,128)S(1)}, f32[4,216,256]{2,1,0:T(8,128)S(1)}) custom-call(f32[4,216,256]{2,1,0:T(8,128)S(1)} %copy-done.1, bf16[128,256]{1,0:T(8,128)(2,1)S(1)} %get-tuple-element.49.refs_1_.refs_8_.refs_4_.members, ...), custom_call_target="tpu_custom_call" | custom-call | flops 100000000 | bytes 2000000 | tf_op jit(solution)/shard_map/pallas_call | solution.py:129
  33.2 2.1 %collective-permute-start = (f32[32,128]{1,0:T(8,128)S(1)}, f32[32,128]{1,0:T(8,128)S(1)}, u32[]{:S(2)}, u32[]{:S(2)}) collective-permute-start(f32[32,128]{1,0:T(8,128)S(1)} %get-tuple-element.54), channel_id=1, source_target_pairs={{0,1},{1,2},{2,3},{3,4},{4,5},{5,6},{6,7},{8,9},{9,10},{10,11},{11... | collective-permute-start | bytes 49160 | tf_op jit(solution)/shard_map/ppermute | solution.py:512
  35.3 3.5 %collective-permute-start.1 = (f32[32,128]{1,0:T(8,128)S(1)}, f32[32,128]{1,0:T(8,128)S(1)}, u32[]{:S(2)}, u32[]{:S(2)}) collective-permute-start(f32[32,128]{1,0:T(8,128)S(1)} %get-tuple-element.55), channel_id=1, source_target_pairs={{1,0},{2,1},{3,2},{4,3},{5,4},{6,5},{7,6},{9,8},{10,9},{11,10},{12... | collective-permute-start | bytes 49160 | tf_op jit(solution)/shard_map/ppermute | solution.py:512
  38.8 2.7 %collective-permute-start.2 = (f32[32,128]{1,0:T(8,128)S(1)}, f32[32,128]{1,0:T(8,128)S(1)}, u32[]{:S(2)}, u32[]{:S(2)}) collective-permute-start(f32[32,128]{1,0:T(8,128)S(1)} %get-tuple-element.56), channel_id=1, source_target_pairs={{0,8},{8,16},{16,24},{24,32},{32,40},{40,48},{48,56},{56,64},{64,7... | collective-permute-start | bytes 49160 | tf_op jit(solution)/shard_map/ppermute | solution.py:512
  41.5 3.1 %collective-permute-start.3 = (f32[32,128]{1,0:T(8,128)S(1)}, f32[32,128]{1,0:T(8,128)S(1)}, u32[]{:S(2)}, u32[]{:S(2)}) collective-permute-start(f32[32,128]{1,0:T(8,128)S(1)} %get-tuple-element.57), channel_id=1, source_target_pairs={{8,0},{16,8},{24,16},{32,24},{40,32},{48,40},{56,48},{64,56},{72,6... | collective-permute-start | bytes 49160 | tf_op jit(solution)/shard_map/ppermute | solution.py:512
  44.7 4.6 %collective-permute-done.3.refs_4_ = f32[32,128]{1,0:T(8,128)S(1)} collective-permute-done((f32[32,128]{1,0:T(8,128)S(1)}, f32[32,128]{1,0:T(8,128)S(1)}, u32[]{:S(2)}, u32[]{:S(2)}) %collective-permute-start.3) | collective-permute-done | bytes 16416 | tf_op jit(solution)/shard_map/ppermute | solution.py:512
  49.3 1.2 shard_map.113
  50.5 0.9 copy-done.8
  52.8 0.8 copy-done.12
  53.6 0.8 copy-done.26
  54.4 0.9 copy-done.42
  55.3 0.8 shard_map.114
  56.1 0.7 copy-done.33
  57.4 9.4 %all-to-all-start.2 = ((f32[128,4,128]{2,1,0:T(4,128)}), f32[128,4,128]{2,1,0:T(4,128)S(1)}, u32[]{:S(2)}, u32[]{:S(2)}) async-start(f32[128,4,128]{2,1,0:T(4,128)} %bitcast.15), calls=%async_computation.2 | async-start | bytes 524288 | tf_op jit(solution)/shard_map/all_to_all | solution.py:501
  67.4 1.2 copy-done.9
  68.6 0.8 copy-done.17
  69.4 0.8 copy-done.23
  71.0 0.8 copy-done.50
  71.8 2.5 %shard_map.115 = (f32[32,128]{1,0:T(8,128)S(1)}, f32[32,128]{1,0:T(8,128)S(1)}, f32[32,128]{1,0:T(8,128)S(1)}, f32[32,128]{1,0:T(8,128)S(1)}, f32[4,216,256]{2,1,0:T(8,128)S(1)}) custom-call(f32[4,216,256]{2,1,0:T(8,128)S(1)} %copy-done.9, f32[4,216,256]{2,1,0:T(8,128)S(1)} %copy-done.1, f32[128,128]{1,0:T(8,128)S(1)} %copy-done.50, ...), custom_call_target="tpu_custom_call" | custom-call | flops 100000000 | bytes 2000000 | tf_op jit(solution)/shard_map/pallas_call | solution.py:129
  74.3 2.1 %collective-permute-start.4 = (f32[32,128]{1,0:T(8,128)S(1)}, f32[32,128]{1,0:T(8,128)S(1)}, u32[]{:S(2)}, u32[]{:S(2)}) collective-permute-start(f32[32,128]{1,0:T(8,128)S(1)} %get-tuple-element.64), channel_id=1, source_target_pairs={{0,1},{1,2},{2,3},{3,4},{4,5},{5,6},{6,7},{8,9},{9,10},{10,11},{11... | collective-permute-start | bytes 49160 | tf_op jit(solution)/shard_map/ppermute | solution.py:512
  76.4 3.5 %collective-permute-start.5 = (f32[32,128]{1,0:T(8,128)S(1)}, f32[32,128]{1,0:T(8,128)S(1)}, u32[]{:S(2)}, u32[]{:S(2)}) collective-permute-start(f32[32,128]{1,0:T(8,128)S(1)} %get-tuple-element.65), channel_id=1, source_target_pairs={{1,0},{2,1},{3,2},{4,3},{5,4},{6,5},{7,6},{9,8},{10,9},{11,10},{12... | collective-permute-start | bytes 49160 | tf_op jit(solution)/shard_map/ppermute | solution.py:512
  79.9 2.7 %collective-permute-start.6 = (f32[32,128]{1,0:T(8,128)S(1)}, f32[32,128]{1,0:T(8,128)S(1)}, u32[]{:S(2)}, u32[]{:S(2)}) collective-permute-start(f32[32,128]{1,0:T(8,128)S(1)} %get-tuple-element.66), channel_id=1, source_target_pairs={{0,8},{8,16},{16,24},{24,32},{32,40},{40,48},{48,56},{56,64},{64,7... | collective-permute-start | bytes 49160 | tf_op jit(solution)/shard_map/ppermute | solution.py:512
  82.6 3.1 %collective-permute-start.7 = (f32[32,128]{1,0:T(8,128)S(1)}, f32[32,128]{1,0:T(8,128)S(1)}, u32[]{:S(2)}, u32[]{:S(2)}) collective-permute-start(f32[32,128]{1,0:T(8,128)S(1)} %get-tuple-element.67), channel_id=1, source_target_pairs={{8,0},{16,8},{24,16},{32,24},{40,32},{48,40},{56,48},{64,56},{72,6... | collective-permute-start | bytes 49160 | tf_op jit(solution)/shard_map/ppermute | solution.py:512
  85.8 4.6 %collective-permute-done.7.refs_4_ = f32[32,128]{1,0:T(8,128)S(1)} collective-permute-done((f32[32,128]{1,0:T(8,128)S(1)}, f32[32,128]{1,0:T(8,128)S(1)}, u32[]{:S(2)}, u32[]{:S(2)}) %collective-permute-start.7) | collective-permute-done | bytes 16416 | tf_op jit(solution)/shard_map/ppermute | solution.py:512
  90.4 1.2 shard_map.116
  91.6 0.9 copy-done.6
  93.2 0.8 copy-done.14
  94.0 0.8 copy-done.27
  94.8 0.9 copy-done.40
  96.4 0.8 shard_map.117
  98.5 9.4 %all-to-all-start.3 = ((f32[128,4,128]{2,1,0:T(4,128)}), f32[128,4,128]{2,1,0:T(4,128)S(1)}, u32[]{:S(2)}, u32[]{:S(2)}) async-start(f32[128,4,128]{2,1,0:T(4,128)} %bitcast.14), calls=%async_computation.3 | async-start | bytes 524288 | tf_op jit(solution)/shard_map/all_to_all | solution.py:501
  108.6 1.2 copy-done.7
  109.7 2.5 %shard_map.118 = (f32[32,128]{1,0:T(8,128)S(1)}, f32[32,128]{1,0:T(8,128)S(1)}, f32[32,128]{1,0:T(8,128)S(1)}, f32[32,128]{1,0:T(8,128)S(1)}, f32[4,216,256]{2,1,0:T(8,128)S(1)}) custom-call(f32[4,216,256]{2,1,0:T(8,128)S(1)} %copy-done.7, f32[4,216,256]{2,1,0:T(8,128)S(1)} %copy-done.1, f32[128,128]{1,0:T(8,128)S(1)} %copy-done.48, ...), custom_call_target="tpu_custom_call" | custom-call | flops 100000000 | bytes 2000000 | tf_op jit(solution)/shard_map/pallas_call | solution.py:129
  112.3 2.1 %collective-permute-start.8 = (f32[32,128]{1,0:T(8,128)S(1)}, f32[32,128]{1,0:T(8,128)S(1)}, u32[]{:S(2)}, u32[]{:S(2)}) collective-permute-start(f32[32,128]{1,0:T(8,128)S(1)} %get-tuple-element.73), channel_id=1, source_target_pairs={{0,1},{1,2},{2,3},{3,4},{4,5},{5,6},{6,7},{8,9},{9,10},{10,11},{11... | collective-permute-start | bytes 49160 | tf_op jit(solution)/shard_map/ppermute | solution.py:512
  114.4 3.5 %collective-permute-start.9 = (f32[32,128]{1,0:T(8,128)S(1)}, f32[32,128]{1,0:T(8,128)S(1)}, u32[]{:S(2)}, u32[]{:S(2)}) collective-permute-start(f32[32,128]{1,0:T(8,128)S(1)} %get-tuple-element.74), channel_id=1, source_target_pairs={{1,0},{2,1},{3,2},{4,3},{5,4},{6,5},{7,6},{9,8},{10,9},{11,10},{12... | collective-permute-start | bytes 49160 | tf_op jit(solution)/shard_map/ppermute | solution.py:512
  117.9 2.7 %collective-permute-start.10 = (f32[32,128]{1,0:T(8,128)S(1)}, f32[32,128]{1,0:T(8,128)S(1)}, u32[]{:S(2)}, u32[]{:S(2)}) collective-permute-start(f32[32,128]{1,0:T(8,128)S(1)} %get-tuple-element.75), channel_id=1, source_target_pairs={{0,8},{8,16},{16,24},{24,32},{32,40},{40,48},{48,56},{56,64},{64,7... | collective-permute-start | bytes 49160 | tf_op jit(solution)/shard_map/ppermute | solution.py:512
  120.6 3.1 %collective-permute-start.11 = (f32[32,128]{1,0:T(8,128)S(1)}, f32[32,128]{1,0:T(8,128)S(1)}, u32[]{:S(2)}, u32[]{:S(2)}) collective-permute-start(f32[32,128]{1,0:T(8,128)S(1)} %get-tuple-element.76), channel_id=1, source_target_pairs={{8,0},{16,8},{24,16},{32,24},{40,32},{48,40},{56,48},{64,56},{72,6... | collective-permute-start | bytes 49160 | tf_op jit(solution)/shard_map/ppermute | solution.py:512
  123.8 4.6 %collective-permute-done.11.refs_4_ = f32[32,128]{1,0:T(8,128)S(1)} collective-permute-done((f32[32,128]{1,0:T(8,128)S(1)}, f32[32,128]{1,0:T(8,128)S(1)}, u32[]{:S(2)}, u32[]{:S(2)}) %collective-permute-start.11) | collective-permute-done | bytes 16416 | tf_op jit(solution)/shard_map/ppermute | solution.py:512
  128.3 0.7 shard_map.119.part
  129.1 1.9 %shard_map.120 = f32[4,216,256]{2,1,0:T(8,128)} custom-call(f32[512,128]{1,0:T(8,128)S(1)} %bitcast.13, bf16[512,256]{1,0:T(8,128)(2,1)S(1)} %get-tuple-element.44.refs_1_.receive, f32[6,8,256]{2,1,0:T(8,128)S(1)} %copy-done.28, f32[16,128]{1,0:T(8,128)S(1)} %copy-done.46, f32[4,216,256]{2,1,0:T(8,128)S(1)} %shard_map.119.part, ...), custom_call_target="tpu_custom_call" | custom-call | flops 100000000 | bytes 2000000 | tf_op jit(solution)/shard_map/pallas_call | solution.py:129
  (110 shorter events, 12.7 us)
Async XLA Ops:
  1.5 9.9 %copy-start.29 = (bf16[80,216]{1,0:T(8,128)(2,1)S(1)}, bf16[80,216]{1,0:T(8,128)(2,1)}, u32[]{:S(2)}) copy-start(bf16[80,216]{1,0:T(8,128)(2,1)} %constant.13.clone.sel45.refs_10_) | copy-start | bytes 103684
  1.5 9.9 %copy-start.35 = (s32[6,256]{1,0:T(8,128)S(1)}, s32[6,256]{1,0:T(8,128)}, u32[]{:S(2)}) copy-start(s32[6,256]{1,0:T(8,128)} %refs_9_.4) | copy-start | bytes 18436
  1.5 9.9 %copy-start.55 = (s32[3,512]{1,0:T(4,128)S(1)}, s32[3,512]{1,0:T(4,128)}, u32[]{:S(2)}) copy-start(s32[3,512]{1,0:T(4,128)} %sends.1) | copy-start | bytes 18436
  1.5 16.2 %all-to-all-start = ((f32[128,1,128]{2,1,0:T(1,128)}), f32[128,1,128]{2,1,0:T(1,128)S(1)}, u32[]{:S(2)}, u32[]{:S(2)}) async-start(f32[128,1,128]{2,1,0:T(1,128)} %bitcast.1), calls=%async_computation | async-start | bytes 131072 | tf_op jit(solution)/shard_map/all_to_all | solution.py:501
  12.1 1.2 copy-start
  13.2 15.6 %copy-start.1 = (f32[4,216,256]{2,1,0:T(8,128)S(1)}, f32[4,216,256]{2,1,0:T(8,128)}, u32[]{:S(2)}) copy-start(f32[4,216,256]{2,1,0:T(8,128)} %refs_1_.3) | copy-start | bytes 2654212
  17.5 11.3 %copy-start.2 = (bf16[6,216,216]{2,1,0:T(8,128)(2,1)S(1)}, bf16[6,216,216]{2,1,0:T(8,128)(2,1)}, u32[]{:S(2)}) copy-start(bf16[6,216,216]{2,1,0:T(8,128)(2,1)} %constant.17.clone.refs_7_.refs_10_) | copy-start | bytes 1679620
  19.2 9.6 %copy-start.3 = (bf16[240,216]{1,0:T(8,128)(2,1)S(1)}, bf16[240,216]{1,0:T(8,128)(2,1)}, u32[]{:S(2)}) copy-start(bf16[240,216]{1,0:T(8,128)(2,1)} %constant.12.clone.refs_8_.refs_11_) | copy-start | bytes 311044
  19.2 9.6 %copy-start.5 = (bf16[216,240]{1,0:T(8,128)(2,1)S(1)}, bf16[216,240]{1,0:T(8,128)(2,1)}, u32[]{:S(2)}) copy-start(bf16[216,240]{1,0:T(8,128)(2,1)} %constant.14.clone.refs_9_.refs_12_) | copy-start | bytes 311044
  19.3 32.8 %all-to-all-start.1 = ((f32[128,4,128]{2,1,0:T(4,128)}), f32[128,4,128]{2,1,0:T(4,128)S(1)}, u32[]{:S(2)}, u32[]{:S(2)}) async-start(f32[128,4,128]{2,1,0:T(4,128)} %bitcast.16), calls=%async_computation.1 | async-start | bytes 524288 | tf_op jit(solution)/shard_map/all_to_all | solution.py:501
  29.5 0.8 copy-start.16
  31.1 18.2 %copy-start.4 = (bf16[216,160]{1,0:T(8,128)(2,1)S(1)}, bf16[216,160]{1,0:T(8,128)(2,1)}, u32[]{:S(2)}) copy-start(bf16[216,160]{1,0:T(8,128)(2,1)} %constant.15.clone.refs_7_) | copy-start | bytes 207364
  31.1 18.2 %copy-start.11 = (f32[6,8,256]{2,1,0:T(8,128)S(1)}, f32[6,8,256]{2,1,0:T(8,128)}, u32[]{:S(2)}) copy-start(f32[6,8,256]{2,1,0:T(8,128)} %copy-done.10) | copy-start | bytes 147460
  31.1 18.2 %copy-start.20 = (bf16[128,256]{1,0:T(8,128)(2,1)S(1)}, bf16[128,256]{1,0:T(8,128)(2,1)}, u32[]{:S(2)}) copy-start(bf16[128,256]{1,0:T(8,128)(2,1)} %copy-done.19) | copy-start | bytes 196612
  31.1 18.2 %copy-start.30 = (bf16[80,216]{1,0:T(8,128)(2,1)S(1)}, bf16[80,216]{1,0:T(8,128)(2,1)}, u32[]{:S(2)}) copy-start(bf16[80,216]{1,0:T(8,128)(2,1)} %constant.13.clone.sel45.refs_10_) | copy-start | bytes 103684
  33.2 11.4 %collective-permute-start = (f32[32,128]{1,0:T(8,128)S(1)}, f32[32,128]{1,0:T(8,128)S(1)}, u32[]{:S(2)}, u32[]{:S(2)}) collective-permute-start(f32[32,128]{1,0:T(8,128)S(1)} %get-tuple-element.54), channel_id=1, source_target_pairs={{0,1},{1,2},{2,3},{3,4},{4,5},{5,6},{6,7},{8,9},{9,10},{10,11},{11... | collective-permute-start | bytes 49160 | tf_op jit(solution)/shard_map/ppermute | solution.py:512
  35.3 9.4 %collective-permute-start.1 = (f32[32,128]{1,0:T(8,128)S(1)}, f32[32,128]{1,0:T(8,128)S(1)}, u32[]{:S(2)}, u32[]{:S(2)}) collective-permute-start(f32[32,128]{1,0:T(8,128)S(1)} %get-tuple-element.55), channel_id=1, source_target_pairs={{1,0},{2,1},{3,2},{4,3},{5,4},{6,5},{7,6},{9,8},{10,9},{11,10},{12... | collective-permute-start | bytes 49160 | tf_op jit(solution)/shard_map/ppermute | solution.py:512
  38.8 5.9 %collective-permute-start.2 = (f32[32,128]{1,0:T(8,128)S(1)}, f32[32,128]{1,0:T(8,128)S(1)}, u32[]{:S(2)}, u32[]{:S(2)}) collective-permute-start(f32[32,128]{1,0:T(8,128)S(1)} %get-tuple-element.56), channel_id=1, source_target_pairs={{0,8},{8,16},{16,24},{24,32},{32,40},{40,48},{48,56},{56,64},{64,7... | collective-permute-start | bytes 49160 | tf_op jit(solution)/shard_map/ppermute | solution.py:512
  41.5 7.7 %collective-permute-start.3 = (f32[32,128]{1,0:T(8,128)S(1)}, f32[32,128]{1,0:T(8,128)S(1)}, u32[]{:S(2)}, u32[]{:S(2)}) collective-permute-start(f32[32,128]{1,0:T(8,128)S(1)} %get-tuple-element.57), channel_id=1, source_target_pairs={{8,0},{16,8},{24,16},{32,24},{40,32},{48,40},{56,48},{64,56},{72,6... | collective-permute-start | bytes 49160 | tf_op jit(solution)/shard_map/ppermute | solution.py:512
  50.5 0.9 copy-start.8
  54.4 0.9 copy-start.42
  57.4 35.8 %all-to-all-start.2 = ((f32[128,4,128]{2,1,0:T(4,128)}), f32[128,4,128]{2,1,0:T(4,128)S(1)}, u32[]{:S(2)}, u32[]{:S(2)}) async-start(f32[128,4,128]{2,1,0:T(4,128)} %bitcast.15), calls=%async_computation.2 | async-start | bytes 524288 | tf_op jit(solution)/shard_map/all_to_all | solution.py:501
  67.4 1.2 copy-start.9
  68.6 0.8 copy-start.17
  69.4 0.8 copy-start.23
  71.0 0.8 copy-start.50
  71.8 18.6 %copy-start.13 = (f32[6,8,256]{2,1,0:T(8,128)S(1)}, f32[6,8,256]{2,1,0:T(8,128)}, u32[]{:S(2)}) copy-start(f32[6,8,256]{2,1,0:T(8,128)} %copy-done.10) | copy-start | bytes 147460
  71.8 18.6 %copy-start.21 = (bf16[128,256]{1,0:T(8,128)(2,1)S(1)}, bf16[128,256]{1,0:T(8,128)(2,1)}, u32[]{:S(2)}) copy-start(bf16[128,256]{1,0:T(8,128)(2,1)} %copy-done.19) | copy-start | bytes 196612
  71.8 18.6 %copy-start.31 = (bf16[80,216]{1,0:T(8,128)(2,1)S(1)}, bf16[80,216]{1,0:T(8,128)(2,1)}, u32[]{:S(2)}) copy-start(bf16[80,216]{1,0:T(8,128)(2,1)} %constant.13.clone.sel45.refs_10_) | copy-start | bytes 103684
  74.3 11.4 %collective-permute-start.4 = (f32[32,128]{1,0:T(8,128)S(1)}, f32[32,128]{1,0:T(8,128)S(1)}, u32[]{:S(2)}, u32[]{:S(2)}) collective-permute-start(f32[32,128]{1,0:T(8,128)S(1)} %get-tuple-element.64), channel_id=1, source_target_pairs={{0,1},{1,2},{2,3},{3,4},{4,5},{5,6},{6,7},{8,9},{9,10},{10,11},{11... | collective-permute-start | bytes 49160 | tf_op jit(solution)/shard_map/ppermute | solution.py:512
  76.4 9.4 %collective-permute-start.5 = (f32[32,128]{1,0:T(8,128)S(1)}, f32[32,128]{1,0:T(8,128)S(1)}, u32[]{:S(2)}, u32[]{:S(2)}) collective-permute-start(f32[32,128]{1,0:T(8,128)S(1)} %get-tuple-element.65), channel_id=1, source_target_pairs={{1,0},{2,1},{3,2},{4,3},{5,4},{6,5},{7,6},{9,8},{10,9},{11,10},{12... | collective-permute-start | bytes 49160 | tf_op jit(solution)/shard_map/ppermute | solution.py:512
  79.9 5.9 %collective-permute-start.6 = (f32[32,128]{1,0:T(8,128)S(1)}, f32[32,128]{1,0:T(8,128)S(1)}, u32[]{:S(2)}, u32[]{:S(2)}) collective-permute-start(f32[32,128]{1,0:T(8,128)S(1)} %get-tuple-element.66), channel_id=1, source_target_pairs={{0,8},{8,16},{16,24},{24,32},{32,40},{40,48},{48,56},{56,64},{64,7... | collective-permute-start | bytes 49160 | tf_op jit(solution)/shard_map/ppermute | solution.py:512
  82.6 7.7 %collective-permute-start.7 = (f32[32,128]{1,0:T(8,128)S(1)}, f32[32,128]{1,0:T(8,128)S(1)}, u32[]{:S(2)}, u32[]{:S(2)}) collective-permute-start(f32[32,128]{1,0:T(8,128)S(1)} %get-tuple-element.67), channel_id=1, source_target_pairs={{8,0},{16,8},{24,16},{32,24},{40,32},{48,40},{56,48},{64,56},{72,6... | collective-permute-start | bytes 49160 | tf_op jit(solution)/shard_map/ppermute | solution.py:512
  91.6 0.9 copy-start.6
  94.8 0.9 copy-start.40
  98.5 9.4 %copy-start.18 = (bf16[128,256]{1,0:T(8,128)(2,1)S(1)}, bf16[128,256]{1,0:T(8,128)(2,1)}, u32[]{:S(2)}) copy-start(bf16[128,256]{1,0:T(8,128)(2,1)} %copy-done.15) | copy-start | bytes 196612
  98.5 9.4 %copy-start.24 = (bf16[216,80]{1,0:T(8,128)(2,1)S(1)}, bf16[216,80]{1,0:T(8,128)(2,1)}, u32[]{:S(2)}) copy-start(bf16[216,80]{1,0:T(8,128)(2,1)} %constant.16.clone.refs_3_.place45) | copy-start | bytes 103684
  98.5 9.4 %copy-start.38 = (s32[6,256]{1,0:T(8,128)S(1)}, s32[6,256]{1,0:T(8,128)}, u32[]{:S(2)}) copy-start(s32[6,256]{1,0:T(8,128)} %refs_9_.4) | copy-start | bytes 18436
  98.5 9.4 %copy-start.48 = (f32[128,128]{1,0:T(8,128)S(1)}, f32[128,128]{1,0:T(8,128)}, u32[]{:S(2)}) copy-start(f32[128,128]{1,0:T(8,128)} %copy-done.47) | copy-start | bytes 196612
  98.5 30.6 %all-to-all-start.3 = ((f32[128,4,128]{2,1,0:T(4,128)}), f32[128,4,128]{2,1,0:T(4,128)S(1)}, u32[]{:S(2)}, u32[]{:S(2)}) async-start(f32[128,4,128]{2,1,0:T(4,128)} %bitcast.14), calls=%async_computation.3 | async-start | bytes 524288 | tf_op jit(solution)/shard_map/all_to_all | solution.py:501
  108.6 1.2 copy-start.7
  109.7 18.6 %copy-start.22 = (bf16[128,256]{1,0:T(8,128)(2,1)S(1)}, bf16[128,256]{1,0:T(8,128)(2,1)}, u32[]{:S(2)}) copy-start(bf16[128,256]{1,0:T(8,128)(2,1)} %copy-done.19) | copy-start | bytes 196612
  112.3 11.4 %collective-permute-start.8 = (f32[32,128]{1,0:T(8,128)S(1)}, f32[32,128]{1,0:T(8,128)S(1)}, u32[]{:S(2)}, u32[]{:S(2)}) collective-permute-start(f32[32,128]{1,0:T(8,128)S(1)} %get-tuple-element.73), channel_id=1, source_target_pairs={{0,1},{1,2},{2,3},{3,4},{4,5},{5,6},{6,7},{8,9},{9,10},{10,11},{11... | collective-permute-start | bytes 49160 | tf_op jit(solution)/shard_map/ppermute | solution.py:512
  114.4 9.4 %collective-permute-start.9 = (f32[32,128]{1,0:T(8,128)S(1)}, f32[32,128]{1,0:T(8,128)S(1)}, u32[]{:S(2)}, u32[]{:S(2)}) collective-permute-start(f32[32,128]{1,0:T(8,128)S(1)} %get-tuple-element.74), channel_id=1, source_target_pairs={{1,0},{2,1},{3,2},{4,3},{5,4},{6,5},{7,6},{9,8},{10,9},{11,10},{12... | collective-permute-start | bytes 49160 | tf_op jit(solution)/shard_map/ppermute | solution.py:512
  117.9 5.9 %collective-permute-start.10 = (f32[32,128]{1,0:T(8,128)S(1)}, f32[32,128]{1,0:T(8,128)S(1)}, u32[]{:S(2)}, u32[]{:S(2)}) collective-permute-start(f32[32,128]{1,0:T(8,128)S(1)} %get-tuple-element.75), channel_id=1, source_target_pairs={{0,8},{8,16},{16,24},{24,32},{32,40},{40,48},{48,56},{56,64},{64,7... | collective-permute-start | bytes 49160 | tf_op jit(solution)/shard_map/ppermute | solution.py:512
  120.6 7.7 %collective-permute-start.11 = (f32[32,128]{1,0:T(8,128)S(1)}, f32[32,128]{1,0:T(8,128)S(1)}, u32[]{:S(2)}, u32[]{:S(2)}) collective-permute-start(f32[32,128]{1,0:T(8,128)S(1)} %get-tuple-element.76), channel_id=1, source_target_pairs={{8,0},{16,8},{24,16},{32,24},{40,32},{48,40},{56,48},{64,56},{72,6... | collective-permute-start | bytes 49160 | tf_op jit(solution)/shard_map/ppermute | solution.py:512
  128.3 0.8 copy-start.28
  128.3 0.8 copy-start.46
  (25 other events, 17.1 us)

commit v2 on v1

--- a/solution.py
+++ b/solution.py
@@ -123,6 +123,10 @@
 
 def my_device():
     return lax.axis_index("blk") * 8 + lax.axis_index("sub")
+
+
+def even_place(turn):
+    return (lax.axis_index(("sub", "blk")[turn]) & 1) == 0
 
 
 def call(body, outs, args, scratch=(), flops=1e8, moved=2e6):
@@ -371,9 +375,14 @@
         leaving.append(jnp.concatenate([cut[0] + normal] + tangent + [blank], axis=0))
         inside.append(jnp.concatenate([cut[0] - normal] + tangent + [blank], axis=0))
     leaving = [halves(x) for x in leaving]
+    parts = []
     for face in range(4):
         pick = rim_out[face * RIM : (face + 1) * RIM, :]
-        rims[face][...] = nt(pick, leaving[face][0]) + nt(pick, leaving[face][1])
+        parts.append(nt(pick, leaving[face][0]) + nt(pick, leaving[face][1]))
+    for turn, (down, up) in enumerate((parts[:2], parts[2:])):
+        even = even_place(turn)
+        rims[2 * turn][...] = jnp.where(even, up, down)
+        rims[2 * turn + 1][...] = jnp.where(even, down, up)
     spread(at_faces(inside[4], inside[5], members[...]), pad, FACES)
     mixed[...] = jnp.zeros(mixed.shape, F32)
     for c in range(3):
@@ -430,8 +439,13 @@
         members, basis, sel45, after, mortars, pad = refs[8:]
     scale = metric[...] * (SECTIONS[section][2] * LIFT)
     terms = []
-    for face, ref in enumerate((r0, r1, r2, r3)):
-        high, low = halves(ref[...])
+    got = []
+    for turn, (one, two) in enumerate(((r0, r1), (r2, r3))):
+        even = even_place(turn)
+        got.append(jnp.where(even, two[...], one[...]))
+        got.append(jnp.where(even, one[...], two[...]))
+    for face, value in enumerate(got):
+        high, low = halves(value)
         pick = rim_in[face * RIM : (face + 1) * RIM, :]
         terms.append(0.5 * (tn(high, pick) + tn(low, pick)))
     fields = []
@@ -504,12 +518,14 @@
 
 def pass_rims(rims):
     arrived = []
-    for face in range(4):
-        axis = ("sub", "blk")[face // 2]
+    for turn in range(4):
+        axis = ("sub", "blk")[turn // 2]
         count = lax.axis_size(axis)
-        step = -1 if face % 2 else 1
-        pairs = [(i, i + step) for i in range(count) if 0 <= i + step < count]
-        arrived.append(lax.ppermute(rims[face ^ 1], axis, pairs))
+        pairs = []
+        for i in range(turn % 2, count, 2):
+            j = (i + 1) % count
+            pairs += [(i, j), (j, i)]
+        arrived.append(lax.ppermute(rims[turn], axis, pairs))
     return arrived
 
 

time: 133 us -> 114 us (0.86)
  the two profiles are of different devices: /device:TPU:98 before, /device:TPU:0 now
where the time goes in v2:
time: 114 us; the launch traced here: 112 us
  starting transfers between devices  57.4 us (50%)
  local copies, waits for them, and re-layouts  27.5 us (24%)
  Pallas kernels  16.8 us (15%)
  waiting for transfers between devices  10.3 us (9%)
    all_to_all x4, starting transfers between devices, exchange(): lax.all_to_all(whole, ('blk', 'sub'), split_axis=0, concat_axis=0, tiled=...  31.5 us
    unnamed x114, local copies, waits for them, and re-layouts  27.5 us
    ppermute x12, starting transfers between devices, pass_rims(): arrived.append(lax.ppermute(rims[turn], axis, pairs))  25.9 us
    pallas_call x12, Pallas kernels, call(): pl.pallas_call(body, out_shape=[jax.ShapeDtypeStruct(s, d) for s, d in ou...  16.8 us
    ppermute x12, waiting for transfers between devices, pass_rims(): arrived.append(lax.ppermute(rims[turn], axis, pairs))  7.22 us
    all_to_all x4, waiting for transfers between devices, exchange(): lax.all_to_all(whole, ('blk', 'sub'), split_axis=0, concat_axis=0, tiled=...  3.1 us
  transfers between devices with their start and end apart: 16, of which 4 were waited for; matrix products, arithmetic and copies ran while one was open for 0% of the time, Pallas kernels for 10%

profile of v2, /device:TPU:0, one launch (start us, length us, event | category | flops | bytes accessed | tf_op | source)
XLA Modules:
  0.0 112.4 jit_solution(1068487410420855930)
XLA Ops:
  0.7 0.9 shard_map.109
  1.5 11.1 %all-to-all-start = ((f32[128,1,128]{2,1,0:T(1,128)}), f32[128,1,128]{2,1,0:T(1,128)S(1)}, u32[]{:S(2)}, u32[]{:S(2)}) async-start(f32[128,1,128]{2,1,0:T(1,128)} %bitcast.1), calls=%async_computation | async-start | bytes 131072 | tf_op jit(solution)/shard_map/all_to_all | solution.py:515
  13.4 1.2 %copy-done = f32[4,216,256]{2,1,0:T(8,128)S(1)} copy-done((f32[4,216,256]{2,1,0:T(8,128)S(1)}, f32[4,216,256]{2,1,0:T(8,128)}, u32[]{:S(2)}) %copy-start) | copy-done | bytes 884760
  14.5 1.2 %shard_map.110 = (bf16[6,256,256]{2,1,0:T(8,128)(2,1)S(1)}, bf16[128,256]{1,0:T(8,128)(2,1)S(1)}, bf16[128,256]{1,0:T(8,128)(2,1)S(1)}, bf16[128,256]{1,0:T(8,12...) custom-call(s32[6,256]{1,0:T(8,128)S(1)} %copy-done.35, ...), custom_call_target="tpu_custom_call" | custom-call | flops 100000000 | bytes 2000000 | tf_op jit(solution)/shard_map/pallas_call | solution.py:133
  18.8 3.1 %all-to-all-done = f32[128,1,128]{2,1,0:T(1,128)S(1)} async-done(((f32[128,1,128]{2,1,0:T(1,128)}), f32[128,1,128]{2,1,0:T(1,128)S(1)}, u32[]{:S(2)}, u32[]{:S(2)}) %all-to-all-start) | async-done | bytes 65568 | tf_op jit(solution)/shard_map/all_to_all | solution.py:515
  21.9 0.8 shard_map.111
  22.8 0.7 copy-done.34
  23.5 6.7 %all-to-all-start.1 = ((f32[128,4,128]{2,1,0:T(4,128)}), f32[128,4,128]{2,1,0:T(4,128)S(1)}, u32[]{:S(2)}, u32[]{:S(2)}) async-start(f32[128,4,128]{2,1,0:T(4,128)} %bitcast.16), calls=%async_computation.1 | async-start | bytes 524288 | tf_op jit(solution)/shard_map/all_to_all | solution.py:515
  30.8 0.8 copy-done.16
  32.4 2.1 %shard_map.112 = (f32[32,128]{1,0:T(8,128)S(1)}, f32[32,128]{1,0:T(8,128)S(1)}, f32[32,128]{1,0:T(8,128)S(1)}, f32[32,128]{1,0:T(8,128)S(1)}, f32[4,216,256]{2,1,0:T(8,128)S(1)}) custom-call(f32[4,216,256]{2,1,0:T(8,128)S(1)} %copy-done.1, bf16[128,256]{1,0:T(8,128)(2,1)S(1)} %get-tuple-element.49.refs_1_.refs_8_.refs_4_.members, ...), custom_call_target="tpu_custom_call" | custom-call | flops 100000000 | bytes 2000000 | tf_op jit(solution)/shard_map/pallas_call | solution.py:133
  34.6 2.3 %collective-permute-start.1 = (f32[32,128]{1,0:T(8,128)S(1)}, f32[32,128]{1,0:T(8,128)S(1)}, u32[]{:S(2)}, u32[]{:S(2)}) collective-permute-start(f32[32,128]{1,0:T(8,128)S(1)} %get-tuple-element.55), channel_id=1, source_target_pairs={{1,2},{2,1},{3,4},{4,3},{5,6},{6,5},{7,0},{0,7},{9,10},{10,9},{11,... | collective-permute-start | bytes 49160 | tf_op jit(solution)/shard_map/ppermute | solution.py:528
  36.9 1.6 %collective-permute-start.2 = (f32[32,128]{1,0:T(8,128)S(1)}, f32[32,128]{1,0:T(8,128)S(1)}, u32[]{:S(2)}, u32[]{:S(2)}) collective-permute-start(f32[32,128]{1,0:T(8,128)S(1)} %get-tuple-element.56), channel_id=1, source_target_pairs={{0,8},{8,0},{16,24},{24,16},{32,40},{40,32},{48,56},{56,48},{64,72... | collective-permute-start | bytes 49160 | tf_op jit(solution)/shard_map/ppermute | solution.py:528
  38.5 4.6 %collective-permute-start.3 = (f32[32,128]{1,0:T(8,128)S(1)}, f32[32,128]{1,0:T(8,128)S(1)}, u32[]{:S(2)}, u32[]{:S(2)}) collective-permute-start(f32[32,128]{1,0:T(8,128)S(1)} %get-tuple-element.57), channel_id=1, source_target_pairs={{8,16},{16,8},{24,32},{32,24},{40,48},{48,40},{56,64},{64,56},{72,... | collective-permute-start | bytes 49160 | tf_op jit(solution)/shard_map/ppermute | solution.py:528
  43.2 2.4 %collective-permute-done.3.refs_4_ = f32[32,128]{1,0:T(8,128)S(1)} collective-permute-done((f32[32,128]{1,0:T(8,128)S(1)}, f32[32,128]{1,0:T(8,128)S(1)}, u32[]{:S(2)}, u32[]{:S(2)}) %collective-permute-start.3) | collective-permute-done | bytes 16416 | tf_op jit(solution)/shard_map/ppermute | solution.py:528
  45.6 1.2 %shard_map.113 = (f32[4,216,256]{2,1,0:T(8,128)S(1)}, f32[128,256]{1,0:T(8,128)S(1)}) custom-call(f32[4,216,256]{2,1,0:T(8,128)S(1)} %get-tuple-element.53.refs_0_, f32[32,128]{1,0:T(8,128)S(1)} %collective-permute-done.refs_1_, f32[32,128]{1,0:T(8,128)S(1)} %collective-permute-done.1.refs_2_, f32[32,128]{1,0:T(8,128)S(1)} %collective-permute-done.2.refs_3_, ...), custom_call_target="tpu_custom_call" | custom-call | flops 100000000 | bytes 2000000 | tf_op jit(solution)/shard_map/pallas_call | solution.py:133
  46.9 0.9 copy-done.8
  48.4 0.7 copy-done.44
  49.1 0.8 copy-done.12
  49.9 0.8 copy-done.26
  50.7 0.9 copy-done.42
  51.6 0.8 shard_map.114
  52.4 0.7 copy-done.33
  53.7 6.9 %all-to-all-start.2 = ((f32[128,4,128]{2,1,0:T(4,128)}), f32[128,4,128]{2,1,0:T(4,128)S(1)}, u32[]{:S(2)}, u32[]{:S(2)}) async-start(f32[128,4,128]{2,1,0:T(4,128)} %bitcast.15), calls=%async_computation.2 | async-start | bytes 524288 | tf_op jit(solution)/shard_map/all_to_all | solution.py:515
  61.3 1.2 %copy-done.9 = f32[4,216,256]{2,1,0:T(8,128)S(1)} copy-done((f32[4,216,256]{2,1,0:T(8,128)S(1)}, f32[4,216,256]{2,1,0:T(8,128)}, u32[]{:S(2)}) %copy-start.9) | copy-done | bytes 884760
  62.4 0.8 copy-done.17
  63.3 0.8 copy-done.23
  64.8 0.8 copy-done.50
  65.6 2.5 %shard_map.115 = (f32[32,128]{1,0:T(8,128)S(1)}, f32[32,128]{1,0:T(8,128)S(1)}, f32[32,128]{1,0:T(8,128)S(1)}, f32[32,128]{1,0:T(8,128)S(1)}, f32[4,216,256]{2,1,0:T(8,128)S(1)}) custom-call(f32[4,216,256]{2,1,0:T(8,128)S(1)} %copy-done.9, f32[4,216,256]{2,1,0:T(8,128)S(1)} %copy-done.1, f32[128,128]{1,0:T(8,128)S(1)} %copy-done.50, ...), custom_call_target="tpu_custom_call" | custom-call | flops 100000000 | bytes 2000000 | tf_op jit(solution)/shard_map/pallas_call | solution.py:133
  68.3 2.3 %collective-permute-start.5 = (f32[32,128]{1,0:T(8,128)S(1)}, f32[32,128]{1,0:T(8,128)S(1)}, u32[]{:S(2)}, u32[]{:S(2)}) collective-permute-start(f32[32,128]{1,0:T(8,128)S(1)} %get-tuple-element.65), channel_id=1, source_target_pairs={{1,2},{2,1},{3,4},{4,3},{5,6},{6,5},{7,0},{0,7},{9,10},{10,9},{11,... | collective-permute-start | bytes 49160 | tf_op jit(solution)/shard_map/ppermute | solution.py:528
  70.5 1.6 %collective-permute-start.6 = (f32[32,128]{1,0:T(8,128)S(1)}, f32[32,128]{1,0:T(8,128)S(1)}, u32[]{:S(2)}, u32[]{:S(2)}) collective-permute-start(f32[32,128]{1,0:T(8,128)S(1)} %get-tuple-element.66), channel_id=1, source_target_pairs={{0,8},{8,0},{16,24},{24,16},{32,40},{40,32},{48,56},{56,48},{64,72... | collective-permute-start | bytes 49160 | tf_op jit(solution)/shard_map/ppermute | solution.py:528
  72.2 4.6 %collective-permute-start.7 = (f32[32,128]{1,0:T(8,128)S(1)}, f32[32,128]{1,0:T(8,128)S(1)}, u32[]{:S(2)}, u32[]{:S(2)}) collective-permute-start(f32[32,128]{1,0:T(8,128)S(1)} %get-tuple-element.67), channel_id=1, source_target_pairs={{8,16},{16,8},{24,32},{32,24},{40,48},{48,40},{56,64},{64,56},{72,... | collective-permute-start | bytes 49160 | tf_op jit(solution)/shard_map/ppermute | solution.py:528
  76.8 2.4 %collective-permute-done.7.refs_4_ = f32[32,128]{1,0:T(8,128)S(1)} collective-permute-done((f32[32,128]{1,0:T(8,128)S(1)}, f32[32,128]{1,0:T(8,128)S(1)}, u32[]{:S(2)}, u32[]{:S(2)}) %collective-permute-start.7) | collective-permute-done | bytes 16416 | tf_op jit(solution)/shard_map/ppermute | solution.py:528
  79.2 1.2 %shard_map.116 = (f32[4,216,256]{2,1,0:T(8,128)S(1)}, f32[128,256]{1,0:T(8,128)S(1)}) custom-call(f32[4,216,256]{2,1,0:T(8,128)S(1)} %get-tuple-element.63.refs_0_, f32[32,128]{1,0:T(8,128)S(1)} %collective-permute-done.4.refs_1_, f32[32,128]{1,0:T(8,128)S(1)} %collective-permute-done.5.refs_2_, f32[32,128]{1,0:T(8,128)S(1)} %collective-permute-done.6.refs_3_, ...), custom_call_target="tpu_custom_call" | custom-call | flops 100000000 | bytes 2000000 | tf_op jit(solution)/shard_map/pallas_call | solution.py:133
  80.5 0.9 copy-done.6
  82.1 0.8 copy-done.14
  82.9 0.8 copy-done.27
  83.7 0.9 copy-done.40
  85.3 0.8 shard_map.117
  86.1 0.7 copy-done.32
  87.4 6.9 %all-to-all-start.3 = ((f32[128,4,128]{2,1,0:T(4,128)}), f32[128,4,128]{2,1,0:T(4,128)S(1)}, u32[]{:S(2)}, u32[]{:S(2)}) async-start(f32[128,4,128]{2,1,0:T(4,128)} %bitcast.14), calls=%async_computation.3 | async-start | bytes 524288 | tf_op jit(solution)/shard_map/all_to_all | solution.py:515
  95.0 1.2 %copy-done.7 = f32[4,216,256]{2,1,0:T(8,128)S(1)} copy-done((f32[4,216,256]{2,1,0:T(8,128)S(1)}, f32[4,216,256]{2,1,0:T(8,128)}, u32[]{:S(2)}) %copy-start.7) | copy-done | bytes 884760
  96.1 2.5 %shard_map.118 = (f32[32,128]{1,0:T(8,128)S(1)}, f32[32,128]{1,0:T(8,128)S(1)}, f32[32,128]{1,0:T(8,128)S(1)}, f32[32,128]{1,0:T(8,128)S(1)}, f32[4,216,256]{2,1,0:T(8,128)S(1)}) custom-call(f32[4,216,256]{2,1,0:T(8,128)S(1)} %copy-done.7, f32[4,216,256]{2,1,0:T(8,128)S(1)} %copy-done.1, f32[128,128]{1,0:T(8,128)S(1)} %copy-done.48, ...), custom_call_target="tpu_custom_call" | custom-call | flops 100000000 | bytes 2000000 | tf_op jit(solution)/shard_map/pallas_call | solution.py:133
  98.8 2.3 %collective-permute-start.9 = (f32[32,128]{1,0:T(8,128)S(1)}, f32[32,128]{1,0:T(8,128)S(1)}, u32[]{:S(2)}, u32[]{:S(2)}) collective-permute-start(f32[32,128]{1,0:T(8,128)S(1)} %get-tuple-element.74), channel_id=1, source_target_pairs={{1,2},{2,1},{3,4},{4,3},{5,6},{6,5},{7,0},{0,7},{9,10},{10,9},{11,... | collective-permute-start | bytes 49160 | tf_op jit(solution)/shard_map/ppermute | solution.py:528
  101.0 1.6 %collective-permute-start.10 = (f32[32,128]{1,0:T(8,128)S(1)}, f32[32,128]{1,0:T(8,128)S(1)}, u32[]{:S(2)}, u32[]{:S(2)}) collective-permute-start(f32[32,128]{1,0:T(8,128)S(1)} %get-tuple-element.75), channel_id=1, source_target_pairs={{0,8},{8,0},{16,24},{24,16},{32,40},{40,32},{48,56},{56,48},{64,72... | collective-permute-start | bytes 49160 | tf_op jit(solution)/shard_map/ppermute | solution.py:528
  102.7 4.7 %collective-permute-start.11 = (f32[32,128]{1,0:T(8,128)S(1)}, f32[32,128]{1,0:T(8,128)S(1)}, u32[]{:S(2)}, u32[]{:S(2)}) collective-permute-start(f32[32,128]{1,0:T(8,128)S(1)} %get-tuple-element.76), channel_id=1, source_target_pairs={{8,16},{16,8},{24,32},{32,24},{40,48},{48,40},{56,64},{64,56},{72,... | collective-permute-start | bytes 49160 | tf_op jit(solution)/shard_map/ppermute | solution.py:528
  107.3 2.4 %collective-permute-done.11.refs_4_ = f32[32,128]{1,0:T(8,128)S(1)} collective-permute-done((f32[32,128]{1,0:T(8,128)S(1)}, f32[32,128]{1,0:T(8,128)S(1)}, u32[]{:S(2)}, u32[]{:S(2)}) %collective-permute-start.11) | collective-permute-done | bytes 16416 | tf_op jit(solution)/shard_map/ppermute | solution.py:528
  109.7 0.7 shard_map.119.part
  110.5 1.9 %shard_map.120 = f32[4,216,256]{2,1,0:T(8,128)} custom-call(f32[512,128]{1,0:T(8,128)S(1)} %bitcast.13, bf16[512,256]{1,0:T(8,128)(2,1)S(1)} %get-tuple-element.44.refs_1_.receive, f32[6,8,256]{2,1,0:T(8,128)S(1)} %copy-done.28, f32[16,128]{1,0:T(8,128)S(1)} %copy-done.46, f32[4,216,256]{2,1,0:T(8,128)S(1)} %shard_map.119.part, ...), custom_call_target="tpu_custom_call" | custom-call | flops 100000000 | bytes 2000000 | tf_op jit(solution)/shard_map/pallas_call | solution.py:133
  (110 shorter events, 11.4 us)
Async XLA Ops:
  1.5 11.2 %copy-start.29 = (bf16[80,216]{1,0:T(8,128)(2,1)S(1)}, bf16[80,216]{1,0:T(8,128)(2,1)}, u32[]{:S(2)}) copy-start(bf16[80,216]{1,0:T(8,128)(2,1)} %constant.13.clone.sel45.refs_10_) | copy-start | bytes 103684
  1.5 11.2 %copy-start.35 = (s32[6,256]{1,0:T(8,128)S(1)}, s32[6,256]{1,0:T(8,128)}, u32[]{:S(2)}) copy-start(s32[6,256]{1,0:T(8,128)} %refs_9_.4) | copy-start | bytes 18436
  1.5 11.2 %copy-start.55 = (s32[3,512]{1,0:T(4,128)S(1)}, s32[3,512]{1,0:T(4,128)}, u32[]{:S(2)}) copy-start(s32[3,512]{1,0:T(4,128)} %sends.1) | copy-start | bytes 18436
  1.5 20.4 %all-to-all-start = ((f32[128,1,128]{2,1,0:T(1,128)}), f32[128,1,128]{2,1,0:T(1,128)S(1)}, u32[]{:S(2)}, u32[]{:S(2)}) async-start(f32[128,1,128]{2,1,0:T(1,128)} %bitcast.1), calls=%async_computation | async-start | bytes 131072 | tf_op jit(solution)/shard_map/all_to_all | solution.py:515
  13.4 1.2 %copy-start = (f32[4,216,256]{2,1,0:T(8,128)S(1)}, f32[4,216,256]{2,1,0:T(8,128)}, u32[]{:S(2)}) copy-start(f32[4,216,256]{2,1,0:T(8,128)} %refs_1_.3) | copy-start | bytes 2654212
  14.5 15.6 %copy-start.1 = (f32[4,216,256]{2,1,0:T(8,128)S(1)}, f32[4,216,256]{2,1,0:T(8,128)}, u32[]{:S(2)}) copy-start(f32[4,216,256]{2,1,0:T(8,128)} %refs_1_.3) | copy-start | bytes 2654212
  18.8 11.3 %copy-start.2 = (bf16[6,216,216]{2,1,0:T(8,128)(2,1)S(1)}, bf16[6,216,216]{2,1,0:T(8,128)(2,1)}, u32[]{:S(2)}) copy-start(bf16[6,216,216]{2,1,0:T(8,128)(2,1)} %constant.17.clone.refs_7_.refs_10_) | copy-start | bytes 1679620
  23.5 6.7 %copy-start.3 = (bf16[240,216]{1,0:T(8,128)(2,1)S(1)}, bf16[240,216]{1,0:T(8,128)(2,1)}, u32[]{:S(2)}) copy-start(bf16[240,216]{1,0:T(8,128)(2,1)} %constant.12.clone.refs_8_.refs_11_) | copy-start | bytes 311044
  23.5 6.7 %copy-start.5 = (bf16[216,240]{1,0:T(8,128)(2,1)S(1)}, bf16[216,240]{1,0:T(8,128)(2,1)}, u32[]{:S(2)}) copy-start(bf16[216,240]{1,0:T(8,128)(2,1)} %constant.14.clone.refs_9_.refs_12_) | copy-start | bytes 311044
  23.5 24.9 %all-to-all-start.1 = ((f32[128,4,128]{2,1,0:T(4,128)}), f32[128,4,128]{2,1,0:T(4,128)S(1)}, u32[]{:S(2)}, u32[]{:S(2)}) async-start(f32[128,4,128]{2,1,0:T(4,128)} %bitcast.16), calls=%async_computation.1 | async-start | bytes 524288 | tf_op jit(solution)/shard_map/all_to_all | solution.py:515
  30.8 0.8 copy-start.16
  32.4 13.2 %copy-start.4 = (bf16[216,160]{1,0:T(8,128)(2,1)S(1)}, bf16[216,160]{1,0:T(8,128)(2,1)}, u32[]{:S(2)}) copy-start(bf16[216,160]{1,0:T(8,128)(2,1)} %constant.15.clone.refs_7_) | copy-start | bytes 207364
  32.4 13.2 %copy-start.11 = (f32[6,8,256]{2,1,0:T(8,128)S(1)}, f32[6,8,256]{2,1,0:T(8,128)}, u32[]{:S(2)}) copy-start(f32[6,8,256]{2,1,0:T(8,128)} %copy-done.10) | copy-start | bytes 147460
  32.4 13.2 %copy-start.20 = (bf16[128,256]{1,0:T(8,128)(2,1)S(1)}, bf16[128,256]{1,0:T(8,128)(2,1)}, u32[]{:S(2)}) copy-start(bf16[128,256]{1,0:T(8,128)(2,1)} %copy-done.19) | copy-start | bytes 196612
  32.4 13.2 %copy-start.30 = (bf16[80,216]{1,0:T(8,128)(2,1)S(1)}, bf16[80,216]{1,0:T(8,128)(2,1)}, u32[]{:S(2)}) copy-start(bf16[80,216]{1,0:T(8,128)(2,1)} %constant.13.clone.sel45.refs_10_) | copy-start | bytes 103684
  34.5 8.6 %collective-permute-start = (f32[32,128]{1,0:T(8,128)S(1)}, f32[32,128]{1,0:T(8,128)S(1)}, u32[]{:S(2)}, u32[]{:S(2)}) collective-permute-start(f32[32,128]{1,0:T(8,128)S(1)} %get-tuple-element.54), channel_id=1, source_target_pairs={{0,1},{1,0},{2,3},{3,2},{4,5},{5,4},{6,7},{7,6},{8,9},{9,8},{10,11... | collective-permute-start | bytes 49160 | tf_op jit(solution)/shard_map/ppermute | solution.py:528
  34.6 8.6 %collective-permute-start.1 = (f32[32,128]{1,0:T(8,128)S(1)}, f32[32,128]{1,0:T(8,128)S(1)}, u32[]{:S(2)}, u32[]{:S(2)}) collective-permute-start(f32[32,128]{1,0:T(8,128)S(1)} %get-tuple-element.55), channel_id=1, source_target_pairs={{1,2},{2,1},{3,4},{4,3},{5,6},{6,5},{7,0},{0,7},{9,10},{10,9},{11,... | collective-permute-start | bytes 49160 | tf_op jit(solution)/shard_map/ppermute | solution.py:528
  36.9 6.3 %collective-permute-start.2 = (f32[32,128]{1,0:T(8,128)S(1)}, f32[32,128]{1,0:T(8,128)S(1)}, u32[]{:S(2)}, u32[]{:S(2)}) collective-permute-start(f32[32,128]{1,0:T(8,128)S(1)} %get-tuple-element.56), channel_id=1, source_target_pairs={{0,8},{8,0},{16,24},{24,16},{32,40},{40,32},{48,56},{56,48},{64,72... | collective-permute-start | bytes 49160 | tf_op jit(solution)/shard_map/ppermute | solution.py:528
  38.5 7.1 %collective-permute-start.3 = (f32[32,128]{1,0:T(8,128)S(1)}, f32[32,128]{1,0:T(8,128)S(1)}, u32[]{:S(2)}, u32[]{:S(2)}) collective-permute-start(f32[32,128]{1,0:T(8,128)S(1)} %get-tuple-element.57), channel_id=1, source_target_pairs={{8,16},{16,8},{24,32},{32,24},{40,48},{48,40},{56,64},{64,56},{72,... | collective-permute-start | bytes 49160 | tf_op jit(solution)/shard_map/ppermute | solution.py:528
  46.8 0.9 copy-start.8
  50.7 0.9 copy-start.42
  53.7 28.3 %all-to-all-start.2 = ((f32[128,4,128]{2,1,0:T(4,128)}), f32[128,4,128]{2,1,0:T(4,128)S(1)}, u32[]{:S(2)}, u32[]{:S(2)}) async-start(f32[128,4,128]{2,1,0:T(4,128)} %bitcast.15), calls=%async_computation.2 | async-start | bytes 524288 | tf_op jit(solution)/shard_map/all_to_all | solution.py:515
  61.3 1.2 %copy-start.9 = (f32[4,216,256]{2,1,0:T(8,128)S(1)}, f32[4,216,256]{2,1,0:T(8,128)}, u32[]{:S(2)}) copy-start(f32[4,216,256]{2,1,0:T(8,128)} %copy-done.8) | copy-start | bytes 2654212
  62.4 0.8 copy-start.17
  63.3 0.8 copy-start.23
  64.8 0.8 copy-start.50
  65.6 13.6 %copy-start.13 = (f32[6,8,256]{2,1,0:T(8,128)S(1)}, f32[6,8,256]{2,1,0:T(8,128)}, u32[]{:S(2)}) copy-start(f32[6,8,256]{2,1,0:T(8,128)} %copy-done.10) | copy-start | bytes 147460
  65.6 13.6 %copy-start.21 = (bf16[128,256]{1,0:T(8,128)(2,1)S(1)}, bf16[128,256]{1,0:T(8,128)(2,1)}, u32[]{:S(2)}) copy-start(bf16[128,256]{1,0:T(8,128)(2,1)} %copy-done.19) | copy-start | bytes 196612
  65.6 13.6 %copy-start.31 = (bf16[80,216]{1,0:T(8,128)(2,1)S(1)}, bf16[80,216]{1,0:T(8,128)(2,1)}, u32[]{:S(2)}) copy-start(bf16[80,216]{1,0:T(8,128)(2,1)} %constant.13.clone.sel45.refs_10_) | copy-start | bytes 103684
  68.2 8.6 %collective-permute-start.4 = (f32[32,128]{1,0:T(8,128)S(1)}, f32[32,128]{1,0:T(8,128)S(1)}, u32[]{:S(2)}, u32[]{:S(2)}) collective-permute-start(f32[32,128]{1,0:T(8,128)S(1)} %get-tuple-element.64), channel_id=1, source_target_pairs={{0,1},{1,0},{2,3},{3,2},{4,5},{5,4},{6,7},{7,6},{8,9},{9,8},{10,11... | collective-permute-start | bytes 49160 | tf_op jit(solution)/shard_map/ppermute | solution.py:528
  68.3 8.6 %collective-permute-start.5 = (f32[32,128]{1,0:T(8,128)S(1)}, f32[32,128]{1,0:T(8,128)S(1)}, u32[]{:S(2)}, u32[]{:S(2)}) collective-permute-start(f32[32,128]{1,0:T(8,128)S(1)} %get-tuple-element.65), channel_id=1, source_target_pairs={{1,2},{2,1},{3,4},{4,3},{5,6},{6,5},{7,0},{0,7},{9,10},{10,9},{11,... | collective-permute-start | bytes 49160 | tf_op jit(solution)/shard_map/ppermute | solution.py:528
  70.5 6.3 %collective-permute-start.6 = (f32[32,128]{1,0:T(8,128)S(1)}, f32[32,128]{1,0:T(8,128)S(1)}, u32[]{:S(2)}, u32[]{:S(2)}) collective-permute-start(f32[32,128]{1,0:T(8,128)S(1)} %get-tuple-element.66), channel_id=1, source_target_pairs={{0,8},{8,0},{16,24},{24,16},{32,40},{40,32},{48,56},{56,48},{64,72... | collective-permute-start | bytes 49160 | tf_op jit(solution)/shard_map/ppermute | solution.py:528
  72.2 7.1 %collective-permute-start.7 = (f32[32,128]{1,0:T(8,128)S(1)}, f32[32,128]{1,0:T(8,128)S(1)}, u32[]{:S(2)}, u32[]{:S(2)}) collective-permute-start(f32[32,128]{1,0:T(8,128)S(1)} %get-tuple-element.67), channel_id=1, source_target_pairs={{8,16},{16,8},{24,32},{32,24},{40,48},{48,40},{56,64},{64,56},{72,... | collective-permute-start | bytes 49160 | tf_op jit(solution)/shard_map/ppermute | solution.py:528
  80.5 0.9 copy-start.6
  83.7 0.9 copy-start.40
  87.4 6.9 %copy-start.18 = (bf16[128,256]{1,0:T(8,128)(2,1)S(1)}, bf16[128,256]{1,0:T(8,128)(2,1)}, u32[]{:S(2)}) copy-start(bf16[128,256]{1,0:T(8,128)(2,1)} %copy-done.15) | copy-start | bytes 196612
  87.4 6.9 %copy-start.24 = (bf16[216,80]{1,0:T(8,128)(2,1)S(1)}, bf16[216,80]{1,0:T(8,128)(2,1)}, u32[]{:S(2)}) copy-start(bf16[216,80]{1,0:T(8,128)(2,1)} %constant.16.clone.refs_3_.place45) | copy-start | bytes 103684
  87.4 6.9 %copy-start.38 = (s32[6,256]{1,0:T(8,128)S(1)}, s32[6,256]{1,0:T(8,128)}, u32[]{:S(2)}) copy-start(s32[6,256]{1,0:T(8,128)} %refs_9_.4) | copy-start | bytes 18436
  87.4 6.9 %copy-start.48 = (f32[128,128]{1,0:T(8,128)S(1)}, f32[128,128]{1,0:T(8,128)}, u32[]{:S(2)}) copy-start(f32[128,128]{1,0:T(8,128)} %copy-done.47) | copy-start | bytes 196612
  87.4 23.1 %all-to-all-start.3 = ((f32[128,4,128]{2,1,0:T(4,128)}), f32[128,4,128]{2,1,0:T(4,128)S(1)}, u32[]{:S(2)}, u32[]{:S(2)}) async-start(f32[128,4,128]{2,1,0:T(4,128)} %bitcast.14), calls=%async_computation.3 | async-start | bytes 524288 | tf_op jit(solution)/shard_map/all_to_all | solution.py:515
  95.0 1.2 %copy-start.7 = (f32[4,216,256]{2,1,0:T(8,128)S(1)}, f32[4,216,256]{2,1,0:T(8,128)}, u32[]{:S(2)}) copy-start(f32[4,216,256]{2,1,0:T(8,128)} %copy-done.6) | copy-start | bytes 2654212
  96.1 13.6 %copy-start.22 = (bf16[128,256]{1,0:T(8,128)(2,1)S(1)}, bf16[128,256]{1,0:T(8,128)(2,1)}, u32[]{:S(2)}) copy-start(bf16[128,256]{1,0:T(8,128)(2,1)} %copy-done.19) | copy-start | bytes 196612
  98.7 8.7 %collective-permute-start.8 = (f32[32,128]{1,0:T(8,128)S(1)}, f32[32,128]{1,0:T(8,128)S(1)}, u32[]{:S(2)}, u32[]{:S(2)}) collective-permute-start(f32[32,128]{1,0:T(8,128)S(1)} %get-tuple-element.73), channel_id=1, source_target_pairs={{0,1},{1,0},{2,3},{3,2},{4,5},{5,4},{6,7},{7,6},{8,9},{9,8},{10,11... | collective-permute-start | bytes 49160 | tf_op jit(solution)/shard_map/ppermute | solution.py:528
  98.8 8.6 %collective-permute-start.9 = (f32[32,128]{1,0:T(8,128)S(1)}, f32[32,128]{1,0:T(8,128)S(1)}, u32[]{:S(2)}, u32[]{:S(2)}) collective-permute-start(f32[32,128]{1,0:T(8,128)S(1)} %get-tuple-element.74), channel_id=1, source_target_pairs={{1,2},{2,1},{3,4},{4,3},{5,6},{6,5},{7,0},{0,7},{9,10},{10,9},{11,... | collective-permute-start | bytes 49160 | tf_op jit(solution)/shard_map/ppermute | solution.py:528
  101.0 6.3 %collective-permute-start.10 = (f32[32,128]{1,0:T(8,128)S(1)}, f32[32,128]{1,0:T(8,128)S(1)}, u32[]{:S(2)}, u32[]{:S(2)}) collective-permute-start(f32[32,128]{1,0:T(8,128)S(1)} %get-tuple-element.75), channel_id=1, source_target_pairs={{0,8},{8,0},{16,24},{24,16},{32,40},{40,32},{48,56},{56,48},{64,72... | collective-permute-start | bytes 49160 | tf_op jit(solution)/shard_map/ppermute | solution.py:528
  102.7 7.1 %collective-permute-start.11 = (f32[32,128]{1,0:T(8,128)S(1)}, f32[32,128]{1,0:T(8,128)S(1)}, u32[]{:S(2)}, u32[]{:S(2)}) collective-permute-start(f32[32,128]{1,0:T(8,128)S(1)} %get-tuple-element.76), channel_id=1, source_target_pairs={{8,16},{16,8},{24,32},{32,24},{40,48},{48,40},{56,64},{64,56},{72,... | collective-permute-start | bytes 49160 | tf_op jit(solution)/shard_map/ppermute | solution.py:528
  109.7 0.8 copy-start.28
  109.7 0.8 copy-start.46
  (25 other events, 17.1 us)

commit v3 on v2

--- a/solution.py
+++ b/solution.py
@@ -16,11 +16,16 @@
 SLOTS = 512
 DEVICES = 128
 TR = 40
+PROJECT = 48
+METRIC = 96
+FACT_ROWS = 104
+ROUTES = FACT_ROWS + 128
+NEAR, RIM_OUT, RIM_IN, ROTOR, STATOR, SCALE, KEY_ROWS = 0, 6, 10, 14, 15, 16, 24
 FEAT = 128
 DT_STEP = 0.01
 F32 = jnp.float32
 BF16 = jnp.bfloat16
-VMEM_BYTES = 40 * 1024 * 1024
+VMEM_BYTES = 24 * 1024 * 1024
 
 
 def legendre_columns(points, npts):
@@ -129,18 +134,63 @@
     return (lax.axis_index(("sub", "blk")[turn]) & 1) == 0
 
 
+class Fetched:
+    def __init__(self, copy, buffer):
+        self.copy, self.buffer, self.here = copy, buffer, False
+
+    def __getitem__(self, key):
+        if not self.here:
+            self.copy.wait()
+            self.here = True
+        return self.buffer[key]
+
+
 def call(body, outs, args, scratch=(), flops=1e8, moved=2e6):
+    far_in = [i for i, (_, space) in enumerate(args) if space == "h"]
+    far_out = [i for i, (_, _, space) in enumerate(outs) if space == "h"]
+    own = [pltpu.VMEM(args[i][0].shape, args[i][0].dtype) for i in far_in]
+    own += [pltpu.VMEM(outs[i][0], outs[i][1]) for i in far_out]
+    count = len(far_in) + len(far_out)
+
+    def kernel(*refs):
+        refs = list(refs)
+        ins, refs = refs[: len(args)], refs[len(args) :]
+        results, refs = refs[: len(outs)], refs[len(outs) :]
+        extra, refs = refs[: len(scratch)], refs[len(scratch) :]
+        sems = refs[-1] if count else None
+        for n, i in enumerate(far_in):
+            copy = pltpu.make_async_copy(ins[i], refs[n], sems.at[n])
+            copy.start()
+            ins[i] = Fetched(copy, refs[n])
+        shown = list(results)
+        for n, i in enumerate(far_out):
+            shown[i] = refs[len(far_in) + n]
+        body(*ins, *shown, *extra)
+        for i in far_in:
+            if not ins[i].here:
+                ins[i].copy.wait()
+        copies = []
+        for n, i in enumerate(far_out):
+            spot = len(far_in) + n
+            copies.append(pltpu.make_async_copy(refs[spot], results[i], sems.at[spot]))
+            copies[-1].start()
+        for copy in copies:
+            copy.wait()
+
+    spaces = {"h": pltpu.HBM, "v": pltpu.VMEM}
     return pl.pallas_call(
-        body,
-        out_shape=[jax.ShapeDtypeStruct(s, d) for s, d in outs],
-        in_specs=[pl.BlockSpec(memory_space=pltpu.VMEM)] * len(args),
-        out_specs=[pl.BlockSpec(memory_space=pltpu.VMEM)] * len(outs),
-        scratch_shapes=list(scratch),
+        kernel,
+        out_shape=[jax.ShapeDtypeStruct(o[0], o[1]) for o in outs],
+        in_specs=[pl.BlockSpec(memory_space=spaces[space]) for _, space in args],
+        out_specs=[pl.BlockSpec(memory_space=spaces[o[2]]) for o in outs],
+        scratch_shapes=list(scratch)
+        + own
+        + ([pltpu.SemaphoreType.DMA((count,))] if count else []),
         compiler_params=pltpu.CompilerParams(vmem_limit_bytes=VMEM_BYTES),
         cost_estimate=pl.CostEstimate(
             flops=int(flops), bytes_accessed=int(moved), transcendentals=0
         ),
-    )(*args)
+    )(*[array for array, _ in args])
 
 
 def spread(values, pad, width):
@@ -150,14 +200,15 @@
         pad[group, 0:P_SIZE, 0:width] = values[start : start + P_SIZE, :]
 
 
-def to_mortars(basis, pad, out, comps, add):
+def to_mortars(facts, pad, out, comps, add):
     for half in range(2):
         lanes = slice(half * FACES, (half + 1) * FACES)
         for c in comps:
             for m in range(P_SIZE):
-                total = basis[0, m : m + 1, lanes] * pad[c * P_SIZE, :, 0:FACES]
+                total = facts[m : m + 1, lanes] * pad[c * P_SIZE, :, 0:FACES]
                 for i in range(1, P_SIZE):
-                    total += basis[i, m : m + 1, lanes] * pad[c * P_SIZE + i, :, 0:FACES]
+                    row = i * 8 + m
+                    total += facts[row : row + 1, lanes] * pad[c * P_SIZE + i, :, 0:FACES]
                 start = c * TR + m * P_SIZE
                 rows = slice(start, start + P_SIZE)
                 if add:
@@ -213,14 +264,25 @@
     out[...] = total
 
 
+def picked(keys, row, count):
+    return mark(iota((count, ELEMS), 0).astype(F32) == keys[row : row + 1, :]).astype(BF16)
+
+
+def member_picks(keys):
+    number = iota((FACES, ELEMS), 0).astype(F32)
+    rotor = number == keys[ROTOR : ROTOR + 1, :]
+    stator = number == keys[STATOR : STATOR + 1, :]
+    return mark(rotor | stator).astype(BF16)
+
+
 def tables_body(
-    neighbours, sends, metric, fields, sel45,
-    local, rim_out, rim_in, members, basis, project, own, info, face_metric, mortars,
+    neighbours, sends, metric, fields, select,
+    keys, facts, own, info, mortars,
     rows, pad,
 ):
     me = my_device()
     nb = neighbours[...]
-    face_id = iota(nb.shape, 0)
+    face_id = iota((6, ELEMS), 0)
     remote = (nb >= 0) & ((nb >> 8) != me)
     here = (nb >= 0) & ((nb >> 8) == me)
     spot = nb & 255
@@ -236,10 +298,8 @@
     same = mark(down == across).astype(BF16)
     rank = nn(flag_rows, before)
     spot_down = jnp.where(nt(same, flag_rows) > 0.5, nt(same, spot_rows), 1e4)
-    key = jnp.where(here, spot, -1)
-    for face in range(6):
-        local[face] = mark(down == key[face : face + 1, :]).astype(BF16)
-    slot = iota((RIM, ELEMS), 0).astype(F32)
+    keys[...] = jnp.zeros(keys.shape, F32)
+    keys[NEAR : NEAR + 6, :] = jnp.where(here, spot, -1).astype(F32)
     for face in range(4):
         live = flags[face : face + 1, :] > 0.5
         order = jnp.sum(
@@ -247,24 +307,23 @@
             axis=0,
             keepdims=True,
         )
-        lines = slice(face * RIM, (face + 1) * RIM)
-        rim_out[lines, :] = mark((slot == rank[face : face + 1, :]) & live).astype(BF16)
-        rim_in[lines, :] = mark((slot == order) & live).astype(BF16)
-    number = iota((FACES, ELEMS), 0)
-    wanted = number.astype(F32)
-    rotor = (wanted == rank[5:6, :]) & (flags[5:6, :] > 0.5)
-    stator = (wanted - IFD == rank[4:5, :]) & (flags[4:5, :] > 0.5)
-    member = jnp.where(number < IFD, mark(rotor), mark(stator)).astype(BF16)
-    members[...] = member
+        place = RIM_OUT + face
+        keys[place : place + 1, :] = jnp.where(live, rank[face : face + 1, :], -1.0)
+        place = RIM_IN + face
+        keys[place : place + 1, :] = jnp.where(live, order, -1.0)
+    keys[ROTOR : ROTOR + 1, :] = jnp.where(flags[5:6, :] > 0.5, rank[5:6, :], -1.0)
+    keys[STATOR : STATOR + 1, :] = jnp.where(flags[4:5, :] > 0.5, rank[4:5, :] + IFD, -1.0)
+    keys[SCALE : SCALE + 1, :] = metric[...]
+    member = member_picks(keys)
     face_of = sends[0:1, :]
     lo_of = sends[1:2, :]
     lane_of = jnp.where(face_of >= 0, face_of + jnp.where(lo_of > 0, FACES, 0), -1)
     slot_lane = mark(iota((2 * FACES, SLOTS), 0) == lane_of).astype(BF16)
     kind = iota((16, SLOTS), 0)
     number = iota((16, SLOTS), 1)
-    facts = jnp.where(kind == 0, number >> 2, 0) + jnp.where(kind == 1, number & 3, 0)
-    facts += jnp.where(kind == 2, lo_of, 0) + jnp.where(kind == 3, sends[2:3, :], 0)
-    found = nt(facts.astype(F32).astype(BF16), slot_lane)
+    lines = jnp.where(kind == 0, number >> 2, 0) + jnp.where(kind == 1, number & 3, 0)
+    lines += jnp.where(kind == 2, lo_of, 0) + jnp.where(kind == 3, sends[2:3, :], 0)
+    found = nt(lines.astype(F32).astype(BF16), slot_lane)
     info[...] = found
     lo = found[2:3, :]
     width = found[3:4, :] - lo
@@ -281,21 +340,29 @@
             if j != i:
                 term = (spots - float(POINTS[j])) * float(1.0 / (POINTS[i] - POINTS[j]))
                 product = term if product is None else product * term
-        basis[i] = product
-        project[i] = product * weight * width * float(1.0 / WEIGHTS[i])
+        facts[i * 8 : i * 8 + 8, :] = product
+        start = PROJECT + i * 8
+        facts[start : start + 8, :] = product * weight * width * float(1.0 / WEIGHTS[i])
     for i in range(P_SIZE):
         for k in range(P_SIZE):
-            term = jnp.sum(project[i] * basis[k], axis=0, keepdims=True)
-            own[i, k : k + 1, :] = term[:, 0:FACES] + term[:, FACES:]
+            start = PROJECT + i * 8
+            term = facts[start : start + 8, :] * facts[k * 8 : k * 8 + 8, :]
+            term = jnp.sum(term, axis=0, keepdims=True)
+            own[i * 8 + k : i * 8 + k + 1, :] = term[:, 0:FACES] + term[:, FACES:]
     scale = jnp.broadcast_to(metric[...], (16, ELEMS))
     high, rest = scale.astype(BF16), scale - scale.astype(BF16).astype(F32)
     middle, low = halves(rest)
-    face_metric[...] = nt(high, member) + nt(middle, member) + nt(low, member)
-    traces = [nn2(sel45[...], fields[c]) for c in range(4)]
+    scale = nt(high, member) + nt(middle, member) + nt(low, member)
+    facts[METRIC:FACT_ROWS, :] = jnp.concatenate([scale[0:8, :]] * 2, axis=1)
+    traces = [nn2(select[4 * TR : 6 * TR, :], fields[c]) for c in range(4)]
     out4, out5 = outgoing([t[:TR] for t in traces], [t[TR:] for t in traces])
     spread(at_faces(out4, out5, member), pad, FACES)
-    mortars[...] = jnp.zeros(mortars.shape, F32)
-    to_mortars(basis, pad, mortars, (0, 1, 2), False)
+    mortars[...] = jnp.zeros((FEAT, 2 * FACES), F32)
+    to_mortars(facts, pad, mortars, (0, 1, 2), False)
+
+
+def slot_picks(row):
+    return mark(iota((SLOTS, 2 * FACES), 0).astype(F32) == row).astype(BF16)
 
 
 def send_rows(exact, values):
@@ -303,7 +370,7 @@
     return nt(exact, high) + nt(exact, low)
 
 
-def route_body(facts, info, mortars, send, receive, payload):
+def route_body(facts, info, mortars, routes, payload):
     owner = info[0:1, :]
     turn = info[1:2, :]
     owner_pick = mark(iota((DEVICES, 2 * FACES), 0).astype(F32) == owner).astype(BF16)
@@ -327,82 +394,97 @@
     theirs = owner * 4.0 + other
     ahead = jnp.sum(mark(together & (mine_down < mine)), axis=0, keepdims=True)
     behind = jnp.sum(mark(together & (theirs_down < theirs)), axis=0, keepdims=True)
-    place = iota((SLOTS, 2 * FACES), 0).astype(F32)
-    sending = mark(place == partner * 4.0 + ahead).astype(BF16)
-    send[...] = sending
-    receive[...] = mark(place == partner * 4.0 + behind).astype(BF16)
-    payload[...] = send_rows(sending, mortars[...])
-
-
-def place_interface(part, arrived, members, place45):
-    to4, to5 = at_elements(arrived[...], members[...])
+    kind = iota((8, 2 * FACES), 0)
+    routes[...] = partner * 4.0 + jnp.where(kind == 0, ahead, behind)
+    payload[...] = send_rows(slot_picks(partner * 4.0 + ahead), mortars[...])
+
+
+def placed(picks, x):
+    high, low = halves(x)
+    return tn(picks, high) + tn(picks, low)
+
+
+def place_interface(part, arrived, keys, select):
+    picks = select[4 * TR : 6 * TR, :]
+    to4, to5 = at_elements(arrived[...], member_picks(keys))
     result = []
     for c in range(4):
         source = (0, 1, 2, 0)[c]
         sign5 = -1.0 if c == 3 else 1.0
         stack = jnp.concatenate([comp(to4, source), sign5 * comp(to5, source)], axis=0)
-        result.append(part[c] + nn2(place45[...], stack))
+        result.append(part[c] + placed(picks, stack))
     return result
 
 
-def inner_body(section, *refs):
-    if section == 0:
-        part, refs = refs[0], refs[1:]
-        first = part
-        arrived = None
-    else:
-        part, first, arrived, place45 = refs[:4]
-        refs = refs[4:]
-    (members, local, rim_out, own, metric, neighbours, derive, select, place) = refs[:9]
-    rims = refs[9:13]
-    after, pad, mixed = refs[13:]
-    keep, stay, rate = SECTIONS[section]
-    if section == 0:
-        fields = [part[c] for c in range(4)]
-    else:
-        fields = place_interface(part, arrived, members, place45)
-    high, low = zip(*[halves(x) for x in fields])
-    sel = select[...]
-    traces = [nn(sel, high[c]) + nn(sel, low[c]) for c in range(4)]
+def characteristics(traces, faces):
     blank = jnp.zeros((FEAT - 3 * TR, ELEMS), F32)
     leaving, inside = [], []
-    for face in range(6):
+    for face in range(faces):
         sign = 1.0 if face % 2 else -1.0
         cut = [t[face * TR : (face + 1) * TR, :] for t in traces]
         along = face // 2
         tangent = [cut[1 + c] for c in range(3) if c != along]
         normal = sign * cut[1 + along]
-        leaving.append(jnp.concatenate([cut[0] + normal] + tangent + [blank], axis=0))
+        leaving.append(halves(jnp.concatenate([cut[0] + normal] + tangent + [blank], axis=0)))
         inside.append(jnp.concatenate([cut[0] - normal] + tangent + [blank], axis=0))
-    leaving = [halves(x) for x in leaving]
+    return leaving, inside
+
+
+def edge_body(section, *refs):
+    part, keys, select = refs[:3]
+    if section == 0:
+        fields = [part[c] for c in range(4)]
+        rims = refs[3:]
+    else:
+        arrived, whole = refs[3:5]
+        fields = place_interface(part, arrived, keys, select)
+        rims = refs[5:]
+        for c in range(4):
+            whole[c] = fields[c]
+    leaving, _ = characteristics([nn2(select[0 : 4 * TR, :], x) for x in fields], 4)
     parts = []
     for face in range(4):
-        pick = rim_out[face * RIM : (face + 1) * RIM, :]
+        pick = picked(keys, RIM_OUT + face, RIM)
         parts.append(nt(pick, leaving[face][0]) + nt(pick, leaving[face][1]))
     for turn, (down, up) in enumerate((parts[:2], parts[2:])):
         even = even_place(turn)
         rims[2 * turn][...] = jnp.where(even, up, down)
         rims[2 * turn + 1][...] = jnp.where(even, down, up)
-    spread(at_faces(inside[4], inside[5], members[...]), pad, FACES)
+
+
+def inner_body(section, *refs):
+    whole, refs = refs[0], refs[1:]
+    if section:
+        first, refs = refs[0], refs[1:]
+    select, derive, neighbours, keys, own, after, pad, mixed = refs
+    keep, stay, rate = SECTIONS[section]
+    fields = [whole[c] for c in range(4)]
+    high, low = zip(*[halves(x) for x in fields])
+    sel = select[...]
+    traces = [nn(sel, high[c]) + nn(sel, low[c]) for c in range(4)]
+    leaving, inside = characteristics(traces, 6)
+    members = member_picks(keys)
+    spread(at_faces(inside[4], inside[5], members), pad, FACES)
     mixed[...] = jnp.zeros(mixed.shape, F32)
     for c in range(3):
         for i in range(P_SIZE):
-            total = own[i, 0:1, :] * pad[c * P_SIZE]
+            total = own[i * 8 : i * 8 + 1, :] * pad[c * P_SIZE]
             for k in range(1, P_SIZE):
-                total += own[i, k : k + 1, :] * pad[c * P_SIZE + k]
+                row = i * 8 + k
+                total += own[row : row + 1, :] * pad[c * P_SIZE + k]
             start = c * TR + i * P_SIZE
             mixed[start : start + P_SIZE, :] = -total[0:P_SIZE, :]
-    to4, to5 = at_elements(mixed[...], members[...])
+    to4, to5 = at_elements(mixed[...], members)
     terms = []
     for face in range(6):
-        pick = local[face]
+        pick = picked(keys, NEAR + face, ELEMS)
         arriving = nn(leaving[face ^ 1][0], pick) + nn(leaving[face ^ 1][1], pick)
         term = 0.5 * (arriving - inside[face])
         if face >= 4:
             term = jnp.where(neighbours[face : face + 1, :] == -2, 0.0, term)
             term = term + (to4, to5)[face - 4]
         terms.append(term)
-    scale = metric[...] * rate
+    scale = keys[SCALE : SCALE + 1, :] * rate
     for c in range(4):
         pieces = []
         for face in range(6):
@@ -414,7 +496,7 @@
             else:
                 tangents = [k for k in range(3) if k != along]
                 pieces.append(comp(terms[face], 1 + tangents.index(c - 1)))
-        surface = nn2(place[...], jnp.concatenate(pieces, axis=0))
+        surface = placed(sel, jnp.concatenate(pieces, axis=0))
         if c == 0:
             pairs = ((0, 1), (1, 2), (2, 3))
         else:
@@ -431,13 +513,11 @@
 
 
 def rim_body(section, *refs):
-    before, r0, r1, r2, r3, rim_in, metric, place03 = refs[:8]
+    before, r0, r1, r2, r3, select, keys, facts, routes = refs[:9]
     last = section == 2
-    if last:
-        (after,) = refs[8:]
-    else:
-        members, basis, sel45, after, mortars, pad = refs[8:]
-    scale = metric[...] * (SECTIONS[section][2] * LIFT)
+    after, pack = refs[9:11]
+    scale = keys[SCALE : SCALE + 1, :] * (SECTIONS[section][2] * LIFT)
+    terms = []
     terms = []
     got = []
     for turn, (one, two) in enumerate(((r0, r1), (r2, r3))):
@@ -446,7 +526,7 @@
         got.append(jnp.where(even, one[...], two[...]))
     for face, value in enumerate(got):
         high, low = halves(value)
-        pick = rim_in[face * RIM : (face + 1) * RIM, :]
+        pick = picked(keys, RIM_IN + face, RIM)
         terms.append(0.5 * (tn(high, pick) + tn(low, pick)))
     fields = []
     for c in range(4):
@@ -460,22 +540,26 @@
             else:
                 tangents = [k for k in range(3) if k != along]
                 pieces.append(comp(terms[face], 1 + tangents.index(c - 1)))
-        value = before[c] + scale * nn2(place03[...], jnp.concatenate(pieces, axis=0))
+        value = before[c] + scale * placed(select[0 : 4 * TR, :], jnp.concatenate(pieces, axis=0))
         after[c] = value
         fields.append(value)
+    pack[0:FACT_ROWS, :] = facts[...]
+    pack[ROUTES : ROUTES + 8, :] = routes[...]
     if not last:
-        traces = [nn2(sel45[...], x) for x in fields]
+        pad = refs[11]
+        traces = [nn2(select[4 * TR : 6 * TR, :], x) for x in fields]
         out4, out5 = outgoing([t[:TR] for t in traces], [t[TR:] for t in traces])
-        spread(at_faces(out4, out5, members[...]), pad, FACES)
-        mortars[...] = jnp.zeros(mortars.shape, F32)
-        to_mortars(basis, pad, mortars, (0, 1, 2), False)
-
-
-def arrive(section, arrivals, receive, project, face_metric, pad, wide, out):
+        spread(at_faces(out4, out5, member_picks(keys)), pad, FACES)
+        mortars = pack.at[FACT_ROWS:ROUTES, :]
+        mortars[...] = jnp.zeros((FEAT, 2 * FACES), F32)
+        to_mortars(facts, pad, mortars, (0, 1, 2), False)
+
+
+def arrive(section, arrivals, held, pad, wide, out):
     high, low = halves(arrivals[...])
-    pick = receive[...]
+    pick = slot_picks(held[ROUTES + 1 : ROUTES + 2, :])
     spread(tn(high, pick) + tn(low, pick), wide, 2 * FACES)
-    scale = face_metric[0:1, :] * (SECTIONS[section][2] * LIFT)
+    scale = held[METRIC : METRIC + 1, 0:FACES] * (SECTIONS[section][2] * LIFT)
     out[...] = jnp.zeros(out.shape, F32)
     for c in range(3):
         for i in range(P_SIZE):
@@ -483,7 +567,8 @@
             for half in range(2):
                 lanes = slice(half * FACES, (half + 1) * FACES)
                 for m in range(P_SIZE):
-                    term = project[i, m : m + 1, lanes] * wide[c * P_SIZE + m, :, lanes]
+                    row = PROJECT + i * 8 + m
+                    term = held[row : row + 1, lanes] * wide[c * P_SIZE + m, :, lanes]
                     total = term if total is None else total + term
             total = total * scale
             pad[c * P_SIZE + i] = total
@@ -491,21 +576,16 @@
             out[start : start + P_SIZE, :] = total[0:P_SIZE, :]
 
 
-def flux_body(
-    section, arrivals, receive, send, project, basis, face_metric, mortars,
-    arrived, payload, pad, wide, mixed,
-):
-    arrive(section, arrivals, receive, project, face_metric, pad, wide, arrived)
-    mixed[...] = mortars[...]
-    to_mortars(basis, pad, mixed, (1, 2), True)
-    payload[...] = send_rows(send[...], mixed[...])
-
-
-def last_body(
-    arrivals, receive, project, face_metric, part, members, place45, after, pad, wide, arrived
-):
-    arrive(2, arrivals, receive, project, face_metric, pad, wide, arrived)
-    result = place_interface(part, arrived, members, place45)
+def flux_body(section, arrivals, held, arrived, payload, pad, wide, mixed):
+    arrive(section, arrivals, held, pad, wide, arrived)
+    mixed[...] = held[FACT_ROWS:ROUTES, :]
+    to_mortars(held, pad, mixed, (1, 2), True)
+    payload[...] = send_rows(slot_picks(held[ROUTES : ROUTES + 1, :]), mixed[...])
+
+
+def last_body(arrivals, held, part, keys, select, after, pad, wide, arrived):
+    arrive(2, arrivals, held, pad, wide, arrived)
+    result = place_interface(part, arrived, keys, select)
     for c in range(4):
         after[c] = result[c]
 
@@ -537,74 +617,80 @@
 
 
 def per_device(fields, metric, neighbours, mortar_sends, mortar_pairs):
-    picks = face_rows()
-    select = jnp.asarray(picks, BF16)
-    sel45 = jnp.asarray(picks[4 * TR :], BF16)
-    place = jnp.asarray(picks.T, BF16)
-    place03 = jnp.asarray(picks[: 4 * TR].T, BF16)
-    place45 = jnp.asarray(picks[4 * TR :].T, BF16)
+    select = jnp.asarray(face_rows(), BF16)
     derive = jnp.asarray(derivative_pieces())
     metric = metric.reshape(1, ELEMS)
-    whole = ((4, NODES, ELEMS), F32)
-    rim = ((RIM, FEAT), F32)
+    whole = ((4, NODES, ELEMS), F32, "v")
+    rim = ((RIM, FEAT), F32, "v")
+    table = ((FACT_ROWS, 2 * FACES), F32, "h")
     pad = pltpu.VMEM((3 * P_SIZE, 8, FACES), F32)
     wide = pltpu.VMEM((3 * P_SIZE, 8, 2 * FACES), F32)
     narrow = pltpu.VMEM((FEAT, FACES), F32)
     broad = pltpu.VMEM((FEAT, 2 * FACES), F32)
 
-    (facts,) = call(partner_body, [((DEVICES, FEAT), F32)], (mortar_pairs,))
-    facts = exchange(facts, 1)
-    local, rim_out, rim_in, members, basis, project, own, info, face_metric, mortars = call(
+    def far(*arrays):
+        return tuple((array, "h") for array in arrays)
+
+    def near(*arrays):
+        return tuple((array, "v") for array in arrays)
+
+    (owned,) = call(partner_body, [((DEVICES, FEAT), F32, "v")], near(mortar_pairs))
+    owned = exchange(owned, 1)
+    keys, facts, own, info, mortars = call(
         tables_body,
         [
-            ((6, ELEMS, ELEMS), BF16),
-            ((4 * RIM, ELEMS), BF16),
-            ((4 * RIM, ELEMS), BF16),
-            ((FACES, ELEMS), BF16),
-            ((P_SIZE, 8, 2 * FACES), F32),
-            ((P_SIZE, 8, 2 * FACES), F32),
-            ((P_SIZE, 8, FACES), F32),
-            ((16, 2 * FACES), F32),
-            ((16, FACES), F32),
-            ((FEAT, 2 * FACES), F32),
+            ((KEY_ROWS, ELEMS), F32, "h"),
+            table,
+            ((48, FACES), F32, "h"),
+            ((16, 2 * FACES), F32, "v"),
+            ((FEAT, 2 * FACES), F32, "v"),
         ],
-        (neighbours, mortar_sends, metric, fields, sel45),
+        near(neighbours, mortar_sends, metric, fields, select),
         scratch=[pltpu.VMEM((2, 16, ELEMS), F32), pad],
     )
-    send, receive, payload = call(
+    routes, payload = call(
         route_body,
-        [((SLOTS, 2 * FACES), BF16), ((SLOTS, 2 * FACES), BF16), ((SLOTS, FEAT), F32)],
-        (facts, info, mortars),
+        [((8, 2 * FACES), F32, "h"), ((SLOTS, FEAT), F32, "v")],
+        near(owned, info, mortars),
     )
     part, arrived = fields, None
+    packed = ((ROUTES + 8, 2 * FACES), F32, "v")
     for section in range(3):
         arrivals = exchange(payload, 4)
-        lead = (part,) if section == 0 else (part, fields, arrived, place45)
-        fixed = (members, local, rim_out, own, metric, neighbours, derive, select, place)
-        *rims, after = call(
-            bind(inner_body, section), [rim] * 4 + [whole], lead + fixed, scratch=[pad, narrow]
+        edge = near(part) + far(keys) + near(select)
+        if section == 0:
+            current = near(fields)
+            rims = call(bind(edge_body, section), [rim] * 4, edge, flops=5e7)
+        else:
+            current, *rims = call(
+                bind(edge_body, section), [whole] + [rim] * 4, edge + far(arrived), flops=5e7
+            )
+            current = near(current, fields)
+        rims = pass_rims(rims)
+        (after,) = call(
+            bind(inner_body, section),
+            [whole],
+            current + near(select, derive, neighbours) + far(keys, own),
+            scratch=[pad, narrow],
+            flops=8e8,
         )
-        rims = pass_rims(rims)
-        held = (after, *rims, rim_in, metric, place03)
-        if section == 2:
-            (part,) = call(bind(rim_body, section), [whole], held)
-        else:
-            part, mortars = call(
-                bind(rim_body, section),
-                [whole, ((FEAT, 2 * FACES), F32)],
-                held + (members, basis, sel45),
-                scratch=[pad],
-            )
+        part, held = call(
+            bind(rim_body, section),
+            [whole, packed],
+            near(after, *rims, select) + far(keys, facts, routes),
+            scratch=[] if section == 2 else [pad],
+        )
+        if section < 2:
             arrived, payload = call(
                 bind(flux_body, section),
-                [((FEAT, FACES), F32), ((SLOTS, FEAT), F32)],
-                (arrivals, receive, send, project, basis, face_metric, mortars),
+                [((FEAT, FACES), F32, "h"), ((SLOTS, FEAT), F32, "v")],
+                near(arrivals, held),
                 scratch=[pad, wide, broad],
             )
     (result,) = call(
         last_body,
         [whole],
-        (arrivals, receive, project, face_metric, part, members, place45),
+        near(arrivals, held, part) + far(keys) + near(select),
         scratch=[pad, wide, narrow],
     )
     return result

time: 114 us -> 88.3 us (0.77); the launches traced: 112 us -> 88 us
  local copies, waits for them, and re-layouts: 27.5 us -> 2.51 us
  Pallas kernels: 16.8 us -> 22.9 us
  waiting for transfers between devices: 10.3 us -> 6.47 us
  starting transfers between devices: 57.4 us -> 55.6 us
    unnamed x114 -> x16, local copies, waits for them, and re-layouts: 27.5 us -> 2.51 us
    ppermute x12, waiting for transfers between devices: 7.22 us -> 0.3 us  [pass_rims(): arrived.append(lax.ppermute(rims[turn], axis, pairs))]
    pallas_call x12 -> x15, Pallas kernels: 16.8 us -> 22.9 us  [call(): pl.pallas_call(kernel, out_shape=[jax.ShapeDtypeStruct(o[0], o[1]) for o...]
    all_to_all x4, waiting for transfers between devices: 3.1 us -> 6.17 us  [exchange(): lax.all_to_all(whole, ('blk', 'sub'), split_axis=0, concat_axis=0, tiled=...]
    all_to_all x4, starting transfers between devices: 31.5 us -> 29.7 us  [exchange(): lax.all_to_all(whole, ('blk', 'sub'), split_axis=0, concat_axis=0, tiled=...]
  transfers between devices with their start and end apart: 16 -> 16, of which waited for: 4 -> 4; matrix products, arithmetic and copies ran while one was open for 0% -> 0% of each run, Pallas kernels for 10% -> 17%
where the time goes in v3:
time: 88.3 us; the launch traced here: 88 us
  starting transfers between devices  55.6 us (63%)
  Pallas kernels  22.9 us (26%)
  waiting for transfers between devices  6.47 us (7%)
  local copies, waits for them, and re-layouts  2.51 us (3%)
    all_to_all x4, starting transfers between devices, exchange(): lax.all_to_all(whole, ('blk', 'sub'), split_axis=0, concat_axis=0, tiled=...  29.7 us
    ppermute x12, starting transfers between devices, pass_rims(): arrived.append(lax.ppermute(rims[turn], axis, pairs))  25.9 us
    pallas_call x15, Pallas kernels, call(): pl.pallas_call(kernel, out_shape=[jax.ShapeDtypeStruct(o[0], o[1]) for o...  22.9 us
    all_to_all x4, waiting for transfers between devices, exchange(): lax.all_to_all(whole, ('blk', 'sub'), split_axis=0, concat_axis=0, tiled=...  6.17 us
    unnamed x16, local copies, waits for them, and re-layouts  2.51 us
  transfers between devices with their start and end apart: 16, of which 4 were waited for; matrix products, arithmetic and copies ran while one was open for 0% of the time, Pallas kernels for 17%

profile of v3, /device:TPU:0, one launch (start us, length us, event | category | flops | bytes accessed | tf_op | source)
XLA Modules:
  0.0 88.0 jit_solution(731303776949603426)
XLA Ops:
  0.0 0.7 copy-done.7
  0.7 0.9 shard_map.73
  1.5 11.1 %all-to-all-start = ((f32[128,1,128]{2,1,0:T(1,128)}), f32[128,1,128]{2,1,0:T(1,128)S(1)}, u32[]{:S(2)}, u32[]{:S(2)}) async-start(f32[128,1,128]{2,1,0:T(1,128)} %bitcast.1), calls=%async_computation | async-start | bytes 131072 | tf_op jit(solution)/shard_map/all_to_all | solution.py:595
  12.7 0.0 copy-start.6
  12.7 0.6 copy-done.6
  13.4 1.2 %copy-done = f32[4,216,256]{2,1,0:T(8,128)S(1)} copy-done((f32[4,216,256]{2,1,0:T(8,128)S(1)}, f32[4,216,256]{2,1,0:T(8,128)}, u32[]{:S(2)}) %copy-start) | copy-done | bytes 884760
  14.5 1.2 %shard_map.74 = (f32[24,256]{1,0:T(8,128)S(1)}, f32[104,256]{1,0:T(8,128)S(1)}, f32[48,128]{1,0:T(8,128)S(1)}, f32[16,256]{1,0:T(8,128)S(1)}, f32[128,256]{1,0:T(8,128)S(1)}) custom-call(s32[6,256]{1,0:T(8,128)S(1)} %copy-done.4, s32[3,512]{1,0:T(4,128)S(1)} %copy-done.5, f32[1,256]{1,0:T(1,128)S(1)} %bitcast.15, f32[4,216,256]{2,1,0:T(8,128)S(1)} %copy-done, ...), custom_call_target="tpu_custom_call" | custom-call | flops 100000000 | bytes 2000000 | tf_op jit(solution)/shard_map/pallas_call | solution.py:181
  15.8 6.2 %all-to-all-done = f32[128,1,128]{2,1,0:T(1,128)S(1)} async-done(((f32[128,1,128]{2,1,0:T(1,128)}), f32[128,1,128]{2,1,0:T(1,128)S(1)}, u32[]{:S(2)}, u32[]{:S(2)}) %all-to-all-start) | async-done | bytes 65568 | tf_op jit(solution)/shard_map/all_to_all | solution.py:595
  21.9 1.5 %shard_map.75 = (f32[8,256]{1,0:T(8,128)S(1)}, f32[512,128]{1,0:T(8,128)}) custom-call(f32[128,128]{1,0:T(8,128)S(1)} %bitcast.14, f32[16,256]{1,0:T(8,128)S(1)} %get-tuple-element.36.refs_1_, f32[128,256]{1,0:T(8,128)S(1)} %get-tuple-element.37.refs_2_), custom_call_target="tpu_custom_call" | custom-call | flops 100000000 | bytes 2000000 | tf_op jit(solution)/shard_map/pallas_call | solution.py:181
  23.5 0.0 copy-start.3
  23.5 4.8 %all-to-all-start.1 = ((f32[128,4,128]{2,1,0:T(4,128)}), f32[128,4,128]{2,1,0:T(4,128)S(1)}, u32[]{:S(2)}, u32[]{:S(2)}) async-start(f32[128,4,128]{2,1,0:T(4,128)} %bitcast.4), calls=%async_computation.1 | async-start | bytes 524288 | tf_op jit(solution)/shard_map/all_to_all | solution.py:595
  28.3 0.8 shard_map.77
  29.1 0.1 collective-permute-start
  29.2 2.3 %collective-permute-start.1 = (f32[32,128]{1,0:T(8,128)S(1)}, f32[32,128]{1,0:T(8,128)S(1)}, u32[]{:S(2)}, u32[]{:S(2)}) collective-permute-start(f32[32,128]{1,0:T(8,128)S(1)} %get-tuple-element.42), channel_id=1, source_target_pairs={{1,2},{2,1},{3,4},{4,3},{5,6},{6,5},{7,0},{0,7},{9,10},{10,9},{11,... | collective-permute-start | bytes 49160 | tf_op jit(solution)/shard_map/ppermute | solution.py:608
  31.5 1.6 %collective-permute-start.2 = (f32[32,128]{1,0:T(8,128)S(1)}, f32[32,128]{1,0:T(8,128)S(1)}, u32[]{:S(2)}, u32[]{:S(2)}) collective-permute-start(f32[32,128]{1,0:T(8,128)S(1)} %get-tuple-element.43), channel_id=1, source_target_pairs={{0,8},{8,0},{16,24},{24,16},{32,40},{40,32},{48,56},{56,48},{64,72... | collective-permute-start | bytes 49160 | tf_op jit(solution)/shard_map/ppermute | solution.py:608
  33.1 4.6 %collective-permute-start.3 = (f32[32,128]{1,0:T(8,128)S(1)}, f32[32,128]{1,0:T(8,128)S(1)}, u32[]{:S(2)}, u32[]{:S(2)}) collective-permute-start(f32[32,128]{1,0:T(8,128)S(1)} %get-tuple-element.44), channel_id=1, source_target_pairs={{8,16},{16,8},{24,32},{32,24},{40,48},{48,40},{56,64},{64,56},{72,... | collective-permute-start | bytes 49160 | tf_op jit(solution)/shard_map/ppermute | solution.py:608
  37.7 2.3 %shard_map.76.refs_0_ = f32[4,216,256]{2,1,0:T(8,128)S(1)} custom-call(f32[4,216,256]{2,1,0:T(8,128)S(1)} %copy-done.1, bf16[240,216]{1,0:T(8,128)(2,1)S(1)} %copy-done.2, bf16[6,216,216]{2,1,0:T(8,128)(2,1)S(1)} %copy-done.3, s32[6,256]{1,0:T(8,128)S(1)} %copy-done.4, f32[24,256]{1,0:T(8,128)S(1)} %get-tuple-element.39.refs_4_.refs_1_.refs_6_.refs_5_.refs_3_, ...), custom_call_target="tpu_custom_call" | custom-call | flops 800000000 | bytes 2000000 | tf_op jit(solution)/shard_map/pallas_call | solution.py:181
  40.0 0.0 collective-permute-done.refs_1_
  40.0 0.0 collective-permute-done.1.refs_2_
  40.0 0.0 collective-permute-done.2.refs_3_
  40.1 0.1 collective-permute-done.3.refs_4_
  40.1 1.5 %shard_map.78 = (f32[4,216,256]{2,1,0:T(8,128)S(1)}, f32[240,256]{1,0:T(8,128)S(1)}) custom-call(f32[4,216,256]{2,1,0:T(8,128)S(1)} %shard_map.76.refs_0_, f32[32,128]{1,0:T(8,128)S(1)} %collective-permute-done.refs_1_, f32[32,128]{1,0:T(8,128)S(1)} %collective-permute-done.1.refs_2_, f32[32,128]{1,0:T(8,128)S(1)} %collective-permute-done.2.refs_3_, ...), custom_call_target="tpu_custom_call" | custom-call | flops 100000000 | bytes 2000000 | tf_op jit(solution)/shard_map/pallas_call | solution.py:181
  41.7 0.0 all-to-all-done.1
  41.7 1.6 %shard_map.79 = (f32[128,128]{1,0:T(8,128)S(1)}, f32[512,128]{1,0:T(8,128)}) custom-call(f32[512,128]{1,0:T(8,128)S(1)} %bitcast.13, f32[240,256]{1,0:T(8,128)S(1)} %get-tuple-element.47.refs_1_), custom_call_target="tpu_custom_call" | custom-call | flops 100000000 | bytes 2000000 | tf_op jit(solution)/shard_map/pallas_call | solution.py:181
  43.3 6.9 %all-to-all-start.2 = ((f32[128,4,128]{2,1,0:T(4,128)}), f32[128,4,128]{2,1,0:T(4,128)S(1)}, u32[]{:S(2)}, u32[]{:S(2)}) async-start(f32[128,4,128]{2,1,0:T(4,128)} %bitcast.6), calls=%async_computation.2 | async-start | bytes 524288 | tf_op jit(solution)/shard_map/all_to_all | solution.py:595
  50.2 1.3 %shard_map.80 = (f32[4,216,256]{2,1,0:T(8,128)S(1)}, f32[32,128]{1,0:T(8,128)S(1)}, f32[32,128]{1,0:T(8,128)S(1)}, f32[32,128]{1,0:T(8,128)S(1)}, f32[32,128]{1,0:T(8,128)S(1)}) custom-call(f32[4,216,256]{2,1,0:T(8,128)S(1)} %get-tuple-element.49.refs_0_, f32[24,256]{1,0:T(8,128)S(1)} %get-tuple-element.39.refs_4_.refs_1_.refs_6_.refs_5_.refs_3_, ...), custom_call_target="tpu_custom_call" | custom-call | flops 50000000 | bytes 2000000 | tf_op jit(solution)/shard_map/pallas_call | solution.py:181
  51.5 0.1 collective-permute-start.4
  51.6 2.3 %collective-permute-start.5 = (f32[32,128]{1,0:T(8,128)S(1)}, f32[32,128]{1,0:T(8,128)S(1)}, u32[]{:S(2)}, u32[]{:S(2)}) collective-permute-start(f32[32,128]{1,0:T(8,128)S(1)} %get-tuple-element.53), channel_id=1, source_target_pairs={{1,2},{2,1},{3,4},{4,3},{5,6},{6,5},{7,0},{0,7},{9,10},{10,9},{11,... | collective-permute-start | bytes 49160 | tf_op jit(solution)/shard_map/ppermute | solution.py:608
  53.8 1.6 %collective-permute-start.6 = (f32[32,128]{1,0:T(8,128)S(1)}, f32[32,128]{1,0:T(8,128)S(1)}, u32[]{:S(2)}, u32[]{:S(2)}) collective-permute-start(f32[32,128]{1,0:T(8,128)S(1)} %get-tuple-element.54), channel_id=1, source_target_pairs={{0,8},{8,0},{16,24},{24,16},{32,40},{40,32},{48,56},{56,48},{64,72... | collective-permute-start | bytes 49160 | tf_op jit(solution)/shard_map/ppermute | solution.py:608
  55.5 4.6 %collective-permute-start.7 = (f32[32,128]{1,0:T(8,128)S(1)}, f32[32,128]{1,0:T(8,128)S(1)}, u32[]{:S(2)}, u32[]{:S(2)}) collective-permute-start(f32[32,128]{1,0:T(8,128)S(1)} %get-tuple-element.55), channel_id=1, source_target_pairs={{8,16},{16,8},{24,32},{32,24},{40,48},{48,40},{56,64},{64,56},{72,... | collective-permute-start | bytes 49160 | tf_op jit(solution)/shard_map/ppermute | solution.py:608
  60.1 2.3 %shard_map.81.refs_0_ = f32[4,216,256]{2,1,0:T(8,128)S(1)} custom-call(f32[4,216,256]{2,1,0:T(8,128)S(1)} %get-tuple-element.51.refs_0_, f32[4,216,256]{2,1,0:T(8,128)S(1)} %copy-done.1, bf16[240,216]{1,0:T(8,128)(2,1)S(1)} %copy-done.2, bf16[6,216,216]{2,1,0:T(8,128)(2,1)S(1)} %copy-done.3, s32[6,256]{1,0:T(8,128)S(1)} %copy-done.4, ...), custom_call_target="tpu_custom_call" | custom-call | flops 800000000 | bytes 2000000 | tf_op jit(solution)/shard_map/pallas_call | solution.py:181
  62.4 0.0 collective-permute-done.5.refs_2_
  62.4 0.1 collective-permute-done.7.refs_4_
  62.5 1.5 %shard_map.82 = (f32[4,216,256]{2,1,0:T(8,128)S(1)}, f32[240,256]{1,0:T(8,128)S(1)}) custom-call(f32[4,216,256]{2,1,0:T(8,128)S(1)} %shard_map.81.refs_0_, f32[32,128]{1,0:T(8,128)S(1)} %collective-permute-done.4.refs_1_, f32[32,128]{1,0:T(8,128)S(1)} %collective-permute-done.5.refs_2_, f32[32,128]{1,0:T(8,128)S(1)} %collective-permute-done.6.refs_3_, ...), custom_call_target="tpu_custom_call" | custom-call | flops 100000000 | bytes 2000000 | tf_op jit(solution)/shard_map/pallas_call | solution.py:181
  64.1 1.6 %shard_map.83 = (f32[128,128]{1,0:T(8,128)S(1)}, f32[512,128]{1,0:T(8,128)}) custom-call(f32[512,128]{1,0:T(8,128)S(1)} %bitcast.12, f32[240,256]{1,0:T(8,128)S(1)} %get-tuple-element.56.refs_1_), custom_call_target="tpu_custom_call" | custom-call | flops 100000000 | bytes 2000000 | tf_op jit(solution)/shard_map/pallas_call | solution.py:181
  65.7 6.9 %all-to-all-start.3 = ((f32[128,4,128]{2,1,0:T(4,128)}), f32[128,4,128]{2,1,0:T(4,128)S(1)}, u32[]{:S(2)}, u32[]{:S(2)}) async-start(f32[128,4,128]{2,1,0:T(4,128)} %bitcast.8), calls=%async_computation.3 | async-start | bytes 524288 | tf_op jit(solution)/shard_map/all_to_all | solution.py:595
  72.6 1.3 %shard_map.84 = (f32[4,216,256]{2,1,0:T(8,128)S(1)}, f32[32,128]{1,0:T(8,128)S(1)}, f32[32,128]{1,0:T(8,128)S(1)}, f32[32,128]{1,0:T(8,128)S(1)}, f32[32,128]{1,0:T(8,128)S(1)}) custom-call(f32[4,216,256]{2,1,0:T(8,128)S(1)} %get-tuple-element.58.refs_0_, f32[24,256]{1,0:T(8,128)S(1)} %get-tuple-element.39.refs_4_.refs_1_.refs_6_.refs_5_.refs_3_, ...), custom_call_target="tpu_custom_call" | custom-call | flops 50000000 | bytes 2000000 | tf_op jit(solution)/shard_map/pallas_call | solution.py:181
  73.9 0.1 collective-permute-start.8
  74.0 2.3 %collective-permute-start.9 = (f32[32,128]{1,0:T(8,128)S(1)}, f32[32,128]{1,0:T(8,128)S(1)}, u32[]{:S(2)}, u32[]{:S(2)}) collective-permute-start(f32[32,128]{1,0:T(8,128)S(1)} %get-tuple-element.62), channel_id=1, source_target_pairs={{1,2},{2,1},{3,4},{4,3},{5,6},{6,5},{7,0},{0,7},{9,10},{10,9},{11,... | collective-permute-start | bytes 49160 | tf_op jit(solution)/shard_map/ppermute | solution.py:608
  76.2 1.6 %collective-permute-start.10 = (f32[32,128]{1,0:T(8,128)S(1)}, f32[32,128]{1,0:T(8,128)S(1)}, u32[]{:S(2)}, u32[]{:S(2)}) collective-permute-start(f32[32,128]{1,0:T(8,128)S(1)} %get-tuple-element.63), channel_id=1, source_target_pairs={{0,8},{8,0},{16,24},{24,16},{32,40},{40,32},{48,56},{56,48},{64,72... | collective-permute-start | bytes 49160 | tf_op jit(solution)/shard_map/ppermute | solution.py:608
  77.9 4.6 %collective-permute-start.11 = (f32[32,128]{1,0:T(8,128)S(1)}, f32[32,128]{1,0:T(8,128)S(1)}, u32[]{:S(2)}, u32[]{:S(2)}) collective-permute-start(f32[32,128]{1,0:T(8,128)S(1)} %get-tuple-element.64), channel_id=1, source_target_pairs={{8,16},{16,8},{24,32},{32,24},{40,48},{48,40},{56,64},{64,56},{72,... | collective-permute-start | bytes 49160 | tf_op jit(solution)/shard_map/ppermute | solution.py:608
  82.5 2.3 %shard_map.85.refs_0_ = f32[4,216,256]{2,1,0:T(8,128)S(1)} custom-call(f32[4,216,256]{2,1,0:T(8,128)S(1)} %get-tuple-element.60.refs_0_, f32[4,216,256]{2,1,0:T(8,128)S(1)} %copy-done.1, bf16[240,216]{1,0:T(8,128)(2,1)S(1)} %copy-done.2, bf16[6,216,216]{2,1,0:T(8,128)(2,1)S(1)} %copy-done.3, s32[6,256]{1,0:T(8,128)S(1)} %copy-done.4, ...), custom_call_target="tpu_custom_call" | custom-call | flops 800000000 | bytes 2000000 | tf_op jit(solution)/shard_map/pallas_call | solution.py:181
  84.8 0.0 collective-permute-done.9.refs_2_
  84.8 0.0 collective-permute-done.10.refs_3_
  84.8 0.1 collective-permute-done.11.refs_4_
  84.9 0.9 %shard_map.86 = (f32[4,216,256]{2,1,0:T(8,128)S(1)}, f32[240,256]{1,0:T(8,128)S(1)}) custom-call(f32[4,216,256]{2,1,0:T(8,128)S(1)} %shard_map.85.refs_0_, f32[32,128]{1,0:T(8,128)S(1)} %collective-permute-done.8.refs_1_, f32[32,128]{1,0:T(8,128)S(1)} %collective-permute-done.9.refs_2_, f32[32,128]{1,0:T(8,128)S(1)} %collective-permute-done.10.refs_3_, ...), custom_call_target="tpu_custom_call" | custom-call | flops 100000000 | bytes 2000000 | tf_op jit(solution)/shard_map/pallas_call | solution.py:181
  85.8 0.0 all-to-all-done.3
  85.8 2.0 %shard_map.87 = f32[4,216,256]{2,1,0:T(8,128)} custom-call(f32[512,128]{1,0:T(8,128)S(1)} %bitcast.11, f32[240,256]{1,0:T(8,128)S(1)} %get-tuple-element.65.refs_1_, f32[4,216,256]{2,1,0:T(8,128)S(1)} %get-tuple-element.66.refs_2_, f32[24,256]{1,0:T(8,128)S(1)} %get-tuple-element.39.refs_4_.refs_1_.refs_6_.refs_5_.refs_3_, bf16[240,216]{1,0:T(8,128)(2,1)S(1)} %copy-done.2), custom_call_target="tpu_custom_call" | custom-call | flops 100000000 | bytes 2000000 | tf_op jit(solution)/shard_map/pallas_call | solution.py:181
  (15 shorter events, 0.0 us)
Async XLA Ops:
  0.0 0.7 copy-start.7
  0.7 12.0 %copy-start.5 = (s32[3,512]{1,0:T(4,128)S(1)}, s32[3,512]{1,0:T(4,128)}, u32[]{:S(2)}) copy-start(s32[3,512]{1,0:T(4,128)} %refs_1_.4) | copy-start | bytes 18436
  1.5 11.2 %copy-start.2 = (bf16[240,216]{1,0:T(8,128)(2,1)S(1)}, bf16[240,216]{1,0:T(8,128)(2,1)}, u32[]{:S(2)}) copy-start(bf16[240,216]{1,0:T(8,128)(2,1)} %constant.4.clone.refs_4_.refs_1_.refs_2_.refs_5_) | copy-start | bytes 311044
  1.5 11.2 %copy-start.4 = (s32[6,256]{1,0:T(8,128)S(1)}, s32[6,256]{1,0:T(8,128)}, u32[]{:S(2)}) copy-start(s32[6,256]{1,0:T(8,128)} %refs_4_.5) | copy-start | bytes 18436
  1.5 20.4 %all-to-all-start = ((f32[128,1,128]{2,1,0:T(1,128)}), f32[128,1,128]{2,1,0:T(1,128)S(1)}, u32[]{:S(2)}, u32[]{:S(2)}) async-start(f32[128,1,128]{2,1,0:T(1,128)} %bitcast.1), calls=%async_computation | async-start | bytes 131072 | tf_op jit(solution)/shard_map/all_to_all | solution.py:595
  12.7 0.7 copy-start.6
  13.4 1.2 %copy-start = (f32[4,216,256]{2,1,0:T(8,128)S(1)}, f32[4,216,256]{2,1,0:T(8,128)}, u32[]{:S(2)}) copy-start(f32[4,216,256]{2,1,0:T(8,128)} %refs_1_.6) | copy-start | bytes 2654212
  14.5 13.7 %copy-start.1 = (f32[4,216,256]{2,1,0:T(8,128)S(1)}, f32[4,216,256]{2,1,0:T(8,128)}, u32[]{:S(2)}) copy-start(f32[4,216,256]{2,1,0:T(8,128)} %refs_1_.6) | copy-start | bytes 2654212
  23.5 14.3 %copy-start.3 = (bf16[6,216,216]{2,1,0:T(8,128)(2,1)S(1)}, bf16[6,216,216]{2,1,0:T(8,128)(2,1)}, u32[]{:S(2)}) copy-start(bf16[6,216,216]{2,1,0:T(8,128)(2,1)} %constant.5.clone.refs_2_.refs_3_) | copy-start | bytes 1679620
  23.5 18.2 %all-to-all-start.1 = ((f32[128,4,128]{2,1,0:T(4,128)}), f32[128,4,128]{2,1,0:T(4,128)S(1)}, u32[]{:S(2)}, u32[]{:S(2)}) async-start(f32[128,4,128]{2,1,0:T(4,128)} %bitcast.4), calls=%async_computation.1 | async-start | bytes 524288 | tf_op jit(solution)/shard_map/all_to_all | solution.py:595
  29.1 10.9 %collective-permute-start = (f32[32,128]{1,0:T(8,128)S(1)}, f32[32,128]{1,0:T(8,128)S(1)}, u32[]{:S(2)}, u32[]{:S(2)}) collective-permute-start(f32[32,128]{1,0:T(8,128)S(1)} %get-tuple-element.41), channel_id=1, source_target_pairs={{0,1},{1,0},{2,3},{3,2},{4,5},{5,4},{6,7},{7,6},{8,9},{9,8},{10,11... | collective-permute-start | bytes 49160 | tf_op jit(solution)/shard_map/ppermute | solution.py:608
  29.2 10.9 %collective-permute-start.1 = (f32[32,128]{1,0:T(8,128)S(1)}, f32[32,128]{1,0:T(8,128)S(1)}, u32[]{:S(2)}, u32[]{:S(2)}) collective-permute-start(f32[32,128]{1,0:T(8,128)S(1)} %get-tuple-element.42), channel_id=1, source_target_pairs={{1,2},{2,1},{3,4},{4,3},{5,6},{6,5},{7,0},{0,7},{9,10},{10,9},{11,... | collective-permute-start | bytes 49160 | tf_op jit(solution)/shard_map/ppermute | solution.py:608
  31.5 8.6 %collective-permute-start.2 = (f32[32,128]{1,0:T(8,128)S(1)}, f32[32,128]{1,0:T(8,128)S(1)}, u32[]{:S(2)}, u32[]{:S(2)}) collective-permute-start(f32[32,128]{1,0:T(8,128)S(1)} %get-tuple-element.43), channel_id=1, source_target_pairs={{0,8},{8,0},{16,24},{24,16},{32,40},{40,32},{48,56},{56,48},{64,72... | collective-permute-start | bytes 49160 | tf_op jit(solution)/shard_map/ppermute | solution.py:608
  33.1 7.1 %collective-permute-start.3 = (f32[32,128]{1,0:T(8,128)S(1)}, f32[32,128]{1,0:T(8,128)S(1)}, u32[]{:S(2)}, u32[]{:S(2)}) collective-permute-start(f32[32,128]{1,0:T(8,128)S(1)} %get-tuple-element.44), channel_id=1, source_target_pairs={{8,16},{16,8},{24,32},{32,24},{40,48},{48,40},{56,64},{64,56},{72,... | collective-permute-start | bytes 49160 | tf_op jit(solution)/shard_map/ppermute | solution.py:608
  43.3 20.8 %all-to-all-start.2 = ((f32[128,4,128]{2,1,0:T(4,128)}), f32[128,4,128]{2,1,0:T(4,128)S(1)}, u32[]{:S(2)}, u32[]{:S(2)}) async-start(f32[128,4,128]{2,1,0:T(4,128)} %bitcast.6), calls=%async_computation.2 | async-start | bytes 524288 | tf_op jit(solution)/shard_map/all_to_all | solution.py:595
  51.5 10.9 %collective-permute-start.4 = (f32[32,128]{1,0:T(8,128)S(1)}, f32[32,128]{1,0:T(8,128)S(1)}, u32[]{:S(2)}, u32[]{:S(2)}) collective-permute-start(f32[32,128]{1,0:T(8,128)S(1)} %get-tuple-element.52), channel_id=1, source_target_pairs={{0,1},{1,0},{2,3},{3,2},{4,5},{5,4},{6,7},{7,6},{8,9},{9,8},{10,11... | collective-permute-start | bytes 49160 | tf_op jit(solution)/shard_map/ppermute | solution.py:608
  51.6 10.9 %collective-permute-start.5 = (f32[32,128]{1,0:T(8,128)S(1)}, f32[32,128]{1,0:T(8,128)S(1)}, u32[]{:S(2)}, u32[]{:S(2)}) collective-permute-start(f32[32,128]{1,0:T(8,128)S(1)} %get-tuple-element.53), channel_id=1, source_target_pairs={{1,2},{2,1},{3,4},{4,3},{5,6},{6,5},{7,0},{0,7},{9,10},{10,9},{11,... | collective-permute-start | bytes 49160 | tf_op jit(solution)/shard_map/ppermute | solution.py:608
  53.8 8.6 %collective-permute-start.6 = (f32[32,128]{1,0:T(8,128)S(1)}, f32[32,128]{1,0:T(8,128)S(1)}, u32[]{:S(2)}, u32[]{:S(2)}) collective-permute-start(f32[32,128]{1,0:T(8,128)S(1)} %get-tuple-element.54), channel_id=1, source_target_pairs={{0,8},{8,0},{16,24},{24,16},{32,40},{40,32},{48,56},{56,48},{64,72... | collective-permute-start | bytes 49160 | tf_op jit(solution)/shard_map/ppermute | solution.py:608
  55.5 7.1 %collective-permute-start.7 = (f32[32,128]{1,0:T(8,128)S(1)}, f32[32,128]{1,0:T(8,128)S(1)}, u32[]{:S(2)}, u32[]{:S(2)}) collective-permute-start(f32[32,128]{1,0:T(8,128)S(1)} %get-tuple-element.55), channel_id=1, source_target_pairs={{8,16},{16,8},{24,32},{32,24},{40,48},{48,40},{56,64},{64,56},{72,... | collective-permute-start | bytes 49160 | tf_op jit(solution)/shard_map/ppermute | solution.py:608
  65.7 20.1 %all-to-all-start.3 = ((f32[128,4,128]{2,1,0:T(4,128)}), f32[128,4,128]{2,1,0:T(4,128)S(1)}, u32[]{:S(2)}, u32[]{:S(2)}) async-start(f32[128,4,128]{2,1,0:T(4,128)} %bitcast.8), calls=%async_computation.3 | async-start | bytes 524288 | tf_op jit(solution)/shard_map/all_to_all | solution.py:595
  73.9 10.9 %collective-permute-start.8 = (f32[32,128]{1,0:T(8,128)S(1)}, f32[32,128]{1,0:T(8,128)S(1)}, u32[]{:S(2)}, u32[]{:S(2)}) collective-permute-start(f32[32,128]{1,0:T(8,128)S(1)} %get-tuple-element.61), channel_id=1, source_target_pairs={{0,1},{1,0},{2,3},{3,2},{4,5},{5,4},{6,7},{7,6},{8,9},{9,8},{10,11... | collective-permute-start | bytes 49160 | tf_op jit(solution)/shard_map/ppermute | solution.py:608
  74.0 10.9 %collective-permute-start.9 = (f32[32,128]{1,0:T(8,128)S(1)}, f32[32,128]{1,0:T(8,128)S(1)}, u32[]{:S(2)}, u32[]{:S(2)}) collective-permute-start(f32[32,128]{1,0:T(8,128)S(1)} %get-tuple-element.62), channel_id=1, source_target_pairs={{1,2},{2,1},{3,4},{4,3},{5,6},{6,5},{7,0},{0,7},{9,10},{10,9},{11,... | collective-permute-start | bytes 49160 | tf_op jit(solution)/shard_map/ppermute | solution.py:608
  76.2 8.6 %collective-permute-start.10 = (f32[32,128]{1,0:T(8,128)S(1)}, f32[32,128]{1,0:T(8,128)S(1)}, u32[]{:S(2)}, u32[]{:S(2)}) collective-permute-start(f32[32,128]{1,0:T(8,128)S(1)} %get-tuple-element.63), channel_id=1, source_target_pairs={{0,8},{8,0},{16,24},{24,16},{32,40},{40,32},{48,56},{56,48},{64,72... | collective-permute-start | bytes 49160 | tf_op jit(solution)/shard_map/ppermute | solution.py:608
  77.9 7.1 %collective-permute-start.11 = (f32[32,128]{1,0:T(8,128)S(1)}, f32[32,128]{1,0:T(8,128)S(1)}, u32[]{:S(2)}, u32[]{:S(2)}) collective-permute-start(f32[32,128]{1,0:T(8,128)S(1)} %get-tuple-element.64), channel_id=1, source_target_pairs={{8,16},{16,8},{24,32},{32,24},{40,48},{48,40},{56,64},{64,56},{72,... | collective-permute-start | bytes 49160 | tf_op jit(solution)/shard_map/ppermute | solution.py:608

commit v4 on v3

--- a/solution.py
+++ b/solution.py
@@ -598,14 +598,20 @@
 
 def pass_rims(rims):
     arrived = []
+    blks, subs = lax.axis_size("blk"), lax.axis_size("sub")
     for turn in range(4):
-        axis = ("sub", "blk")[turn // 2]
-        count = lax.axis_size(axis)
         pairs = []
-        for i in range(turn % 2, count, 2):
-            j = (i + 1) % count
-            pairs += [(i, j), (j, i)]
-        arrived.append(lax.ppermute(rims[turn], axis, pairs))
+        for blk in range(blks):
+            for sub in range(subs):
+                at, count = ((sub, subs), (blk, blks))[turn // 2]
+                other = at + 1 if at % 2 == turn % 2 else at - 1
+                there = [blk, sub]
+                if 0 <= other < count:
+                    there[1 - turn // 2] = other
+                else:
+                    there[turn // 2] ^= 1
+                pairs.append((blk * subs + sub, there[0] * subs + there[1]))
+        arrived.append(lax.ppermute(rims[turn], ("blk", "sub"), pairs))
     return arrived
 
 

time: 88.3 us -> 84.3 us (0.955)
  starting transfers between devices: 55.6 us -> 41.5 us
  waiting for transfers between devices: 6.47 us -> 16.1 us
    ppermute x12, starting transfers between devices: 25.9 us -> 7.85 us  [pass_rims(): arrived.append(lax.ppermute(rims[turn], ('blk', 'sub'), pairs))]
    all_to_all x4, waiting for transfers between devices: 6.17 us -> 14.7 us  [exchange(): lax.all_to_all(whole, ('blk', 'sub'), split_axis=0, concat_axis=0, tiled=...]
    all_to_all x4, starting transfers between devices: 29.7 us -> 33.6 us  [exchange(): lax.all_to_all(whole, ('blk', 'sub'), split_axis=0, concat_axis=0, tiled=...]
    ppermute x12, waiting for transfers between devices: 0.3 us -> 1.4 us  [pass_rims(): arrived.append(lax.ppermute(rims[turn], ('blk', 'sub'), pairs))]
  transfers between devices with their start and end apart: 16 -> 16, of which waited for: 4 -> 7; matrix products, arithmetic and copies ran while one was open for 0% -> 0% of each run, Pallas kernels for 17% -> 18%
where the time goes in v4:
time: 84.3 us; the launch traced here: 83.4 us
  starting transfers between devices  41.5 us (49%)
  Pallas kernels  22.9 us (27%)
  waiting for transfers between devices  16.1 us (19%)
  local copies, waits for them, and re-layouts  2.51 us (3%)
    all_to_all x4, starting transfers between devices, exchange(): lax.all_to_all(whole, ('blk', 'sub'), split_axis=0, concat_axis=0, tiled=...  33.6 us
    pallas_call x15, Pallas kernels, call(): pl.pallas_call(kernel, out_shape=[jax.ShapeDtypeStruct(o[0], o[1]) for o...  22.9 us
    all_to_all x4, waiting for transfers between devices, exchange(): lax.all_to_all(whole, ('blk', 'sub'), split_axis=0, concat_axis=0, tiled=...  14.7 us
    ppermute x12, starting transfers between devices, pass_rims(): arrived.append(lax.ppermute(rims[turn], ('blk', 'sub'), pairs))  7.85 us
    unnamed x16, local copies, waits for them, and re-layouts  2.51 us
  transfers between devices with their start and end apart: 16, of which 7 were waited for; matrix products, arithmetic and copies ran while one was open for 0% of the time, Pallas kernels for 18%

profile of v4, /device:TPU:0, one launch (start us, length us, event | category | flops | bytes accessed | tf_op | source)
XLA Modules:
  0.0 83.4 jit_solution(3987145172641398501)
XLA Ops:
  0.0 0.7 copy-done.7
  0.7 0.9 %shard_map.73 = f32[128,128]{1,0:T(8,128)} custom-call(s32[2,256]{1,0:T(2,128)S(1)} %copy-done.7), custom_call_target="tpu_custom_call" | custom-call | flops 100000000 | bytes 2000000 | tf_op jit(solution)/shard_map/pallas_call | solution.py:181
  1.5 11.1 %all-to-all-start = ((f32[128,1,128]{2,1,0:T(1,128)}), f32[128,1,128]{2,1,0:T(1,128)S(1)}, u32[]{:S(2)}, u32[]{:S(2)}) async-start(f32[128,1,128]{2,1,0:T(1,128)} %bitcast.1), calls=%async_computation | async-start | bytes 131072 | tf_op jit(solution)/shard_map/all_to_all | solution.py:595
  12.7 0.0 copy-start.6
  12.7 0.6 copy-done.6
  13.4 1.2 %copy-done = f32[4,216,256]{2,1,0:T(8,128)S(1)} copy-done((f32[4,216,256]{2,1,0:T(8,128)S(1)}, f32[4,216,256]{2,1,0:T(8,128)}, u32[]{:S(2)}) %copy-start) | copy-done | bytes 884760
  14.5 1.2 %shard_map.74 = (f32[24,256]{1,0:T(8,128)S(1)}, f32[104,256]{1,0:T(8,128)S(1)}, f32[48,128]{1,0:T(8,128)S(1)}, f32[16,256]{1,0:T(8,128)S(1)}, f32[128,256]{1,0:T(8,128)S(1)}) custom-call(s32[6,256]{1,0:T(8,128)S(1)} %copy-done.4, s32[3,512]{1,0:T(4,128)S(1)} %copy-done.5, f32[1,256]{1,0:T(1,128)S(1)} %bitcast.15, f32[4,216,256]{2,1,0:T(8,128)S(1)} %copy-done, ...), custom_call_target="tpu_custom_call" | custom-call | flops 100000000 | bytes 2000000 | tf_op jit(solution)/shard_map/pallas_call | solution.py:181
  15.8 6.2 %all-to-all-done = f32[128,1,128]{2,1,0:T(1,128)S(1)} async-done(((f32[128,1,128]{2,1,0:T(1,128)}), f32[128,1,128]{2,1,0:T(1,128)S(1)}, u32[]{:S(2)}, u32[]{:S(2)}) %all-to-all-start) | async-done | bytes 65568 | tf_op jit(solution)/shard_map/all_to_all | solution.py:595
  21.9 1.5 %shard_map.75 = (f32[8,256]{1,0:T(8,128)S(1)}, f32[512,128]{1,0:T(8,128)}) custom-call(f32[128,128]{1,0:T(8,128)S(1)} %bitcast.14, f32[16,256]{1,0:T(8,128)S(1)} %get-tuple-element.36.refs_1_, f32[128,256]{1,0:T(8,128)S(1)} %get-tuple-element.37.refs_2_), custom_call_target="tpu_custom_call" | custom-call | flops 100000000 | bytes 2000000 | tf_op jit(solution)/shard_map/pallas_call | solution.py:181
  23.5 0.0 copy-start.3
  23.5 4.8 %all-to-all-start.1 = ((f32[128,4,128]{2,1,0:T(4,128)}), f32[128,4,128]{2,1,0:T(4,128)S(1)}, u32[]{:S(2)}, u32[]{:S(2)}) async-start(f32[128,4,128]{2,1,0:T(4,128)} %bitcast.4), calls=%async_computation.1 | async-start | bytes 524288 | tf_op jit(solution)/shard_map/all_to_all | solution.py:595
  28.3 0.8 shard_map.77
  29.1 0.1 collective-permute-start
  29.2 1.2 %collective-permute-start.1 = (f32[32,128]{1,0:T(8,128)S(1)}, f32[32,128]{1,0:T(8,128)S(1)}, u32[]{:S(2)}, u32[]{:S(2)}) collective-permute-start(f32[32,128]{1,0:T(8,128)S(1)} %get-tuple-element.42), channel_id=1, source_target_pairs={{0,8},{1,2},{2,1},{3,4},{4,3},{5,6},{6,5},{7,15},{8,0},{9,10},{10,... | collective-permute-start | bytes 49160 | tf_op jit(solution)/shard_map/ppermute | solution.py:614
  30.4 0.9 %collective-permute-start.2 = (f32[32,128]{1,0:T(8,128)S(1)}, f32[32,128]{1,0:T(8,128)S(1)}, u32[]{:S(2)}, u32[]{:S(2)}) collective-permute-start(f32[32,128]{1,0:T(8,128)S(1)} %get-tuple-element.43), channel_id=1, source_target_pairs={{0,8},{1,9},{2,10},{3,11},{4,12},{5,13},{6,14},{7,15},{8,0},{9,1},... | collective-permute-start | bytes 49160 | tf_op jit(solution)/shard_map/ppermute | solution.py:614
  31.3 0.4 collective-permute-start.3
  31.7 2.3 %shard_map.76.refs_0_ = f32[4,216,256]{2,1,0:T(8,128)S(1)} custom-call(f32[4,216,256]{2,1,0:T(8,128)S(1)} %copy-done.1, bf16[240,216]{1,0:T(8,128)(2,1)S(1)} %copy-done.2, bf16[6,216,216]{2,1,0:T(8,128)(2,1)S(1)} %copy-done.3, s32[6,256]{1,0:T(8,128)S(1)} %copy-done.4, f32[24,256]{1,0:T(8,128)S(1)} %get-tuple-element.39.refs_4_.refs_1_.refs_6_.refs_5_.refs_3_, ...), custom_call_target="tpu_custom_call" | custom-call | flops 800000000 | bytes 2000000 | tf_op jit(solution)/shard_map/pallas_call | solution.py:181
  34.0 0.0 collective-permute-done.refs_1_
  34.0 0.0 collective-permute-done.1.refs_2_
  34.0 0.3 collective-permute-done.2.refs_3_
  34.3 0.0 collective-permute-done.3.refs_4_
  34.3 1.6 %shard_map.78 = (f32[4,216,256]{2,1,0:T(8,128)S(1)}, f32[240,256]{1,0:T(8,128)S(1)}) custom-call(f32[4,216,256]{2,1,0:T(8,128)S(1)} %shard_map.76.refs_0_, f32[32,128]{1,0:T(8,128)S(1)} %collective-permute-done.refs_1_, f32[32,128]{1,0:T(8,128)S(1)} %collective-permute-done.1.refs_2_, f32[32,128]{1,0:T(8,128)S(1)} %collective-permute-done.2.refs_3_, ...), custom_call_target="tpu_custom_call" | custom-call | flops 100000000 | bytes 2000000 | tf_op jit(solution)/shard_map/pallas_call | solution.py:181
  35.9 3.1 %all-to-all-done.1 = f32[128,4,128]{2,1,0:T(4,128)S(1)} async-done(((f32[128,4,128]{2,1,0:T(4,128)}), f32[128,4,128]{2,1,0:T(4,128)S(1)}, u32[]{:S(2)}, u32[]{:S(2)}) %all-to-all-start.1) | async-done | bytes 262176 | tf_op jit(solution)/shard_map/all_to_all | solution.py:595
  39.0 1.6 %shard_map.79 = (f32[128,128]{1,0:T(8,128)S(1)}, f32[512,128]{1,0:T(8,128)}) custom-call(f32[512,128]{1,0:T(8,128)S(1)} %bitcast.13, f32[240,256]{1,0:T(8,128)S(1)} %get-tuple-element.47.refs_1_), custom_call_target="tpu_custom_call" | custom-call | flops 100000000 | bytes 2000000 | tf_op jit(solution)/shard_map/pallas_call | solution.py:181
  40.6 8.6 %all-to-all-start.2 = ((f32[128,4,128]{2,1,0:T(4,128)}), f32[128,4,128]{2,1,0:T(4,128)S(1)}, u32[]{:S(2)}, u32[]{:S(2)}) async-start(f32[128,4,128]{2,1,0:T(4,128)} %bitcast.6), calls=%async_computation.2 | async-start | bytes 524288 | tf_op jit(solution)/shard_map/all_to_all | solution.py:595
  49.2 1.3 %shard_map.80 = (f32[4,216,256]{2,1,0:T(8,128)S(1)}, f32[32,128]{1,0:T(8,128)S(1)}, f32[32,128]{1,0:T(8,128)S(1)}, f32[32,128]{1,0:T(8,128)S(1)}, f32[32,128]{1,0:T(8,128)S(1)}) custom-call(f32[4,216,256]{2,1,0:T(8,128)S(1)} %get-tuple-element.49.refs_0_, f32[24,256]{1,0:T(8,128)S(1)} %get-tuple-element.39.refs_4_.refs_1_.refs_6_.refs_5_.refs_3_, ...), custom_call_target="tpu_custom_call" | custom-call | flops 50000000 | bytes 2000000 | tf_op jit(solution)/shard_map/pallas_call | solution.py:181
  50.5 0.1 collective-permute-start.4
  50.6 1.2 %collective-permute-start.5 = (f32[32,128]{1,0:T(8,128)S(1)}, f32[32,128]{1,0:T(8,128)S(1)}, u32[]{:S(2)}, u32[]{:S(2)}) collective-permute-start(f32[32,128]{1,0:T(8,128)S(1)} %get-tuple-element.53), channel_id=1, source_target_pairs={{0,8},{1,2},{2,1},{3,4},{4,3},{5,6},{6,5},{7,15},{8,0},{9,10},{10,... | collective-permute-start | bytes 49160 | tf_op jit(solution)/shard_map/ppermute | solution.py:614
  51.8 0.9 %collective-permute-start.6 = (f32[32,128]{1,0:T(8,128)S(1)}, f32[32,128]{1,0:T(8,128)S(1)}, u32[]{:S(2)}, u32[]{:S(2)}) collective-permute-start(f32[32,128]{1,0:T(8,128)S(1)} %get-tuple-element.54), channel_id=1, source_target_pairs={{0,8},{1,9},{2,10},{3,11},{4,12},{5,13},{6,14},{7,15},{8,0},{9,1},... | collective-permute-start | bytes 49160 | tf_op jit(solution)/shard_map/ppermute | solution.py:614
  52.7 0.4 collective-permute-start.7
  53.1 2.3 %shard_map.81.refs_0_ = f32[4,216,256]{2,1,0:T(8,128)S(1)} custom-call(f32[4,216,256]{2,1,0:T(8,128)S(1)} %get-tuple-element.51.refs_0_, f32[4,216,256]{2,1,0:T(8,128)S(1)} %copy-done.1, bf16[240,216]{1,0:T(8,128)(2,1)S(1)} %copy-done.2, bf16[6,216,216]{2,1,0:T(8,128)(2,1)S(1)} %copy-done.3, s32[6,256]{1,0:T(8,128)S(1)} %copy-done.4, ...), custom_call_target="tpu_custom_call" | custom-call | flops 800000000 | bytes 2000000 | tf_op jit(solution)/shard_map/pallas_call | solution.py:181
  55.4 0.0 collective-permute-done.4.refs_1_
  55.4 0.0 collective-permute-done.5.refs_2_
  55.4 0.5 collective-permute-done.6.refs_3_
  56.0 1.6 %shard_map.82 = (f32[4,216,256]{2,1,0:T(8,128)S(1)}, f32[240,256]{1,0:T(8,128)S(1)}) custom-call(f32[4,216,256]{2,1,0:T(8,128)S(1)} %shard_map.81.refs_0_, f32[32,128]{1,0:T(8,128)S(1)} %collective-permute-done.4.refs_1_, f32[32,128]{1,0:T(8,128)S(1)} %collective-permute-done.5.refs_2_, f32[32,128]{1,0:T(8,128)S(1)} %collective-permute-done.6.refs_3_, ...), custom_call_target="tpu_custom_call" | custom-call | flops 100000000 | bytes 2000000 | tf_op jit(solution)/shard_map/pallas_call | solution.py:181
  57.5 2.4 %all-to-all-done.2 = f32[128,4,128]{2,1,0:T(4,128)S(1)} async-done(((f32[128,4,128]{2,1,0:T(4,128)}), f32[128,4,128]{2,1,0:T(4,128)S(1)}, u32[]{:S(2)}, u32[]{:S(2)}) %all-to-all-start.2) | async-done | bytes 262176 | tf_op jit(solution)/shard_map/all_to_all | solution.py:595
  59.9 1.6 %shard_map.83 = (f32[128,128]{1,0:T(8,128)S(1)}, f32[512,128]{1,0:T(8,128)}) custom-call(f32[512,128]{1,0:T(8,128)S(1)} %bitcast.12, f32[240,256]{1,0:T(8,128)S(1)} %get-tuple-element.56.refs_1_), custom_call_target="tpu_custom_call" | custom-call | flops 100000000 | bytes 2000000 | tf_op jit(solution)/shard_map/pallas_call | solution.py:181
  61.5 9.1 %all-to-all-start.3 = ((f32[128,4,128]{2,1,0:T(4,128)}), f32[128,4,128]{2,1,0:T(4,128)S(1)}, u32[]{:S(2)}, u32[]{:S(2)}) async-start(f32[128,4,128]{2,1,0:T(4,128)} %bitcast.8), calls=%async_computation.3 | async-start | bytes 524288 | tf_op jit(solution)/shard_map/all_to_all | solution.py:595
  70.6 1.3 %shard_map.84 = (f32[4,216,256]{2,1,0:T(8,128)S(1)}, f32[32,128]{1,0:T(8,128)S(1)}, f32[32,128]{1,0:T(8,128)S(1)}, f32[32,128]{1,0:T(8,128)S(1)}, f32[32,128]{1,0:T(8,128)S(1)}) custom-call(f32[4,216,256]{2,1,0:T(8,128)S(1)} %get-tuple-element.58.refs_0_, f32[24,256]{1,0:T(8,128)S(1)} %get-tuple-element.39.refs_4_.refs_1_.refs_6_.refs_5_.refs_3_, ...), custom_call_target="tpu_custom_call" | custom-call | flops 50000000 | bytes 2000000 | tf_op jit(solution)/shard_map/pallas_call | solution.py:181
  71.9 0.1 collective-permute-start.8
  72.0 1.2 %collective-permute-start.9 = (f32[32,128]{1,0:T(8,128)S(1)}, f32[32,128]{1,0:T(8,128)S(1)}, u32[]{:S(2)}, u32[]{:S(2)}) collective-permute-start(f32[32,128]{1,0:T(8,128)S(1)} %get-tuple-element.62), channel_id=1, source_target_pairs={{0,8},{1,2},{2,1},{3,4},{4,3},{5,6},{6,5},{7,15},{8,0},{9,10},{10,... | collective-permute-start | bytes 49160 | tf_op jit(solution)/shard_map/ppermute | solution.py:614
  73.2 0.9 %collective-permute-start.10 = (f32[32,128]{1,0:T(8,128)S(1)}, f32[32,128]{1,0:T(8,128)S(1)}, u32[]{:S(2)}, u32[]{:S(2)}) collective-permute-start(f32[32,128]{1,0:T(8,128)S(1)} %get-tuple-element.63), channel_id=1, source_target_pairs={{0,8},{1,9},{2,10},{3,11},{4,12},{5,13},{6,14},{7,15},{8,0},{9,1},... | collective-permute-start | bytes 49160 | tf_op jit(solution)/shard_map/ppermute | solution.py:614
  74.1 0.4 collective-permute-start.11
  74.5 2.3 %shard_map.85.refs_0_ = f32[4,216,256]{2,1,0:T(8,128)S(1)} custom-call(f32[4,216,256]{2,1,0:T(8,128)S(1)} %get-tuple-element.60.refs_0_, f32[4,216,256]{2,1,0:T(8,128)S(1)} %copy-done.1, bf16[240,216]{1,0:T(8,128)(2,1)S(1)} %copy-done.2, bf16[6,216,216]{2,1,0:T(8,128)(2,1)S(1)} %copy-done.3, s32[6,256]{1,0:T(8,128)S(1)} %copy-done.4, ...), custom_call_target="tpu_custom_call" | custom-call | flops 800000000 | bytes 2000000 | tf_op jit(solution)/shard_map/pallas_call | solution.py:181
  76.8 0.5 collective-permute-done.10.refs_3_
  77.4 0.9 %shard_map.86 = (f32[4,216,256]{2,1,0:T(8,128)S(1)}, f32[240,256]{1,0:T(8,128)S(1)}) custom-call(f32[4,216,256]{2,1,0:T(8,128)S(1)} %shard_map.85.refs_0_, f32[32,128]{1,0:T(8,128)S(1)} %collective-permute-done.8.refs_1_, f32[32,128]{1,0:T(8,128)S(1)} %collective-permute-done.9.refs_2_, f32[32,128]{1,0:T(8,128)S(1)} %collective-permute-done.10.refs_3_, ...), custom_call_target="tpu_custom_call" | custom-call | flops 100000000 | bytes 2000000 | tf_op jit(solution)/shard_map/pallas_call | solution.py:181
  78.3 3.0 %all-to-all-done.3 = f32[128,4,128]{2,1,0:T(4,128)S(1)} async-done(((f32[128,4,128]{2,1,0:T(4,128)}), f32[128,4,128]{2,1,0:T(4,128)S(1)}, u32[]{:S(2)}, u32[]{:S(2)}) %all-to-all-start.3) | async-done | bytes 262176 | tf_op jit(solution)/shard_map/all_to_all | solution.py:595
  81.3 2.0 %shard_map.87 = f32[4,216,256]{2,1,0:T(8,128)} custom-call(f32[512,128]{1,0:T(8,128)S(1)} %bitcast.11, f32[240,256]{1,0:T(8,128)S(1)} %get-tuple-element.65.refs_1_, f32[4,216,256]{2,1,0:T(8,128)S(1)} %get-tuple-element.66.refs_2_, f32[24,256]{1,0:T(8,128)S(1)} %get-tuple-element.39.refs_4_.refs_1_.refs_6_.refs_5_.refs_3_, bf16[240,216]{1,0:T(8,128)(2,1)S(1)} %copy-done.2), custom_call_target="tpu_custom_call" | custom-call | flops 100000000 | bytes 2000000 | tf_op jit(solution)/shard_map/pallas_call | solution.py:181
  (15 shorter events, 0.0 us)
Async XLA Ops:
  0.0 0.7 copy-start.7
  0.7 12.0 %copy-start.5 = (s32[3,512]{1,0:T(4,128)S(1)}, s32[3,512]{1,0:T(4,128)}, u32[]{:S(2)}) copy-start(s32[3,512]{1,0:T(4,128)} %refs_1_.4) | copy-start | bytes 18436
  1.5 11.2 %copy-start.2 = (bf16[240,216]{1,0:T(8,128)(2,1)S(1)}, bf16[240,216]{1,0:T(8,128)(2,1)}, u32[]{:S(2)}) copy-start(bf16[240,216]{1,0:T(8,128)(2,1)} %constant.4.clone.refs_4_.refs_1_.refs_2_.refs_5_) | copy-start | bytes 311044
  1.5 11.2 %copy-start.4 = (s32[6,256]{1,0:T(8,128)S(1)}, s32[6,256]{1,0:T(8,128)}, u32[]{:S(2)}) copy-start(s32[6,256]{1,0:T(8,128)} %refs_4_.5) | copy-start | bytes 18436
  1.5 20.4 %all-to-all-start = ((f32[128,1,128]{2,1,0:T(1,128)}), f32[128,1,128]{2,1,0:T(1,128)S(1)}, u32[]{:S(2)}, u32[]{:S(2)}) async-start(f32[128,1,128]{2,1,0:T(1,128)} %bitcast.1), calls=%async_computation | async-start | bytes 131072 | tf_op jit(solution)/shard_map/all_to_all | solution.py:595
  12.7 0.7 copy-start.6
  13.4 1.2 %copy-start = (f32[4,216,256]{2,1,0:T(8,128)S(1)}, f32[4,216,256]{2,1,0:T(8,128)}, u32[]{:S(2)}) copy-start(f32[4,216,256]{2,1,0:T(8,128)} %refs_1_.6) | copy-start | bytes 2654212
  14.5 13.7 %copy-start.1 = (f32[4,216,256]{2,1,0:T(8,128)S(1)}, f32[4,216,256]{2,1,0:T(8,128)}, u32[]{:S(2)}) copy-start(f32[4,216,256]{2,1,0:T(8,128)} %refs_1_.6) | copy-start | bytes 2654212
  23.5 8.3 %copy-start.3 = (bf16[6,216,216]{2,1,0:T(8,128)(2,1)S(1)}, bf16[6,216,216]{2,1,0:T(8,128)(2,1)}, u32[]{:S(2)}) copy-start(bf16[6,216,216]{2,1,0:T(8,128)(2,1)} %constant.5.clone.refs_2_.refs_3_) | copy-start | bytes 1679620
  23.5 15.5 %all-to-all-start.1 = ((f32[128,4,128]{2,1,0:T(4,128)}), f32[128,4,128]{2,1,0:T(4,128)S(1)}, u32[]{:S(2)}, u32[]{:S(2)}) async-start(f32[128,4,128]{2,1,0:T(4,128)} %bitcast.4), calls=%async_computation.1 | async-start | bytes 524288 | tf_op jit(solution)/shard_map/all_to_all | solution.py:595
  29.1 4.9 %collective-permute-start = (f32[32,128]{1,0:T(8,128)S(1)}, f32[32,128]{1,0:T(8,128)S(1)}, u32[]{:S(2)}, u32[]{:S(2)}) collective-permute-start(f32[32,128]{1,0:T(8,128)S(1)} %get-tuple-element.41), channel_id=1, source_target_pairs={{0,1},{1,0},{2,3},{3,2},{4,5},{5,4},{6,7},{7,6},{8,9},{9,8},{10,11... | collective-permute-start | bytes 49160 | tf_op jit(solution)/shard_map/ppermute | solution.py:614
  29.2 4.9 %collective-permute-start.1 = (f32[32,128]{1,0:T(8,128)S(1)}, f32[32,128]{1,0:T(8,128)S(1)}, u32[]{:S(2)}, u32[]{:S(2)}) collective-permute-start(f32[32,128]{1,0:T(8,128)S(1)} %get-tuple-element.42), channel_id=1, source_target_pairs={{0,8},{1,2},{2,1},{3,4},{4,3},{5,6},{6,5},{7,15},{8,0},{9,10},{10,... | collective-permute-start | bytes 49160 | tf_op jit(solution)/shard_map/ppermute | solution.py:614
  30.4 3.9 %collective-permute-start.2 = (f32[32,128]{1,0:T(8,128)S(1)}, f32[32,128]{1,0:T(8,128)S(1)}, u32[]{:S(2)}, u32[]{:S(2)}) collective-permute-start(f32[32,128]{1,0:T(8,128)S(1)} %get-tuple-element.43), channel_id=1, source_target_pairs={{0,8},{1,9},{2,10},{3,11},{4,12},{5,13},{6,14},{7,15},{8,0},{9,1},... | collective-permute-start | bytes 49160 | tf_op jit(solution)/shard_map/ppermute | solution.py:614
  31.3 3.1 %collective-permute-start.3 = (f32[32,128]{1,0:T(8,128)S(1)}, f32[32,128]{1,0:T(8,128)S(1)}, u32[]{:S(2)}, u32[]{:S(2)}) collective-permute-start(f32[32,128]{1,0:T(8,128)S(1)} %get-tuple-element.44), channel_id=1, source_target_pairs={{0,1},{1,0},{2,3},{3,2},{4,5},{5,4},{6,7},{7,6},{8,16},{9,17},{10,... | collective-permute-start | bytes 49160 | tf_op jit(solution)/shard_map/ppermute | solution.py:614
  40.6 19.3 %all-to-all-start.2 = ((f32[128,4,128]{2,1,0:T(4,128)}), f32[128,4,128]{2,1,0:T(4,128)S(1)}, u32[]{:S(2)}, u32[]{:S(2)}) async-start(f32[128,4,128]{2,1,0:T(4,128)} %bitcast.6), calls=%async_computation.2 | async-start | bytes 524288 | tf_op jit(solution)/shard_map/all_to_all | solution.py:595
  50.5 4.9 %collective-permute-start.4 = (f32[32,128]{1,0:T(8,128)S(1)}, f32[32,128]{1,0:T(8,128)S(1)}, u32[]{:S(2)}, u32[]{:S(2)}) collective-permute-start(f32[32,128]{1,0:T(8,128)S(1)} %get-tuple-element.52), channel_id=1, source_target_pairs={{0,1},{1,0},{2,3},{3,2},{4,5},{5,4},{6,7},{7,6},{8,9},{9,8},{10,11... | collective-permute-start | bytes 49160 | tf_op jit(solution)/shard_map/ppermute | solution.py:614
  50.6 4.8 %collective-permute-start.5 = (f32[32,128]{1,0:T(8,128)S(1)}, f32[32,128]{1,0:T(8,128)S(1)}, u32[]{:S(2)}, u32[]{:S(2)}) collective-permute-start(f32[32,128]{1,0:T(8,128)S(1)} %get-tuple-element.53), channel_id=1, source_target_pairs={{0,8},{1,2},{2,1},{3,4},{4,3},{5,6},{6,5},{7,15},{8,0},{9,10},{10,... | collective-permute-start | bytes 49160 | tf_op jit(solution)/shard_map/ppermute | solution.py:614
  51.8 4.2 %collective-permute-start.6 = (f32[32,128]{1,0:T(8,128)S(1)}, f32[32,128]{1,0:T(8,128)S(1)}, u32[]{:S(2)}, u32[]{:S(2)}) collective-permute-start(f32[32,128]{1,0:T(8,128)S(1)} %get-tuple-element.54), channel_id=1, source_target_pairs={{0,8},{1,9},{2,10},{3,11},{4,12},{5,13},{6,14},{7,15},{8,0},{9,1},... | collective-permute-start | bytes 49160 | tf_op jit(solution)/shard_map/ppermute | solution.py:614
  52.7 3.3 %collective-permute-start.7 = (f32[32,128]{1,0:T(8,128)S(1)}, f32[32,128]{1,0:T(8,128)S(1)}, u32[]{:S(2)}, u32[]{:S(2)}) collective-permute-start(f32[32,128]{1,0:T(8,128)S(1)} %get-tuple-element.55), channel_id=1, source_target_pairs={{0,1},{1,0},{2,3},{3,2},{4,5},{5,4},{6,7},{7,6},{8,16},{9,17},{10,... | collective-permute-start | bytes 49160 | tf_op jit(solution)/shard_map/ppermute | solution.py:614
  61.5 19.8 %all-to-all-start.3 = ((f32[128,4,128]{2,1,0:T(4,128)}), f32[128,4,128]{2,1,0:T(4,128)S(1)}, u32[]{:S(2)}, u32[]{:S(2)}) async-start(f32[128,4,128]{2,1,0:T(4,128)} %bitcast.8), calls=%async_computation.3 | async-start | bytes 524288 | tf_op jit(solution)/shard_map/all_to_all | solution.py:595
  71.9 4.9 %collective-permute-start.8 = (f32[32,128]{1,0:T(8,128)S(1)}, f32[32,128]{1,0:T(8,128)S(1)}, u32[]{:S(2)}, u32[]{:S(2)}) collective-permute-start(f32[32,128]{1,0:T(8,128)S(1)} %get-tuple-element.61), channel_id=1, source_target_pairs={{0,1},{1,0},{2,3},{3,2},{4,5},{5,4},{6,7},{7,6},{8,9},{9,8},{10,11... | collective-permute-start | bytes 49160 | tf_op jit(solution)/shard_map/ppermute | solution.py:614
  72.0 4.8 %collective-permute-start.9 = (f32[32,128]{1,0:T(8,128)S(1)}, f32[32,128]{1,0:T(8,128)S(1)}, u32[]{:S(2)}, u32[]{:S(2)}) collective-permute-start(f32[32,128]{1,0:T(8,128)S(1)} %get-tuple-element.62), channel_id=1, source_target_pairs={{0,8},{1,2},{2,1},{3,4},{4,3},{5,6},{6,5},{7,15},{8,0},{9,10},{10,... | collective-permute-start | bytes 49160 | tf_op jit(solution)/shard_map/ppermute | solution.py:614
  73.2 4.1 %collective-permute-start.10 = (f32[32,128]{1,0:T(8,128)S(1)}, f32[32,128]{1,0:T(8,128)S(1)}, u32[]{:S(2)}, u32[]{:S(2)}) collective-permute-start(f32[32,128]{1,0:T(8,128)S(1)} %get-tuple-element.63), channel_id=1, source_target_pairs={{0,8},{1,9},{2,10},{3,11},{4,12},{5,13},{6,14},{7,15},{8,0},{9,1},... | collective-permute-start | bytes 49160 | tf_op jit(solution)/shard_map/ppermute | solution.py:614
  74.1 3.3 %collective-permute-start.11 = (f32[32,128]{1,0:T(8,128)S(1)}, f32[32,128]{1,0:T(8,128)S(1)}, u32[]{:S(2)}, u32[]{:S(2)}) collective-permute-start(f32[32,128]{1,0:T(8,128)S(1)} %get-tuple-element.64), channel_id=1, source_target_pairs={{0,1},{1,0},{2,3},{3,2},{4,5},{5,4},{6,7},{7,6},{8,16},{9,17},{10,... | collective-permute-start | bytes 49160 | tf_op jit(solution)/shard_map/ppermute | solution.py:614

commit v5 on v4

--- a/solution.py
+++ b/solution.py
@@ -628,14 +628,14 @@
     metric = metric.reshape(1, ELEMS)
     whole = ((4, NODES, ELEMS), F32, "v")
     rim = ((RIM, FEAT), F32, "v")
-    table = ((FACT_ROWS, 2 * FACES), F32, "h")
+    table = ((FACT_ROWS, 2 * FACES), F32, "v")
     pad = pltpu.VMEM((3 * P_SIZE, 8, FACES), F32)
     wide = pltpu.VMEM((3 * P_SIZE, 8, 2 * FACES), F32)
     narrow = pltpu.VMEM((FEAT, FACES), F32)
     broad = pltpu.VMEM((FEAT, 2 * FACES), F32)
 
     def far(*arrays):
-        return tuple((array, "h") for array in arrays)
+        return tuple((array, "v") for array in arrays)
 
     def near(*arrays):
         return tuple((array, "v") for array in arrays)
@@ -645,9 +645,9 @@
     keys, facts, own, info, mortars = call(
         tables_body,
         [
-            ((KEY_ROWS, ELEMS), F32, "h"),
+            ((KEY_ROWS, ELEMS), F32, "v"),
             table,
-            ((48, FACES), F32, "h"),
+            ((48, FACES), F32, "v"),
             ((16, 2 * FACES), F32, "v"),
             ((FEAT, 2 * FACES), F32, "v"),
         ],
@@ -656,7 +656,7 @@
     )
     routes, payload = call(
         route_body,
-        [((8, 2 * FACES), F32, "h"), ((SLOTS, FEAT), F32, "v")],
+        [((8, 2 * FACES), F32, "v"), ((SLOTS, FEAT), F32, "v")],
         near(owned, info, mortars),
     )
     part, arrived = fields, None
@@ -689,7 +689,7 @@
         if section < 2:
             arrived, payload = call(
                 bind(flux_body, section),
-                [((FEAT, FACES), F32, "h"), ((SLOTS, FEAT), F32, "v")],
+                [((FEAT, FACES), F32, "v"), ((SLOTS, FEAT), F32, "v")],
                 near(arrivals, held),
                 scratch=[pad, wide, broad],
             )

time: 84.3 us -> 82.9 us (0.983)
  Pallas kernels: 22.9 us -> 20.5 us
  waiting for transfers between devices: 16.1 us -> 18.5 us
  starting transfers between devices: 41.5 us -> 40.3 us
    pallas_call x15, Pallas kernels: 22.9 us -> 20.5 us  [call(): pl.pallas_call(kernel, out_shape=[jax.ShapeDtypeStruct(o[0], o[1]) for o...]
    all_to_all x4, waiting for transfers between devices: 14.7 us -> 16.6 us  [exchange(): lax.all_to_all(whole, ('blk', 'sub'), split_axis=0, concat_axis=0, tiled=...]
    all_to_all x4, starting transfers between devices: 33.6 us -> 32.6 us  [exchange(): lax.all_to_all(whole, ('blk', 'sub'), split_axis=0, concat_axis=0, tiled=...]
  transfers between devices with their start and end apart: 16 -> 16, of which waited for: 7 -> 7; matrix products, arithmetic and copies ran while one was open for 0% -> 0% of each run, Pallas kernels for 18% -> 16%
where the time goes in v5:
time: 82.9 us; the launch traced here: 82 us
  starting transfers between devices  40.3 us (49%)
  Pallas kernels  20.5 us (25%)
  waiting for transfers between devices  18.5 us (22%)
  local copies, waits for them, and re-layouts  2.51 us (3%)
    all_to_all x4, starting transfers between devices, exchange(): lax.all_to_all(whole, ('blk', 'sub'), split_axis=0, concat_axis=0, tiled=...  32.6 us
    pallas_call x15, Pallas kernels, call(): pl.pallas_call(kernel, out_shape=[jax.ShapeDtypeStruct(o[0], o[1]) for o...  20.5 us
    all_to_all x4, waiting for transfers between devices, exchange(): lax.all_to_all(whole, ('blk', 'sub'), split_axis=0, concat_axis=0, tiled=...  16.6 us
    ppermute x12, starting transfers between devices, pass_rims(): arrived.append(lax.ppermute(rims[turn], ('blk', 'sub'), pairs))  7.78 us
    unnamed x16, local copies, waits for them, and re-layouts  2.51 us
    ppermute x12, waiting for transfers between devices, pass_rims(): arrived.append(lax.ppermute(rims[turn], ('blk', 'sub'), pairs))  1.89 us
  transfers between devices with their start and end apart: 16, of which 7 were waited for; matrix products, arithmetic and copies ran while one was open for 0% of the time, Pallas kernels for 16%

profile of v5, /device:TPU:0, one launch (start us, length us, event | category | flops | bytes accessed | tf_op | source)
XLA Modules:
  0.0 82.0 jit_solution(11544867730019124930)
XLA Ops:
  0.0 0.7 copy-done.7
  0.7 0.9 %shard_map.73 = f32[128,128]{1,0:T(8,128)} custom-call(s32[2,256]{1,0:T(2,128)S(1)} %copy-done.7), custom_call_target="tpu_custom_call" | custom-call | flops 100000000 | bytes 2000000 | tf_op jit(solution)/shard_map/pallas_call | solution.py:181
  1.5 11.1 %all-to-all-start = ((f32[128,1,128]{2,1,0:T(1,128)}), f32[128,1,128]{2,1,0:T(1,128)S(1)}, u32[]{:S(2)}, u32[]{:S(2)}) async-start(f32[128,1,128]{2,1,0:T(1,128)} %bitcast.1), calls=%async_computation | async-start | bytes 131072 | tf_op jit(solution)/shard_map/all_to_all | solution.py:595
  12.7 0.0 copy-start.6
  12.7 0.6 copy-done.6
  13.4 1.2 %copy-done = f32[4,216,256]{2,1,0:T(8,128)S(1)} copy-done((f32[4,216,256]{2,1,0:T(8,128)S(1)}, f32[4,216,256]{2,1,0:T(8,128)}, u32[]{:S(2)}) %copy-start) | copy-done | bytes 884760
  14.5 1.0 %shard_map.74 = (f32[24,256]{1,0:T(8,128)S(1)}, f32[104,256]{1,0:T(8,128)S(1)}, f32[48,128]{1,0:T(8,128)S(1)}, f32[16,256]{1,0:T(8,128)S(1)}, f32[128,256]{1,0:T(8,128)S(1)}) custom-call(s32[6,256]{1,0:T(8,128)S(1)} %copy-done.4, s32[3,512]{1,0:T(4,128)S(1)} %copy-done.5, f32[1,256]{1,0:T(1,128)S(1)} %bitcast.15, f32[4,216,256]{2,1,0:T(8,128)S(1)} %copy-done, ...), custom_call_target="tpu_custom_call" | custom-call | flops 100000000 | bytes 2000000 | tf_op jit(solution)/shard_map/pallas_call | solution.py:181
  15.5 6.4 %all-to-all-done = f32[128,1,128]{2,1,0:T(1,128)S(1)} async-done(((f32[128,1,128]{2,1,0:T(1,128)}), f32[128,1,128]{2,1,0:T(1,128)S(1)}, u32[]{:S(2)}, u32[]{:S(2)}) %all-to-all-start) | async-done | bytes 65568 | tf_op jit(solution)/shard_map/all_to_all | solution.py:595
  21.9 1.5 %shard_map.75 = (f32[8,256]{1,0:T(8,128)S(1)}, f32[512,128]{1,0:T(8,128)}) custom-call(f32[128,128]{1,0:T(8,128)S(1)} %bitcast.14, f32[16,256]{1,0:T(8,128)S(1)} %get-tuple-element.36.refs_1_, f32[128,256]{1,0:T(8,128)S(1)} %get-tuple-element.37.refs_2_), custom_call_target="tpu_custom_call" | custom-call | flops 100000000 | bytes 2000000 | tf_op jit(solution)/shard_map/pallas_call | solution.py:181
  23.4 4.8 %all-to-all-start.1 = ((f32[128,4,128]{2,1,0:T(4,128)}), f32[128,4,128]{2,1,0:T(4,128)S(1)}, u32[]{:S(2)}, u32[]{:S(2)}) async-start(f32[128,4,128]{2,1,0:T(4,128)} %bitcast.4), calls=%async_computation.1 | async-start | bytes 524288 | tf_op jit(solution)/shard_map/all_to_all | solution.py:595
  28.3 0.6 shard_map.77
  28.9 0.1 collective-permute-start
  29.0 1.2 %collective-permute-start.1 = (f32[32,128]{1,0:T(8,128)S(1)}, f32[32,128]{1,0:T(8,128)S(1)}, u32[]{:S(2)}, u32[]{:S(2)}) collective-permute-start(f32[32,128]{1,0:T(8,128)S(1)} %get-tuple-element.42), channel_id=1, source_target_pairs={{0,8},{1,2},{2,1},{3,4},{4,3},{5,6},{6,5},{7,15},{8,0},{9,10},{10,... | collective-permute-start | bytes 49160 | tf_op jit(solution)/shard_map/ppermute | solution.py:614
  30.2 0.9 %collective-permute-start.2 = (f32[32,128]{1,0:T(8,128)S(1)}, f32[32,128]{1,0:T(8,128)S(1)}, u32[]{:S(2)}, u32[]{:S(2)}) collective-permute-start(f32[32,128]{1,0:T(8,128)S(1)} %get-tuple-element.43), channel_id=1, source_target_pairs={{0,8},{1,9},{2,10},{3,11},{4,12},{5,13},{6,14},{7,15},{8,0},{9,1},... | collective-permute-start | bytes 49160 | tf_op jit(solution)/shard_map/ppermute | solution.py:614
  31.1 0.4 collective-permute-start.3
  31.5 2.0 %shard_map.76.refs_0_ = f32[4,216,256]{2,1,0:T(8,128)S(1)} custom-call(f32[4,216,256]{2,1,0:T(8,128)S(1)} %copy-done.1, bf16[240,216]{1,0:T(8,128)(2,1)S(1)} %copy-done.2, bf16[6,216,216]{2,1,0:T(8,128)(2,1)S(1)} %copy-done.3, s32[6,256]{1,0:T(8,128)S(1)} %copy-done.4, f32[24,256]{1,0:T(8,128)S(1)} %get-tuple-element.39.refs_4_.refs_1_.refs_6_.refs_5_.refs_3_, ...), custom_call_target="tpu_custom_call" | custom-call | flops 800000000 | bytes 2000000 | tf_op jit(solution)/shard_map/pallas_call | solution.py:181
  33.5 0.0 collective-permute-done.refs_1_
  33.6 0.5 collective-permute-done.2.refs_3_
  34.1 0.0 collective-permute-done.3.refs_4_
  34.1 1.2 %shard_map.78 = (f32[4,216,256]{2,1,0:T(8,128)S(1)}, f32[240,256]{1,0:T(8,128)S(1)}) custom-call(f32[4,216,256]{2,1,0:T(8,128)S(1)} %shard_map.76.refs_0_, f32[32,128]{1,0:T(8,128)S(1)} %collective-permute-done.refs_1_, f32[32,128]{1,0:T(8,128)S(1)} %collective-permute-done.1.refs_2_, f32[32,128]{1,0:T(8,128)S(1)} %collective-permute-done.2.refs_3_, ...), custom_call_target="tpu_custom_call" | custom-call | flops 100000000 | bytes 2000000 | tf_op jit(solution)/shard_map/pallas_call | solution.py:181
  35.3 3.7 %all-to-all-done.1 = f32[128,4,128]{2,1,0:T(4,128)S(1)} async-done(((f32[128,4,128]{2,1,0:T(4,128)}), f32[128,4,128]{2,1,0:T(4,128)S(1)}, u32[]{:S(2)}, u32[]{:S(2)}) %all-to-all-start.1) | async-done | bytes 262176 | tf_op jit(solution)/shard_map/all_to_all | solution.py:595
  39.0 1.5 %shard_map.79 = (f32[128,128]{1,0:T(8,128)S(1)}, f32[512,128]{1,0:T(8,128)}) custom-call(f32[512,128]{1,0:T(8,128)S(1)} %bitcast.13, f32[240,256]{1,0:T(8,128)S(1)} %get-tuple-element.47.refs_1_), custom_call_target="tpu_custom_call" | custom-call | flops 100000000 | bytes 2000000 | tf_op jit(solution)/shard_map/pallas_call | solution.py:181
  40.6 8.0 %all-to-all-start.2 = ((f32[128,4,128]{2,1,0:T(4,128)}), f32[128,4,128]{2,1,0:T(4,128)S(1)}, u32[]{:S(2)}, u32[]{:S(2)}) async-start(f32[128,4,128]{2,1,0:T(4,128)} %bitcast.6), calls=%async_computation.2 | async-start | bytes 524288 | tf_op jit(solution)/shard_map/all_to_all | solution.py:595
  48.6 1.1 %shard_map.80 = (f32[4,216,256]{2,1,0:T(8,128)S(1)}, f32[32,128]{1,0:T(8,128)S(1)}, f32[32,128]{1,0:T(8,128)S(1)}, f32[32,128]{1,0:T(8,128)S(1)}, f32[32,128]{1,0:T(8,128)S(1)}) custom-call(f32[4,216,256]{2,1,0:T(8,128)S(1)} %get-tuple-element.49.refs_0_, f32[24,256]{1,0:T(8,128)S(1)} %get-tuple-element.39.refs_4_.refs_1_.refs_6_.refs_5_.refs_3_, ...), custom_call_target="tpu_custom_call" | custom-call | flops 50000000 | bytes 2000000 | tf_op jit(solution)/shard_map/pallas_call | solution.py:181
  49.7 0.1 collective-permute-start.4
  49.8 1.2 %collective-permute-start.5 = (f32[32,128]{1,0:T(8,128)S(1)}, f32[32,128]{1,0:T(8,128)S(1)}, u32[]{:S(2)}, u32[]{:S(2)}) collective-permute-start(f32[32,128]{1,0:T(8,128)S(1)} %get-tuple-element.53), channel_id=1, source_target_pairs={{0,8},{1,2},{2,1},{3,4},{4,3},{5,6},{6,5},{7,15},{8,0},{9,10},{10,... | collective-permute-start | bytes 49160 | tf_op jit(solution)/shard_map/ppermute | solution.py:614
  51.0 0.9 %collective-permute-start.6 = (f32[32,128]{1,0:T(8,128)S(1)}, f32[32,128]{1,0:T(8,128)S(1)}, u32[]{:S(2)}, u32[]{:S(2)}) collective-permute-start(f32[32,128]{1,0:T(8,128)S(1)} %get-tuple-element.54), channel_id=1, source_target_pairs={{0,8},{1,9},{2,10},{3,11},{4,12},{5,13},{6,14},{7,15},{8,0},{9,1},... | collective-permute-start | bytes 49160 | tf_op jit(solution)/shard_map/ppermute | solution.py:614
  51.9 0.4 collective-permute-start.7
  52.3 2.0 %shard_map.81.refs_0_ = f32[4,216,256]{2,1,0:T(8,128)S(1)} custom-call(f32[4,216,256]{2,1,0:T(8,128)S(1)} %get-tuple-element.51.refs_0_, f32[4,216,256]{2,1,0:T(8,128)S(1)} %copy-done.1, bf16[240,216]{1,0:T(8,128)(2,1)S(1)} %copy-done.2, bf16[6,216,216]{2,1,0:T(8,128)(2,1)S(1)} %copy-done.3, s32[6,256]{1,0:T(8,128)S(1)} %copy-done.4, ...), custom_call_target="tpu_custom_call" | custom-call | flops 800000000 | bytes 2000000 | tf_op jit(solution)/shard_map/pallas_call | solution.py:181
  54.4 0.0 collective-permute-done.5.refs_2_
  54.4 0.7 collective-permute-done.6.refs_3_
  55.1 0.0 collective-permute-done.7.refs_4_
  55.1 1.2 %shard_map.82 = (f32[4,216,256]{2,1,0:T(8,128)S(1)}, f32[240,256]{1,0:T(8,128)S(1)}) custom-call(f32[4,216,256]{2,1,0:T(8,128)S(1)} %shard_map.81.refs_0_, f32[32,128]{1,0:T(8,128)S(1)} %collective-permute-done.4.refs_1_, f32[32,128]{1,0:T(8,128)S(1)} %collective-permute-done.5.refs_2_, f32[32,128]{1,0:T(8,128)S(1)} %collective-permute-done.6.refs_3_, ...), custom_call_target="tpu_custom_call" | custom-call | flops 100000000 | bytes 2000000 | tf_op jit(solution)/shard_map/pallas_call | solution.py:181
  56.3 3.0 %all-to-all-done.2 = f32[128,4,128]{2,1,0:T(4,128)S(1)} async-done(((f32[128,4,128]{2,1,0:T(4,128)}), f32[128,4,128]{2,1,0:T(4,128)S(1)}, u32[]{:S(2)}, u32[]{:S(2)}) %all-to-all-start.2) | async-done | bytes 262176 | tf_op jit(solution)/shard_map/all_to_all | solution.py:595
  59.3 1.5 %shard_map.83 = (f32[128,128]{1,0:T(8,128)S(1)}, f32[512,128]{1,0:T(8,128)}) custom-call(f32[512,128]{1,0:T(8,128)S(1)} %bitcast.12, f32[240,256]{1,0:T(8,128)S(1)} %get-tuple-element.56.refs_1_), custom_call_target="tpu_custom_call" | custom-call | flops 100000000 | bytes 2000000 | tf_op jit(solution)/shard_map/pallas_call | solution.py:181
  60.8 8.6 %all-to-all-start.3 = ((f32[128,4,128]{2,1,0:T(4,128)}), f32[128,4,128]{2,1,0:T(4,128)S(1)}, u32[]{:S(2)}, u32[]{:S(2)}) async-start(f32[128,4,128]{2,1,0:T(4,128)} %bitcast.8), calls=%async_computation.3 | async-start | bytes 524288 | tf_op jit(solution)/shard_map/all_to_all | solution.py:595
  69.4 1.1 %shard_map.84 = (f32[4,216,256]{2,1,0:T(8,128)S(1)}, f32[32,128]{1,0:T(8,128)S(1)}, f32[32,128]{1,0:T(8,128)S(1)}, f32[32,128]{1,0:T(8,128)S(1)}, f32[32,128]{1,0:T(8,128)S(1)}) custom-call(f32[4,216,256]{2,1,0:T(8,128)S(1)} %get-tuple-element.58.refs_0_, f32[24,256]{1,0:T(8,128)S(1)} %get-tuple-element.39.refs_4_.refs_1_.refs_6_.refs_5_.refs_3_, ...), custom_call_target="tpu_custom_call" | custom-call | flops 50000000 | bytes 2000000 | tf_op jit(solution)/shard_map/pallas_call | solution.py:181
  70.5 0.1 collective-permute-start.8
  70.6 1.2 %collective-permute-start.9 = (f32[32,128]{1,0:T(8,128)S(1)}, f32[32,128]{1,0:T(8,128)S(1)}, u32[]{:S(2)}, u32[]{:S(2)}) collective-permute-start(f32[32,128]{1,0:T(8,128)S(1)} %get-tuple-element.62), channel_id=1, source_target_pairs={{0,8},{1,2},{2,1},{3,4},{4,3},{5,6},{6,5},{7,15},{8,0},{9,10},{10,... | collective-permute-start | bytes 49160 | tf_op jit(solution)/shard_map/ppermute | solution.py:614
  71.8 0.9 %collective-permute-start.10 = (f32[32,128]{1,0:T(8,128)S(1)}, f32[32,128]{1,0:T(8,128)S(1)}, u32[]{:S(2)}, u32[]{:S(2)}) collective-permute-start(f32[32,128]{1,0:T(8,128)S(1)} %get-tuple-element.63), channel_id=1, source_target_pairs={{0,8},{1,9},{2,10},{3,11},{4,12},{5,13},{6,14},{7,15},{8,0},{9,1},... | collective-permute-start | bytes 49160 | tf_op jit(solution)/shard_map/ppermute | solution.py:614
  72.7 0.4 collective-permute-start.11
  73.1 2.1 %shard_map.85.refs_0_ = f32[4,216,256]{2,1,0:T(8,128)S(1)} custom-call(f32[4,216,256]{2,1,0:T(8,128)S(1)} %get-tuple-element.60.refs_0_, f32[4,216,256]{2,1,0:T(8,128)S(1)} %copy-done.1, bf16[240,216]{1,0:T(8,128)(2,1)S(1)} %copy-done.2, bf16[6,216,216]{2,1,0:T(8,128)(2,1)S(1)} %copy-done.3, s32[6,256]{1,0:T(8,128)S(1)} %copy-done.4, ...), custom_call_target="tpu_custom_call" | custom-call | flops 800000000 | bytes 2000000 | tf_op jit(solution)/shard_map/pallas_call | solution.py:181
  75.2 0.0 collective-permute-done.9.refs_2_
  75.2 0.7 collective-permute-done.10.refs_3_
  75.9 0.0 collective-permute-done.11.refs_4_
  75.9 0.7 shard_map.86
  76.6 3.5 %all-to-all-done.3 = f32[128,4,128]{2,1,0:T(4,128)S(1)} async-done(((f32[128,4,128]{2,1,0:T(4,128)}), f32[128,4,128]{2,1,0:T(4,128)S(1)}, u32[]{:S(2)}, u32[]{:S(2)}) %all-to-all-start.3) | async-done | bytes 262176 | tf_op jit(solution)/shard_map/all_to_all | solution.py:595
  80.1 1.9 %shard_map.87 = f32[4,216,256]{2,1,0:T(8,128)} custom-call(f32[512,128]{1,0:T(8,128)S(1)} %bitcast.11, f32[240,256]{1,0:T(8,128)S(1)} %get-tuple-element.65.refs_1_, f32[4,216,256]{2,1,0:T(8,128)S(1)} %get-tuple-element.66.refs_2_, f32[24,256]{1,0:T(8,128)S(1)} %get-tuple-element.39.refs_4_.refs_1_.refs_6_.refs_5_.refs_3_, bf16[240,216]{1,0:T(8,128)(2,1)S(1)} %copy-done.2), custom_call_target="tpu_custom_call" | custom-call | flops 100000000 | bytes 2000000 | tf_op jit(solution)/shard_map/pallas_call | solution.py:181
  (15 shorter events, 0.0 us)
Async XLA Ops:
  0.0 0.7 copy-start.7
  0.7 12.0 %copy-start.5 = (s32[3,512]{1,0:T(4,128)S(1)}, s32[3,512]{1,0:T(4,128)}, u32[]{:S(2)}) copy-start(s32[3,512]{1,0:T(4,128)} %refs_1_.4) | copy-start | bytes 18436
  1.5 11.2 %copy-start.2 = (bf16[240,216]{1,0:T(8,128)(2,1)S(1)}, bf16[240,216]{1,0:T(8,128)(2,1)}, u32[]{:S(2)}) copy-start(bf16[240,216]{1,0:T(8,128)(2,1)} %constant.4.clone.refs_4_.refs_1_.refs_2_.refs_5_) | copy-start | bytes 311044
  1.5 11.2 %copy-start.4 = (s32[6,256]{1,0:T(8,128)S(1)}, s32[6,256]{1,0:T(8,128)}, u32[]{:S(2)}) copy-start(s32[6,256]{1,0:T(8,128)} %refs_4_.5) | copy-start | bytes 18436
  1.5 20.4 %all-to-all-start = ((f32[128,1,128]{2,1,0:T(1,128)}), f32[128,1,128]{2,1,0:T(1,128)S(1)}, u32[]{:S(2)}, u32[]{:S(2)}) async-start(f32[128,1,128]{2,1,0:T(1,128)} %bitcast.1), calls=%async_computation | async-start | bytes 131072 | tf_op jit(solution)/shard_map/all_to_all | solution.py:595
  12.7 0.7 copy-start.6
  13.4 1.2 %copy-start = (f32[4,216,256]{2,1,0:T(8,128)S(1)}, f32[4,216,256]{2,1,0:T(8,128)}, u32[]{:S(2)}) copy-start(f32[4,216,256]{2,1,0:T(8,128)} %refs_1_.6) | copy-start | bytes 2654212
  14.5 13.7 %copy-start.1 = (f32[4,216,256]{2,1,0:T(8,128)S(1)}, f32[4,216,256]{2,1,0:T(8,128)}, u32[]{:S(2)}) copy-start(f32[4,216,256]{2,1,0:T(8,128)} %refs_1_.6) | copy-start | bytes 2654212
  23.4 8.1 %copy-start.3 = (bf16[6,216,216]{2,1,0:T(8,128)(2,1)S(1)}, bf16[6,216,216]{2,1,0:T(8,128)(2,1)}, u32[]{:S(2)}) copy-start(bf16[6,216,216]{2,1,0:T(8,128)(2,1)} %constant.5.clone.refs_2_.refs_3_) | copy-start | bytes 1679620
  23.4 15.6 %all-to-all-start.1 = ((f32[128,4,128]{2,1,0:T(4,128)}), f32[128,4,128]{2,1,0:T(4,128)S(1)}, u32[]{:S(2)}, u32[]{:S(2)}) async-start(f32[128,4,128]{2,1,0:T(4,128)} %bitcast.4), calls=%async_computation.1 | async-start | bytes 524288 | tf_op jit(solution)/shard_map/all_to_all | solution.py:595
  28.9 4.6 %collective-permute-start = (f32[32,128]{1,0:T(8,128)S(1)}, f32[32,128]{1,0:T(8,128)S(1)}, u32[]{:S(2)}, u32[]{:S(2)}) collective-permute-start(f32[32,128]{1,0:T(8,128)S(1)} %get-tuple-element.41), channel_id=1, source_target_pairs={{0,1},{1,0},{2,3},{3,2},{4,5},{5,4},{6,7},{7,6},{8,9},{9,8},{10,11... | collective-permute-start | bytes 49160 | tf_op jit(solution)/shard_map/ppermute | solution.py:614
  29.0 4.6 %collective-permute-start.1 = (f32[32,128]{1,0:T(8,128)S(1)}, f32[32,128]{1,0:T(8,128)S(1)}, u32[]{:S(2)}, u32[]{:S(2)}) collective-permute-start(f32[32,128]{1,0:T(8,128)S(1)} %get-tuple-element.42), channel_id=1, source_target_pairs={{0,8},{1,2},{2,1},{3,4},{4,3},{5,6},{6,5},{7,15},{8,0},{9,10},{10,... | collective-permute-start | bytes 49160 | tf_op jit(solution)/shard_map/ppermute | solution.py:614
  30.2 3.9 %collective-permute-start.2 = (f32[32,128]{1,0:T(8,128)S(1)}, f32[32,128]{1,0:T(8,128)S(1)}, u32[]{:S(2)}, u32[]{:S(2)}) collective-permute-start(f32[32,128]{1,0:T(8,128)S(1)} %get-tuple-element.43), channel_id=1, source_target_pairs={{0,8},{1,9},{2,10},{3,11},{4,12},{5,13},{6,14},{7,15},{8,0},{9,1},... | collective-permute-start | bytes 49160 | tf_op jit(solution)/shard_map/ppermute | solution.py:614
  31.1 3.0 %collective-permute-start.3 = (f32[32,128]{1,0:T(8,128)S(1)}, f32[32,128]{1,0:T(8,128)S(1)}, u32[]{:S(2)}, u32[]{:S(2)}) collective-permute-start(f32[32,128]{1,0:T(8,128)S(1)} %get-tuple-element.44), channel_id=1, source_target_pairs={{0,1},{1,0},{2,3},{3,2},{4,5},{5,4},{6,7},{7,6},{8,16},{9,17},{10,... | collective-permute-start | bytes 49160 | tf_op jit(solution)/shard_map/ppermute | solution.py:614
  40.6 18.8 %all-to-all-start.2 = ((f32[128,4,128]{2,1,0:T(4,128)}), f32[128,4,128]{2,1,0:T(4,128)S(1)}, u32[]{:S(2)}, u32[]{:S(2)}) async-start(f32[128,4,128]{2,1,0:T(4,128)} %bitcast.6), calls=%async_computation.2 | async-start | bytes 524288 | tf_op jit(solution)/shard_map/all_to_all | solution.py:595
  49.7 4.7 %collective-permute-start.4 = (f32[32,128]{1,0:T(8,128)S(1)}, f32[32,128]{1,0:T(8,128)S(1)}, u32[]{:S(2)}, u32[]{:S(2)}) collective-permute-start(f32[32,128]{1,0:T(8,128)S(1)} %get-tuple-element.52), channel_id=1, source_target_pairs={{0,1},{1,0},{2,3},{3,2},{4,5},{5,4},{6,7},{7,6},{8,9},{9,8},{10,11... | collective-permute-start | bytes 49160 | tf_op jit(solution)/shard_map/ppermute | solution.py:614
  49.8 4.6 %collective-permute-start.5 = (f32[32,128]{1,0:T(8,128)S(1)}, f32[32,128]{1,0:T(8,128)S(1)}, u32[]{:S(2)}, u32[]{:S(2)}) collective-permute-start(f32[32,128]{1,0:T(8,128)S(1)} %get-tuple-element.53), channel_id=1, source_target_pairs={{0,8},{1,2},{2,1},{3,4},{4,3},{5,6},{6,5},{7,15},{8,0},{9,10},{10,... | collective-permute-start | bytes 49160 | tf_op jit(solution)/shard_map/ppermute | solution.py:614
  51.0 4.1 %collective-permute-start.6 = (f32[32,128]{1,0:T(8,128)S(1)}, f32[32,128]{1,0:T(8,128)S(1)}, u32[]{:S(2)}, u32[]{:S(2)}) collective-permute-start(f32[32,128]{1,0:T(8,128)S(1)} %get-tuple-element.54), channel_id=1, source_target_pairs={{0,8},{1,9},{2,10},{3,11},{4,12},{5,13},{6,14},{7,15},{8,0},{9,1},... | collective-permute-start | bytes 49160 | tf_op jit(solution)/shard_map/ppermute | solution.py:614
  51.9 3.2 %collective-permute-start.7 = (f32[32,128]{1,0:T(8,128)S(1)}, f32[32,128]{1,0:T(8,128)S(1)}, u32[]{:S(2)}, u32[]{:S(2)}) collective-permute-start(f32[32,128]{1,0:T(8,128)S(1)} %get-tuple-element.55), channel_id=1, source_target_pairs={{0,1},{1,0},{2,3},{3,2},{4,5},{5,4},{6,7},{7,6},{8,16},{9,17},{10,... | collective-permute-start | bytes 49160 | tf_op jit(solution)/shard_map/ppermute | solution.py:614
  60.8 19.3 %all-to-all-start.3 = ((f32[128,4,128]{2,1,0:T(4,128)}), f32[128,4,128]{2,1,0:T(4,128)S(1)}, u32[]{:S(2)}, u32[]{:S(2)}) async-start(f32[128,4,128]{2,1,0:T(4,128)} %bitcast.8), calls=%async_computation.3 | async-start | bytes 524288 | tf_op jit(solution)/shard_map/all_to_all | solution.py:595
  70.5 4.7 %collective-permute-start.8 = (f32[32,128]{1,0:T(8,128)S(1)}, f32[32,128]{1,0:T(8,128)S(1)}, u32[]{:S(2)}, u32[]{:S(2)}) collective-permute-start(f32[32,128]{1,0:T(8,128)S(1)} %get-tuple-element.61), channel_id=1, source_target_pairs={{0,1},{1,0},{2,3},{3,2},{4,5},{5,4},{6,7},{7,6},{8,9},{9,8},{10,11... | collective-permute-start | bytes 49160 | tf_op jit(solution)/shard_map/ppermute | solution.py:614
  70.6 4.6 %collective-permute-start.9 = (f32[32,128]{1,0:T(8,128)S(1)}, f32[32,128]{1,0:T(8,128)S(1)}, u32[]{:S(2)}, u32[]{:S(2)}) collective-permute-start(f32[32,128]{1,0:T(8,128)S(1)} %get-tuple-element.62), channel_id=1, source_target_pairs={{0,8},{1,2},{2,1},{3,4},{4,3},{5,6},{6,5},{7,15},{8,0},{9,10},{10,... | collective-permute-start | bytes 49160 | tf_op jit(solution)/shard_map/ppermute | solution.py:614
  71.8 4.1 %collective-permute-start.10 = (f32[32,128]{1,0:T(8,128)S(1)}, f32[32,128]{1,0:T(8,128)S(1)}, u32[]{:S(2)}, u32[]{:S(2)}) collective-permute-start(f32[32,128]{1,0:T(8,128)S(1)} %get-tuple-element.63), channel_id=1, source_target_pairs={{0,8},{1,9},{2,10},{3,11},{4,12},{5,13},{6,14},{7,15},{8,0},{9,1},... | collective-permute-start | bytes 49160 | tf_op jit(solution)/shard_map/ppermute | solution.py:614
  72.7 3.2 %collective-permute-start.11 = (f32[32,128]{1,0:T(8,128)S(1)}, f32[32,128]{1,0:T(8,128)S(1)}, u32[]{:S(2)}, u32[]{:S(2)}) collective-permute-start(f32[32,128]{1,0:T(8,128)S(1)} %get-tuple-element.64), channel_id=1, source_target_pairs={{0,1},{1,0},{2,3},{3,2},{4,5},{5,4},{6,7},{7,6},{8,16},{9,17},{10,... | collective-permute-start | bytes 49160 | tf_op jit(solution)/shard_map/ppermute | solution.py:614

commit v6 on v5

--- a/solution.py
+++ b/solution.py
@@ -513,7 +513,7 @@
 
 
 def rim_body(section, *refs):
-    before, r0, r1, r2, r3, select, keys, facts, routes = refs[:9]
+    before, r3, r2, r1, r0, select, keys, facts, routes = refs[:9]
     last = section == 2
     after, pack = refs[9:11]
     scale = keys[SCALE : SCALE + 1, :] * (SECTIONS[section][2] * LIFT)
@@ -683,7 +683,7 @@
         part, held = call(
             bind(rim_body, section),
             [whole, packed],
-            near(after, *rims, select) + far(keys, facts, routes),
+            near(after, *rims[::-1], select) + far(keys, facts, routes),
             scratch=[] if section == 2 else [pad],
         )
         if section < 2:

time: 82.9 us -> 80.4 us (0.970)
  waiting for transfers between devices: 18.5 us -> 12.9 us
  starting transfers between devices: 40.3 us -> 43.5 us
    ppermute x12, starting transfers between devices: 7.78 us -> 13.4 us  [pass_rims(): arrived.append(lax.ppermute(rims[turn], ('blk', 'sub'), pairs))]
    all_to_all x4, waiting for transfers between devices: 16.6 us -> 12.4 us  [exchange(): lax.all_to_all(whole, ('blk', 'sub'), split_axis=0, concat_axis=0, tiled=...]
    all_to_all x4, starting transfers between devices: 32.6 us -> 30.1 us  [exchange(): lax.all_to_all(whole, ('blk', 'sub'), split_axis=0, concat_axis=0, tiled=...]
    ppermute x12, waiting for transfers between devices: 1.89 us -> 0.48 us  [pass_rims(): arrived.append(lax.ppermute(rims[turn], ('blk', 'sub'), pairs))]
  transfers between devices with their start and end apart: 16 -> 16, of which waited for: 7 -> 7; matrix products, arithmetic and copies ran while one was open for 0% -> 0% of each run, Pallas kernels for 16% -> 17%
where the time goes in v6:
time: 80.4 us; the launch traced here: 79.5 us
  starting transfers between devices  43.5 us (54%)
  Pallas kernels  20.5 us (25%)
  waiting for transfers between devices  12.9 us (16%)
  local copies, waits for them, and re-layouts  2.51 us (3%)
    all_to_all x4, starting transfers between devices, exchange(): lax.all_to_all(whole, ('blk', 'sub'), split_axis=0, concat_axis=0, tiled=...  30.1 us
    pallas_call x15, Pallas kernels, call(): pl.pallas_call(kernel, out_shape=[jax.ShapeDtypeStruct(o[0], o[1]) for o...  20.5 us
    ppermute x12, starting transfers between devices, pass_rims(): arrived.append(lax.ppermute(rims[turn], ('blk', 'sub'), pairs))  13.4 us
    all_to_all x4, waiting for transfers between devices, exchange(): lax.all_to_all(whole, ('blk', 'sub'), split_axis=0, concat_axis=0, tiled=...  12.4 us
    unnamed x16, local copies, waits for them, and re-layouts  2.51 us
  transfers between devices with their start and end apart: 16, of which 7 were waited for; matrix products, arithmetic and copies ran while one was open for 0% of the time, Pallas kernels for 17%

profile of v6, /device:TPU:0, one launch (start us, length us, event | category | flops | bytes accessed | tf_op | source)
XLA Modules:
  0.0 79.5 jit_solution(873280475791995994)
XLA Ops:
  0.0 0.7 copy-done.7
  0.7 0.9 %shard_map.73 = f32[128,128]{1,0:T(8,128)} custom-call(s32[2,256]{1,0:T(2,128)S(1)} %copy-done.7), custom_call_target="tpu_custom_call" | custom-call | flops 100000000 | bytes 2000000 | tf_op jit(solution)/shard_map/pallas_call | solution.py:181
  1.5 11.1 %all-to-all-start = ((f32[128,1,128]{2,1,0:T(1,128)}), f32[128,1,128]{2,1,0:T(1,128)S(1)}, u32[]{:S(2)}, u32[]{:S(2)}) async-start(f32[128,1,128]{2,1,0:T(1,128)} %bitcast.1), calls=%async_computation | async-start | bytes 131072 | tf_op jit(solution)/shard_map/all_to_all | solution.py:595
  12.7 0.0 copy-start.6
  12.7 0.6 copy-done.6
  13.4 1.2 %copy-done = f32[4,216,256]{2,1,0:T(8,128)S(1)} copy-done((f32[4,216,256]{2,1,0:T(8,128)S(1)}, f32[4,216,256]{2,1,0:T(8,128)}, u32[]{:S(2)}) %copy-start) | copy-done | bytes 884760
  14.5 1.0 %shard_map.74 = (f32[24,256]{1,0:T(8,128)S(1)}, f32[104,256]{1,0:T(8,128)S(1)}, f32[48,128]{1,0:T(8,128)S(1)}, f32[16,256]{1,0:T(8,128)S(1)}, f32[128,256]{1,0:T(8,128)S(1)}) custom-call(s32[6,256]{1,0:T(8,128)S(1)} %copy-done.4, s32[3,512]{1,0:T(4,128)S(1)} %copy-done.5, f32[1,256]{1,0:T(1,128)S(1)} %bitcast.15, f32[4,216,256]{2,1,0:T(8,128)S(1)} %copy-done, ...), custom_call_target="tpu_custom_call" | custom-call | flops 100000000 | bytes 2000000 | tf_op jit(solution)/shard_map/pallas_call | solution.py:181
  15.5 6.4 %all-to-all-done = f32[128,1,128]{2,1,0:T(1,128)S(1)} async-done(((f32[128,1,128]{2,1,0:T(1,128)}), f32[128,1,128]{2,1,0:T(1,128)S(1)}, u32[]{:S(2)}, u32[]{:S(2)}) %all-to-all-start) | async-done | bytes 65568 | tf_op jit(solution)/shard_map/all_to_all | solution.py:595
  21.9 1.5 %shard_map.75 = (f32[8,256]{1,0:T(8,128)S(1)}, f32[512,128]{1,0:T(8,128)}) custom-call(f32[128,128]{1,0:T(8,128)S(1)} %bitcast.14, f32[16,256]{1,0:T(8,128)S(1)} %get-tuple-element.36.refs_1_, f32[128,256]{1,0:T(8,128)S(1)} %get-tuple-element.37.refs_2_), custom_call_target="tpu_custom_call" | custom-call | flops 100000000 | bytes 2000000 | tf_op jit(solution)/shard_map/pallas_call | solution.py:181
  23.4 4.8 %all-to-all-start.1 = ((f32[128,4,128]{2,1,0:T(4,128)}), f32[128,4,128]{2,1,0:T(4,128)S(1)}, u32[]{:S(2)}, u32[]{:S(2)}) async-start(f32[128,4,128]{2,1,0:T(4,128)} %bitcast.4), calls=%async_computation.1 | async-start | bytes 524288 | tf_op jit(solution)/shard_map/all_to_all | solution.py:595
  28.3 0.6 shard_map.77
  28.9 0.1 collective-permute-start
  29.0 2.8 %collective-permute-start.1 = (f32[32,128]{1,0:T(8,128)S(1)}, f32[32,128]{1,0:T(8,128)S(1)}, u32[]{:S(2)}, u32[]{:S(2)}) collective-permute-start(f32[32,128]{1,0:T(8,128)S(1)} %get-tuple-element.42), channel_id=1, source_target_pairs={{0,8},{1,9},{2,10},{3,11},{4,12},{5,13},{6,14},{7,15},{8,0},{9,1},... | collective-permute-start | bytes 49160 | tf_op jit(solution)/shard_map/ppermute | solution.py:614
  31.8 0.0 collective-permute-start.2
  31.8 1.6 %collective-permute-start.3 = (f32[32,128]{1,0:T(8,128)S(1)}, f32[32,128]{1,0:T(8,128)S(1)}, u32[]{:S(2)}, u32[]{:S(2)}) collective-permute-start(f32[32,128]{1,0:T(8,128)S(1)} %get-tuple-element.44), channel_id=1, source_target_pairs={{0,1},{1,0},{2,3},{3,2},{4,5},{5,4},{6,7},{7,6},{8,9},{9,8},{10,11... | collective-permute-start | bytes 49160 | tf_op jit(solution)/shard_map/ppermute | solution.py:614
  33.4 2.0 %shard_map.76.refs_0_ = f32[4,216,256]{2,1,0:T(8,128)S(1)} custom-call(f32[4,216,256]{2,1,0:T(8,128)S(1)} %copy-done.1, bf16[240,216]{1,0:T(8,128)(2,1)S(1)} %copy-done.2, bf16[6,216,216]{2,1,0:T(8,128)(2,1)S(1)} %copy-done.3, s32[6,256]{1,0:T(8,128)S(1)} %copy-done.4, f32[24,256]{1,0:T(8,128)S(1)} %get-tuple-element.39.refs_4_.refs_1_.refs_6_.refs_5_.refs_3_, ...), custom_call_target="tpu_custom_call" | custom-call | flops 800000000 | bytes 2000000 | tf_op jit(solution)/shard_map/pallas_call | solution.py:181
  35.4 0.0 collective-permute-done.refs_1_
  35.4 0.0 collective-permute-done.1.refs_2_
  35.4 0.1 collective-permute-done.2.refs_3_
  35.5 0.0 collective-permute-done.3.refs_4_
  35.6 1.2 %shard_map.78 = (f32[4,216,256]{2,1,0:T(8,128)S(1)}, f32[240,256]{1,0:T(8,128)S(1)}) custom-call(f32[4,216,256]{2,1,0:T(8,128)S(1)} %shard_map.76.refs_0_, f32[32,128]{1,0:T(8,128)S(1)} %collective-permute-done.refs_1_, f32[32,128]{1,0:T(8,128)S(1)} %collective-permute-done.1.refs_2_, f32[32,128]{1,0:T(8,128)S(1)} %collective-permute-done.2.refs_3_, ...), custom_call_target="tpu_custom_call" | custom-call | flops 100000000 | bytes 2000000 | tf_op jit(solution)/shard_map/pallas_call | solution.py:181
  36.8 2.2 %all-to-all-done.1 = f32[128,4,128]{2,1,0:T(4,128)S(1)} async-done(((f32[128,4,128]{2,1,0:T(4,128)}), f32[128,4,128]{2,1,0:T(4,128)S(1)}, u32[]{:S(2)}, u32[]{:S(2)}) %all-to-all-start.1) | async-done | bytes 262176 | tf_op jit(solution)/shard_map/all_to_all | solution.py:595
  39.0 1.5 %shard_map.79 = (f32[128,128]{1,0:T(8,128)S(1)}, f32[512,128]{1,0:T(8,128)}) custom-call(f32[512,128]{1,0:T(8,128)S(1)} %bitcast.13, f32[240,256]{1,0:T(8,128)S(1)} %get-tuple-element.47.refs_1_), custom_call_target="tpu_custom_call" | custom-call | flops 100000000 | bytes 2000000 | tf_op jit(solution)/shard_map/pallas_call | solution.py:181
  40.5 6.9 %all-to-all-start.2 = ((f32[128,4,128]{2,1,0:T(4,128)}), f32[128,4,128]{2,1,0:T(4,128)S(1)}, u32[]{:S(2)}, u32[]{:S(2)}) async-start(f32[128,4,128]{2,1,0:T(4,128)} %bitcast.6), calls=%async_computation.2 | async-start | bytes 524288 | tf_op jit(solution)/shard_map/all_to_all | solution.py:595
  47.3 1.1 %shard_map.80 = (f32[4,216,256]{2,1,0:T(8,128)S(1)}, f32[32,128]{1,0:T(8,128)S(1)}, f32[32,128]{1,0:T(8,128)S(1)}, f32[32,128]{1,0:T(8,128)S(1)}, f32[32,128]{1,0:T(8,128)S(1)}) custom-call(f32[4,216,256]{2,1,0:T(8,128)S(1)} %get-tuple-element.49.refs_0_, f32[24,256]{1,0:T(8,128)S(1)} %get-tuple-element.39.refs_4_.refs_1_.refs_6_.refs_5_.refs_3_, ...), custom_call_target="tpu_custom_call" | custom-call | flops 50000000 | bytes 2000000 | tf_op jit(solution)/shard_map/pallas_call | solution.py:181
  48.5 0.1 collective-permute-start.4
  48.5 2.8 %collective-permute-start.5 = (f32[32,128]{1,0:T(8,128)S(1)}, f32[32,128]{1,0:T(8,128)S(1)}, u32[]{:S(2)}, u32[]{:S(2)}) collective-permute-start(f32[32,128]{1,0:T(8,128)S(1)} %get-tuple-element.53), channel_id=1, source_target_pairs={{0,8},{1,9},{2,10},{3,11},{4,12},{5,13},{6,14},{7,15},{8,0},{9,1},... | collective-permute-start | bytes 49160 | tf_op jit(solution)/shard_map/ppermute | solution.py:614
  51.3 0.0 collective-permute-start.6
  51.4 1.6 %collective-permute-start.7 = (f32[32,128]{1,0:T(8,128)S(1)}, f32[32,128]{1,0:T(8,128)S(1)}, u32[]{:S(2)}, u32[]{:S(2)}) collective-permute-start(f32[32,128]{1,0:T(8,128)S(1)} %get-tuple-element.55), channel_id=1, source_target_pairs={{0,1},{1,0},{2,3},{3,2},{4,5},{5,4},{6,7},{7,6},{8,9},{9,8},{10,11... | collective-permute-start | bytes 49160 | tf_op jit(solution)/shard_map/ppermute | solution.py:614
  52.9 2.0 %shard_map.81.refs_0_ = f32[4,216,256]{2,1,0:T(8,128)S(1)} custom-call(f32[4,216,256]{2,1,0:T(8,128)S(1)} %get-tuple-element.51.refs_0_, f32[4,216,256]{2,1,0:T(8,128)S(1)} %copy-done.1, bf16[240,216]{1,0:T(8,128)(2,1)S(1)} %copy-done.2, bf16[6,216,216]{2,1,0:T(8,128)(2,1)S(1)} %copy-done.3, s32[6,256]{1,0:T(8,128)S(1)} %copy-done.4, ...), custom_call_target="tpu_custom_call" | custom-call | flops 800000000 | bytes 2000000 | tf_op jit(solution)/shard_map/pallas_call | solution.py:181
  55.0 0.0 collective-permute-done.4.refs_1_
  55.0 0.2 collective-permute-done.6.refs_3_
  55.2 1.2 %shard_map.82 = (f32[4,216,256]{2,1,0:T(8,128)S(1)}, f32[240,256]{1,0:T(8,128)S(1)}) custom-call(f32[4,216,256]{2,1,0:T(8,128)S(1)} %shard_map.81.refs_0_, f32[32,128]{1,0:T(8,128)S(1)} %collective-permute-done.4.refs_1_, f32[32,128]{1,0:T(8,128)S(1)} %collective-permute-done.5.refs_2_, f32[32,128]{1,0:T(8,128)S(1)} %collective-permute-done.6.refs_3_, ...), custom_call_target="tpu_custom_call" | custom-call | flops 100000000 | bytes 2000000 | tf_op jit(solution)/shard_map/pallas_call | solution.py:181
  56.4 1.6 %all-to-all-done.2 = f32[128,4,128]{2,1,0:T(4,128)S(1)} async-done(((f32[128,4,128]{2,1,0:T(4,128)}), f32[128,4,128]{2,1,0:T(4,128)S(1)}, u32[]{:S(2)}, u32[]{:S(2)}) %all-to-all-start.2) | async-done | bytes 262176 | tf_op jit(solution)/shard_map/all_to_all | solution.py:595
  58.1 1.5 %shard_map.83 = (f32[128,128]{1,0:T(8,128)S(1)}, f32[512,128]{1,0:T(8,128)}) custom-call(f32[512,128]{1,0:T(8,128)S(1)} %bitcast.12, f32[240,256]{1,0:T(8,128)S(1)} %get-tuple-element.56.refs_1_), custom_call_target="tpu_custom_call" | custom-call | flops 100000000 | bytes 2000000 | tf_op jit(solution)/shard_map/pallas_call | solution.py:181
  59.6 7.3 %all-to-all-start.3 = ((f32[128,4,128]{2,1,0:T(4,128)}), f32[128,4,128]{2,1,0:T(4,128)S(1)}, u32[]{:S(2)}, u32[]{:S(2)}) async-start(f32[128,4,128]{2,1,0:T(4,128)} %bitcast.8), calls=%async_computation.3 | async-start | bytes 524288 | tf_op jit(solution)/shard_map/all_to_all | solution.py:595
  66.9 1.1 %shard_map.84 = (f32[4,216,256]{2,1,0:T(8,128)S(1)}, f32[32,128]{1,0:T(8,128)S(1)}, f32[32,128]{1,0:T(8,128)S(1)}, f32[32,128]{1,0:T(8,128)S(1)}, f32[32,128]{1,0:T(8,128)S(1)}) custom-call(f32[4,216,256]{2,1,0:T(8,128)S(1)} %get-tuple-element.58.refs_0_, f32[24,256]{1,0:T(8,128)S(1)} %get-tuple-element.39.refs_4_.refs_1_.refs_6_.refs_5_.refs_3_, ...), custom_call_target="tpu_custom_call" | custom-call | flops 50000000 | bytes 2000000 | tf_op jit(solution)/shard_map/pallas_call | solution.py:181
  68.0 0.1 collective-permute-start.8
  68.1 2.8 %collective-permute-start.9 = (f32[32,128]{1,0:T(8,128)S(1)}, f32[32,128]{1,0:T(8,128)S(1)}, u32[]{:S(2)}, u32[]{:S(2)}) collective-permute-start(f32[32,128]{1,0:T(8,128)S(1)} %get-tuple-element.62), channel_id=1, source_target_pairs={{0,8},{1,9},{2,10},{3,11},{4,12},{5,13},{6,14},{7,15},{8,0},{9,1},... | collective-permute-start | bytes 49160 | tf_op jit(solution)/shard_map/ppermute | solution.py:614
  70.9 0.0 collective-permute-start.10
  70.9 1.6 %collective-permute-start.11 = (f32[32,128]{1,0:T(8,128)S(1)}, f32[32,128]{1,0:T(8,128)S(1)}, u32[]{:S(2)}, u32[]{:S(2)}) collective-permute-start(f32[32,128]{1,0:T(8,128)S(1)} %get-tuple-element.64), channel_id=1, source_target_pairs={{0,1},{1,0},{2,3},{3,2},{4,5},{5,4},{6,7},{7,6},{8,9},{9,8},{10,11... | collective-permute-start | bytes 49160 | tf_op jit(solution)/shard_map/ppermute | solution.py:614
  72.5 2.0 %shard_map.85.refs_0_ = f32[4,216,256]{2,1,0:T(8,128)S(1)} custom-call(f32[4,216,256]{2,1,0:T(8,128)S(1)} %get-tuple-element.60.refs_0_, f32[4,216,256]{2,1,0:T(8,128)S(1)} %copy-done.1, bf16[240,216]{1,0:T(8,128)(2,1)S(1)} %copy-done.2, bf16[6,216,216]{2,1,0:T(8,128)(2,1)S(1)} %copy-done.3, s32[6,256]{1,0:T(8,128)S(1)} %copy-done.4, ...), custom_call_target="tpu_custom_call" | custom-call | flops 800000000 | bytes 2000000 | tf_op jit(solution)/shard_map/pallas_call | solution.py:181
  74.5 0.0 collective-permute-done.8.refs_1_
  74.6 0.0 collective-permute-done.9.refs_2_
  74.6 0.2 collective-permute-done.10.refs_3_
  74.7 0.7 shard_map.86
  75.5 2.2 %all-to-all-done.3 = f32[128,4,128]{2,1,0:T(4,128)S(1)} async-done(((f32[128,4,128]{2,1,0:T(4,128)}), f32[128,4,128]{2,1,0:T(4,128)S(1)}, u32[]{:S(2)}, u32[]{:S(2)}) %all-to-all-start.3) | async-done | bytes 262176 | tf_op jit(solution)/shard_map/all_to_all | solution.py:595
  77.6 1.9 %shard_map.87 = f32[4,216,256]{2,1,0:T(8,128)} custom-call(f32[512,128]{1,0:T(8,128)S(1)} %bitcast.11, f32[240,256]{1,0:T(8,128)S(1)} %get-tuple-element.65.refs_1_, f32[4,216,256]{2,1,0:T(8,128)S(1)} %get-tuple-element.66.refs_2_, f32[24,256]{1,0:T(8,128)S(1)} %get-tuple-element.39.refs_4_.refs_1_.refs_6_.refs_5_.refs_3_, bf16[240,216]{1,0:T(8,128)(2,1)S(1)} %copy-done.2), custom_call_target="tpu_custom_call" | custom-call | flops 100000000 | bytes 2000000 | tf_op jit(solution)/shard_map/pallas_call | solution.py:181
  (15 shorter events, 0.0 us)
Async XLA Ops:
  0.0 0.7 copy-start.7
  0.7 12.0 %copy-start.5 = (s32[3,512]{1,0:T(4,128)S(1)}, s32[3,512]{1,0:T(4,128)}, u32[]{:S(2)}) copy-start(s32[3,512]{1,0:T(4,128)} %refs_1_.4) | copy-start | bytes 18436
  1.5 11.2 %copy-start.2 = (bf16[240,216]{1,0:T(8,128)(2,1)S(1)}, bf16[240,216]{1,0:T(8,128)(2,1)}, u32[]{:S(2)}) copy-start(bf16[240,216]{1,0:T(8,128)(2,1)} %constant.4.clone.refs_4_.refs_1_.refs_2_.refs_5_) | copy-start | bytes 311044
  1.5 11.2 %copy-start.4 = (s32[6,256]{1,0:T(8,128)S(1)}, s32[6,256]{1,0:T(8,128)}, u32[]{:S(2)}) copy-start(s32[6,256]{1,0:T(8,128)} %refs_4_.5) | copy-start | bytes 18436
  1.5 20.4 %all-to-all-start = ((f32[128,1,128]{2,1,0:T(1,128)}), f32[128,1,128]{2,1,0:T(1,128)S(1)}, u32[]{:S(2)}, u32[]{:S(2)}) async-start(f32[128,1,128]{2,1,0:T(1,128)} %bitcast.1), calls=%async_computation | async-start | bytes 131072 | tf_op jit(solution)/shard_map/all_to_all | solution.py:595
  12.7 0.7 copy-start.6
  13.4 1.2 %copy-start = (f32[4,216,256]{2,1,0:T(8,128)S(1)}, f32[4,216,256]{2,1,0:T(8,128)}, u32[]{:S(2)}) copy-start(f32[4,216,256]{2,1,0:T(8,128)} %refs_1_.6) | copy-start | bytes 2654212
  14.5 13.7 %copy-start.1 = (f32[4,216,256]{2,1,0:T(8,128)S(1)}, f32[4,216,256]{2,1,0:T(8,128)}, u32[]{:S(2)}) copy-start(f32[4,216,256]{2,1,0:T(8,128)} %refs_1_.6) | copy-start | bytes 2654212
  23.4 9.9 %copy-start.3 = (bf16[6,216,216]{2,1,0:T(8,128)(2,1)S(1)}, bf16[6,216,216]{2,1,0:T(8,128)(2,1)}, u32[]{:S(2)}) copy-start(bf16[6,216,216]{2,1,0:T(8,128)(2,1)} %constant.5.clone.refs_2_.refs_3_) | copy-start | bytes 1679620
  23.4 15.5 %all-to-all-start.1 = ((f32[128,4,128]{2,1,0:T(4,128)}), f32[128,4,128]{2,1,0:T(4,128)S(1)}, u32[]{:S(2)}, u32[]{:S(2)}) async-start(f32[128,4,128]{2,1,0:T(4,128)} %bitcast.4), calls=%async_computation.1 | async-start | bytes 524288 | tf_op jit(solution)/shard_map/all_to_all | solution.py:595
  28.9 6.5 %collective-permute-start = (f32[32,128]{1,0:T(8,128)S(1)}, f32[32,128]{1,0:T(8,128)S(1)}, u32[]{:S(2)}, u32[]{:S(2)}) collective-permute-start(f32[32,128]{1,0:T(8,128)S(1)} %get-tuple-element.41), channel_id=1, source_target_pairs={{0,1},{1,0},{2,3},{3,2},{4,5},{5,4},{6,7},{7,6},{8,16},{9,17},{10,... | collective-permute-start | bytes 49160 | tf_op jit(solution)/shard_map/ppermute | solution.py:614
  29.0 6.4 %collective-permute-start.1 = (f32[32,128]{1,0:T(8,128)S(1)}, f32[32,128]{1,0:T(8,128)S(1)}, u32[]{:S(2)}, u32[]{:S(2)}) collective-permute-start(f32[32,128]{1,0:T(8,128)S(1)} %get-tuple-element.42), channel_id=1, source_target_pairs={{0,8},{1,9},{2,10},{3,11},{4,12},{5,13},{6,14},{7,15},{8,0},{9,1},... | collective-permute-start | bytes 49160 | tf_op jit(solution)/shard_map/ppermute | solution.py:614
  31.8 3.8 %collective-permute-start.2 = (f32[32,128]{1,0:T(8,128)S(1)}, f32[32,128]{1,0:T(8,128)S(1)}, u32[]{:S(2)}, u32[]{:S(2)}) collective-permute-start(f32[32,128]{1,0:T(8,128)S(1)} %get-tuple-element.43), channel_id=1, source_target_pairs={{0,8},{1,2},{2,1},{3,4},{4,3},{5,6},{6,5},{7,15},{8,0},{9,10},{10,... | collective-permute-start | bytes 49160 | tf_op jit(solution)/shard_map/ppermute | solution.py:614
  31.8 3.7 %collective-permute-start.3 = (f32[32,128]{1,0:T(8,128)S(1)}, f32[32,128]{1,0:T(8,128)S(1)}, u32[]{:S(2)}, u32[]{:S(2)}) collective-permute-start(f32[32,128]{1,0:T(8,128)S(1)} %get-tuple-element.44), channel_id=1, source_target_pairs={{0,1},{1,0},{2,3},{3,2},{4,5},{5,4},{6,7},{7,6},{8,9},{9,8},{10,11... | collective-permute-start | bytes 49160 | tf_op jit(solution)/shard_map/ppermute | solution.py:614
  40.5 17.6 %all-to-all-start.2 = ((f32[128,4,128]{2,1,0:T(4,128)}), f32[128,4,128]{2,1,0:T(4,128)S(1)}, u32[]{:S(2)}, u32[]{:S(2)}) async-start(f32[128,4,128]{2,1,0:T(4,128)} %bitcast.6), calls=%async_computation.2 | async-start | bytes 524288 | tf_op jit(solution)/shard_map/all_to_all | solution.py:595
  48.5 6.5 %collective-permute-start.4 = (f32[32,128]{1,0:T(8,128)S(1)}, f32[32,128]{1,0:T(8,128)S(1)}, u32[]{:S(2)}, u32[]{:S(2)}) collective-permute-start(f32[32,128]{1,0:T(8,128)S(1)} %get-tuple-element.52), channel_id=1, source_target_pairs={{0,1},{1,0},{2,3},{3,2},{4,5},{5,4},{6,7},{7,6},{8,16},{9,17},{10,... | collective-permute-start | bytes 49160 | tf_op jit(solution)/shard_map/ppermute | solution.py:614
  48.5 6.5 %collective-permute-start.5 = (f32[32,128]{1,0:T(8,128)S(1)}, f32[32,128]{1,0:T(8,128)S(1)}, u32[]{:S(2)}, u32[]{:S(2)}) collective-permute-start(f32[32,128]{1,0:T(8,128)S(1)} %get-tuple-element.53), channel_id=1, source_target_pairs={{0,8},{1,9},{2,10},{3,11},{4,12},{5,13},{6,14},{7,15},{8,0},{9,1},... | collective-permute-start | bytes 49160 | tf_op jit(solution)/shard_map/ppermute | solution.py:614
  51.3 3.8 %collective-permute-start.6 = (f32[32,128]{1,0:T(8,128)S(1)}, f32[32,128]{1,0:T(8,128)S(1)}, u32[]{:S(2)}, u32[]{:S(2)}) collective-permute-start(f32[32,128]{1,0:T(8,128)S(1)} %get-tuple-element.54), channel_id=1, source_target_pairs={{0,8},{1,2},{2,1},{3,4},{4,3},{5,6},{6,5},{7,15},{8,0},{9,10},{10,... | collective-permute-start | bytes 49160 | tf_op jit(solution)/shard_map/ppermute | solution.py:614
  51.4 3.8 %collective-permute-start.7 = (f32[32,128]{1,0:T(8,128)S(1)}, f32[32,128]{1,0:T(8,128)S(1)}, u32[]{:S(2)}, u32[]{:S(2)}) collective-permute-start(f32[32,128]{1,0:T(8,128)S(1)} %get-tuple-element.55), channel_id=1, source_target_pairs={{0,1},{1,0},{2,3},{3,2},{4,5},{5,4},{6,7},{7,6},{8,9},{9,8},{10,11... | collective-permute-start | bytes 49160 | tf_op jit(solution)/shard_map/ppermute | solution.py:614
  59.6 18.0 %all-to-all-start.3 = ((f32[128,4,128]{2,1,0:T(4,128)}), f32[128,4,128]{2,1,0:T(4,128)S(1)}, u32[]{:S(2)}, u32[]{:S(2)}) async-start(f32[128,4,128]{2,1,0:T(4,128)} %bitcast.8), calls=%async_computation.3 | async-start | bytes 524288 | tf_op jit(solution)/shard_map/all_to_all | solution.py:595
  68.0 6.5 %collective-permute-start.8 = (f32[32,128]{1,0:T(8,128)S(1)}, f32[32,128]{1,0:T(8,128)S(1)}, u32[]{:S(2)}, u32[]{:S(2)}) collective-permute-start(f32[32,128]{1,0:T(8,128)S(1)} %get-tuple-element.61), channel_id=1, source_target_pairs={{0,1},{1,0},{2,3},{3,2},{4,5},{5,4},{6,7},{7,6},{8,16},{9,17},{10,... | collective-permute-start | bytes 49160 | tf_op jit(solution)/shard_map/ppermute | solution.py:614
  68.1 6.5 %collective-permute-start.9 = (f32[32,128]{1,0:T(8,128)S(1)}, f32[32,128]{1,0:T(8,128)S(1)}, u32[]{:S(2)}, u32[]{:S(2)}) collective-permute-start(f32[32,128]{1,0:T(8,128)S(1)} %get-tuple-element.62), channel_id=1, source_target_pairs={{0,8},{1,9},{2,10},{3,11},{4,12},{5,13},{6,14},{7,15},{8,0},{9,1},... | collective-permute-start | bytes 49160 | tf_op jit(solution)/shard_map/ppermute | solution.py:614
  70.9 3.8 %collective-permute-start.10 = (f32[32,128]{1,0:T(8,128)S(1)}, f32[32,128]{1,0:T(8,128)S(1)}, u32[]{:S(2)}, u32[]{:S(2)}) collective-permute-start(f32[32,128]{1,0:T(8,128)S(1)} %get-tuple-element.63), channel_id=1, source_target_pairs={{0,8},{1,2},{2,1},{3,4},{4,3},{5,6},{6,5},{7,15},{8,0},{9,10},{10,... | collective-permute-start | bytes 49160 | tf_op jit(solution)/shard_map/ppermute | solution.py:614
  70.9 3.8 %collective-permute-start.11 = (f32[32,128]{1,0:T(8,128)S(1)}, f32[32,128]{1,0:T(8,128)S(1)}, u32[]{:S(2)}, u32[]{:S(2)}) collective-permute-start(f32[32,128]{1,0:T(8,128)S(1)} %get-tuple-element.64), channel_id=1, source_target_pairs={{0,1},{1,0},{2,3},{3,2},{4,5},{5,4},{6,7},{7,6},{8,9},{9,8},{10,11... | collective-permute-start | bytes 49160 | tf_op jit(solution)/shard_map/ppermute | solution.py:614

commit v7 on v6

--- a/solution.py
+++ b/solution.py
@@ -111,6 +111,20 @@
 def halves(x):
     high = x.astype(BF16)
     return high, (x - high.astype(F32)).astype(BF16)
+
+
+def stacked(x):
+    return jnp.concatenate(halves(x), axis=0)
+
+
+def fold(x):
+    count = x.shape[0] // 2
+    return x[:count, :] + x[count:, :]
+
+
+def fold_lanes(x):
+    count = x.shape[1] // 2
+    return x[:, :count] + x[:, count:]
 
 
 def nn2(exact, x):
@@ -177,7 +191,7 @@
         for copy in copies:
             copy.wait()
 
-    spaces = {"h": pltpu.HBM, "v": pltpu.VMEM}
+    spaces = {"h": pltpu.HBM, "v": pltpu.VMEM, "r": pltpu.HBM}
     return pl.pallas_call(
         kernel,
         out_shape=[jax.ShapeDtypeStruct(o[0], o[1]) for o in outs],
@@ -225,10 +239,8 @@
 
 
 def at_faces(rows4, rows5, members):
-    high5, low5 = halves(rows5)
-    high4, low4 = halves(rows4)
-    rotor = nt(high5, members) + nt(low5, members)
-    stator = nt(high4, members) + nt(low4, members)
+    rotor = fold(nt(stacked(rows5), members))
+    stator = fold(nt(stacked(rows4), members))
     return jnp.where(iota((FEAT, FACES), 1) < IFD, rotor, stator)
 
 
@@ -240,8 +252,7 @@
 
 
 def nn2b(x, exact):
-    high, low = halves(x)
-    return nn(high, exact) + nn(low, exact)
+    return fold(nn(stacked(x), exact))
 
 
 def comp(rows, c):
@@ -366,8 +377,7 @@
 
 
 def send_rows(exact, values):
-    high, low = halves(values)
-    return nt(exact, high) + nt(exact, low)
+    return fold_lanes(nt(exact, stacked(values)))
 
 
 def route_body(facts, info, mortars, routes, payload):
@@ -407,13 +417,11 @@
 def place_interface(part, arrived, keys, select):
     picks = select[4 * TR : 6 * TR, :]
     to4, to5 = at_elements(arrived[...], member_picks(keys))
-    result = []
     for c in range(4):
         source = (0, 1, 2, 0)[c]
         sign5 = -1.0 if c == 3 else 1.0
         stack = jnp.concatenate([comp(to4, source), sign5 * comp(to5, source)], axis=0)
-        result.append(part[c] + placed(picks, stack))
-    return result
+        yield part[c] + placed(picks, stack)
 
 
 def characteristics(traces, faces):
@@ -425,7 +433,7 @@
         along = face // 2
         tangent = [cut[1 + c] for c in range(3) if c != along]
         normal = sign * cut[1 + along]
-        leaving.append(halves(jnp.concatenate([cut[0] + normal] + tangent + [blank], axis=0)))
+        leaving.append(stacked(jnp.concatenate([cut[0] + normal] + tangent + [blank], axis=0)))
         inside.append(jnp.concatenate([cut[0] - normal] + tangent + [blank], axis=0))
     return leaving, inside
 
@@ -437,7 +445,7 @@
         rims = refs[3:]
     else:
         arrived, whole = refs[3:5]
-        fields = place_interface(part, arrived, keys, select)
+        fields = list(place_interface(part, arrived, keys, select))
         rims = refs[5:]
         for c in range(4):
             whole[c] = fields[c]
@@ -445,7 +453,7 @@
     parts = []
     for face in range(4):
         pick = picked(keys, RIM_OUT + face, RIM)
-        parts.append(nt(pick, leaving[face][0]) + nt(pick, leaving[face][1]))
+        parts.append(fold_lanes(nt(pick, leaving[face])))
     for turn, (down, up) in enumerate((parts[:2], parts[2:])):
         even = even_place(turn)
         rims[2 * turn][...] = jnp.where(even, up, down)
@@ -478,7 +486,7 @@
     terms = []
     for face in range(6):
         pick = picked(keys, NEAR + face, ELEMS)
-        arriving = nn(leaving[face ^ 1][0], pick) + nn(leaving[face ^ 1][1], pick)
+        arriving = fold(nn(leaving[face ^ 1], pick))
         term = 0.5 * (arriving - inside[face])
         if face >= 4:
             term = jnp.where(neighbours[face : face + 1, :] == -2, 0.0, term)
@@ -513,9 +521,12 @@
 
 
 def rim_body(section, *refs):
-    before, r3, r2, r1, r0, select, keys, facts, routes = refs[:9]
+    before, r3, r2, r1, r0, select, keys = refs[:7]
     last = section == 2
-    after, pack = refs[9:11]
+    if last:
+        after = refs[7]
+    else:
+        facts, after = refs[7:9]
     scale = keys[SCALE : SCALE + 1, :] * (SECTIONS[section][2] * LIFT)
     terms = []
     terms = []
@@ -543,22 +554,19 @@
         value = before[c] + scale * placed(select[0 : 4 * TR, :], jnp.concatenate(pieces, axis=0))
         after[c] = value
         fields.append(value)
-    pack[0:FACT_ROWS, :] = facts[...]
-    pack[ROUTES : ROUTES + 8, :] = routes[...]
     if not last:
-        pad = refs[11]
+        mortars, pad = refs[9:]
         traces = [nn2(select[4 * TR : 6 * TR, :], x) for x in fields]
         out4, out5 = outgoing([t[:TR] for t in traces], [t[TR:] for t in traces])
         spread(at_faces(out4, out5, member_picks(keys)), pad, FACES)
-        mortars = pack.at[FACT_ROWS:ROUTES, :]
         mortars[...] = jnp.zeros((FEAT, 2 * FACES), F32)
         to_mortars(facts, pad, mortars, (0, 1, 2), False)
 
 
-def arrive(section, arrivals, held, pad, wide, out):
-    high, low = halves(arrivals[...])
-    pick = slot_picks(held[ROUTES + 1 : ROUTES + 2, :])
-    spread(tn(high, pick) + tn(low, pick), wide, 2 * FACES)
+def arrive(section, arrivals, held, routes, pad, wide, out):
+    both = jnp.concatenate(halves(arrivals[...]), axis=1)
+    pick = slot_picks(routes[1:2, :])
+    spread(fold(tn(both, pick)), wide, 2 * FACES)
     scale = held[METRIC : METRIC + 1, 0:FACES] * (SECTIONS[section][2] * LIFT)
     out[...] = jnp.zeros(out.shape, F32)
     for c in range(3):
@@ -576,18 +584,26 @@
             out[start : start + P_SIZE, :] = total[0:P_SIZE, :]
 
 
-def flux_body(section, arrivals, held, arrived, payload, pad, wide, mixed):
-    arrive(section, arrivals, held, pad, wide, arrived)
-    mixed[...] = held[FACT_ROWS:ROUTES, :]
-    to_mortars(held, pad, mixed, (1, 2), True)
-    payload[...] = send_rows(slot_picks(held[ROUTES : ROUTES + 1, :]), mixed[...])
-
-
-def last_body(arrivals, held, part, keys, select, after, pad, wide, arrived):
-    arrive(2, arrivals, held, pad, wide, arrived)
-    result = place_interface(part, arrived, keys, select)
-    for c in range(4):
-        after[c] = result[c]
+def flux_body(
+    section, arrivals, facts, routes, mortars, arrived, payload, pad, wide, mixed
+):
+    arrive(section, arrivals, facts, routes, pad, wide, arrived)
+    mixed[...] = mortars[...]
+    to_mortars(facts, pad, mixed, (1, 2), True)
+    payload[...] = send_rows(slot_picks(routes[0:1, :]), mixed[...])
+
+
+def last_body(
+    arrivals, facts, routes, part, keys, select, after, pad, wide, arrived, whole, sems
+):
+    arrive(2, arrivals, facts, routes, pad, wide, arrived)
+    copies = []
+    for c, value in enumerate(place_interface(part, arrived, keys, select)):
+        whole[c] = value
+        copies.append(pltpu.make_async_copy(whole.at[c], after.at[c], sems.at[c]))
+        copies[-1].start()
+    for copy in copies:
+        copy.wait()
 
 
 def exchange(rows, width):
@@ -680,24 +696,30 @@
             scratch=[pad, narrow],
             flops=8e8,
         )
-        part, held = call(
-            bind(rim_body, section),
-            [whole, packed],
-            near(after, *rims[::-1], select) + far(keys, facts, routes),
-            scratch=[] if section == 2 else [pad],
-        )
-        if section < 2:
+        given = near(after, *rims[::-1], select, keys)
+        if section == 2:
+            (part,) = call(bind(rim_body, section), [whole], given)
+        else:
+            part, mortars = call(
+                bind(rim_body, section),
+                [whole, ((FEAT, 2 * FACES), F32, "v")],
+                given + near(facts),
+                scratch=[pad],
+            )
             arrived, payload = call(
                 bind(flux_body, section),
                 [((FEAT, FACES), F32, "v"), ((SLOTS, FEAT), F32, "v")],
-                near(arrivals, held),
+                near(arrivals, facts, routes, mortars),
                 scratch=[pad, wide, broad],
             )
     (result,) = call(
         last_body,
-        [whole],
-        near(arrivals, held, part) + far(keys) + near(select),
-        scratch=[pad, wide, narrow],
+        [((4, NODES, ELEMS), F32, "r")],
+        near(arrivals, facts, routes, part, keys, select),
+        scratch=[
+            pad, wide, narrow,
+            pltpu.VMEM((4, NODES, ELEMS), F32), pltpu.SemaphoreType.DMA((4,)),
+        ],
     )
     return result
 

time: 80.4 us -> 80.3 us (level)
  transfers between devices with their start and end apart: 16 -> 16, of which waited for: 7 -> 7; matrix products, arithmetic and copies ran while one was open for 0% -> 0% of each run, Pallas kernels for 17% -> 16%
where the time goes in v7:
time: 80.3 us; the launch traced here: 79.4 us
  starting transfers between devices  43.6 us (54%)
  Pallas kernels  20 us (25%)
  waiting for transfers between devices  12.9 us (16%)
  local copies, waits for them, and re-layouts  2.51 us (3%)
    all_to_all x4, starting transfers between devices, exchange(): lax.all_to_all(whole, ('blk', 'sub'), split_axis=0, concat_axis=0, tiled=...  30.2 us
    pallas_call x15, Pallas kernels, call(): pl.pallas_call(kernel, out_shape=[jax.ShapeDtypeStruct(o[0], o[1]) for o...  20 us
    ppermute x12, starting transfers between devices, pass_rims(): arrived.append(lax.ppermute(rims[turn], ('blk', 'sub'), pairs))  13.4 us
    all_to_all x4, waiting for transfers between devices, exchange(): lax.all_to_all(whole, ('blk', 'sub'), split_axis=0, concat_axis=0, tiled=...  12.3 us
    unnamed x16, local copies, waits for them, and re-layouts  2.51 us
  transfers between devices with their start and end apart: 16, of which 7 were waited for; matrix products, arithmetic and copies ran while one was open for 0% of the time, Pallas kernels for 16%

profile of v7, /device:TPU:0, one launch (start us, length us, event | category | flops | bytes accessed | tf_op | source)
XLA Modules:
  0.0 79.4 jit_solution(7253576317502502872)
XLA Ops:
  0.0 0.7 copy-done.7
  0.7 0.9 %shard_map.73 = f32[128,128]{1,0:T(8,128)} custom-call(s32[2,256]{1,0:T(2,128)S(1)} %copy-done.7), custom_call_target="tpu_custom_call" | custom-call | flops 100000000 | bytes 2000000 | tf_op jit(solution)/shard_map/pallas_call | solution.py:195
  1.5 11.1 %all-to-all-start = ((f32[128,1,128]{2,1,0:T(1,128)}), f32[128,1,128]{2,1,0:T(1,128)S(1)}, u32[]{:S(2)}, u32[]{:S(2)}) async-start(f32[128,1,128]{2,1,0:T(1,128)} %bitcast.1), calls=%async_computation | async-start | bytes 131072 | tf_op jit(solution)/shard_map/all_to_all | solution.py:611
  12.7 0.0 copy-start.6
  12.7 0.6 copy-done.6
  13.4 1.2 %copy-done = f32[4,216,256]{2,1,0:T(8,128)S(1)} copy-done((f32[4,216,256]{2,1,0:T(8,128)S(1)}, f32[4,216,256]{2,1,0:T(8,128)}, u32[]{:S(2)}) %copy-start) | copy-done | bytes 884760
  14.5 1.0 %shard_map.74 = (f32[24,256]{1,0:T(8,128)S(1)}, f32[104,256]{1,0:T(8,128)S(1)}, f32[48,128]{1,0:T(8,128)S(1)}, f32[16,256]{1,0:T(8,128)S(1)}, f32[128,256]{1,0:T(8,128)S(1)}) custom-call(s32[6,256]{1,0:T(8,128)S(1)} %copy-done.4, s32[3,512]{1,0:T(4,128)S(1)} %copy-done.5, f32[1,256]{1,0:T(1,128)S(1)} %bitcast.15, f32[4,216,256]{2,1,0:T(8,128)S(1)} %copy-done, ...), custom_call_target="tpu_custom_call" | custom-call | flops 100000000 | bytes 2000000 | tf_op jit(solution)/shard_map/pallas_call | solution.py:195
  15.5 6.4 %all-to-all-done = f32[128,1,128]{2,1,0:T(1,128)S(1)} async-done(((f32[128,1,128]{2,1,0:T(1,128)}), f32[128,1,128]{2,1,0:T(1,128)S(1)}, u32[]{:S(2)}, u32[]{:S(2)}) %all-to-all-start) | async-done | bytes 65568 | tf_op jit(solution)/shard_map/all_to_all | solution.py:611
  21.9 1.5 %shard_map.75 = (f32[8,256]{1,0:T(8,128)S(1)}, f32[512,128]{1,0:T(8,128)}) custom-call(f32[128,128]{1,0:T(8,128)S(1)} %bitcast.14, f32[16,256]{1,0:T(8,128)S(1)} %get-tuple-element.34.refs_1_, f32[128,256]{1,0:T(8,128)S(1)} %get-tuple-element.35.refs_2_), custom_call_target="tpu_custom_call" | custom-call | flops 100000000 | bytes 2000000 | tf_op jit(solution)/shard_map/pallas_call | solution.py:195
  23.4 4.8 %all-to-all-start.1 = ((f32[128,4,128]{2,1,0:T(4,128)}), f32[128,4,128]{2,1,0:T(4,128)S(1)}, u32[]{:S(2)}, u32[]{:S(2)}) async-start(f32[128,4,128]{2,1,0:T(4,128)} %bitcast.4), calls=%async_computation.1 | async-start | bytes 524288 | tf_op jit(solution)/shard_map/all_to_all | solution.py:611
  28.2 0.7 shard_map.77
  28.9 0.1 collective-permute-start
  28.9 2.8 %collective-permute-start.1 = (f32[32,128]{1,0:T(8,128)S(1)}, f32[32,128]{1,0:T(8,128)S(1)}, u32[]{:S(2)}, u32[]{:S(2)}) collective-permute-start(f32[32,128]{1,0:T(8,128)S(1)} %get-tuple-element.42), channel_id=1, source_target_pairs={{0,8},{1,9},{2,10},{3,11},{4,12},{5,13},{6,14},{7,15},{8,0},{9,1},... | collective-permute-start | bytes 49160 | tf_op jit(solution)/shard_map/ppermute | solution.py:630
  31.7 0.0 collective-permute-start.2
  31.8 1.6 %collective-permute-start.3 = (f32[32,128]{1,0:T(8,128)S(1)}, f32[32,128]{1,0:T(8,128)S(1)}, u32[]{:S(2)}, u32[]{:S(2)}) collective-permute-start(f32[32,128]{1,0:T(8,128)S(1)} %get-tuple-element.44), channel_id=1, source_target_pairs={{0,1},{1,0},{2,3},{3,2},{4,5},{5,4},{6,7},{7,6},{8,9},{9,8},{10,11... | collective-permute-start | bytes 49160 | tf_op jit(solution)/shard_map/ppermute | solution.py:630
  33.3 2.0 %shard_map.76.refs_0_ = f32[4,216,256]{2,1,0:T(8,128)S(1)} custom-call(f32[4,216,256]{2,1,0:T(8,128)S(1)} %copy-done.1, bf16[240,216]{1,0:T(8,128)(2,1)S(1)} %copy-done.2, bf16[6,216,216]{2,1,0:T(8,128)(2,1)S(1)} %copy-done.3, s32[6,256]{1,0:T(8,128)S(1)} %copy-done.4, f32[24,256]{1,0:T(8,128)S(1)} %get-tuple-element.39.refs_4_.refs_1_.refs_6_.refs_5_, ...), custom_call_target="tpu_custom_call" | custom-call | flops 800000000 | bytes 2000000 | tf_op jit(solution)/shard_map/pallas_call | solution.py:195
  35.3 0.0 collective-permute-done.refs_1_
  35.3 0.0 collective-permute-done.1.refs_2_
  35.4 0.2 collective-permute-done.2.refs_3_
  35.5 0.0 collective-permute-done.3.refs_4_
  35.5 1.2 %shard_map.78 = (f32[4,216,256]{2,1,0:T(8,128)S(1)}, f32[128,256]{1,0:T(8,128)S(1)}) custom-call(f32[4,216,256]{2,1,0:T(8,128)S(1)} %shard_map.76.refs_0_, f32[32,128]{1,0:T(8,128)S(1)} %collective-permute-done.refs_1_, f32[32,128]{1,0:T(8,128)S(1)} %collective-permute-done.1.refs_2_, f32[32,128]{1,0:T(8,128)S(1)} %collective-permute-done.2.refs_3_, ...), custom_call_target="tpu_custom_call" | custom-call | flops 100000000 | bytes 2000000 | tf_op jit(solution)/shard_map/pallas_call | solution.py:195
  36.8 2.1 %all-to-all-done.1 = f32[128,4,128]{2,1,0:T(4,128)S(1)} async-done(((f32[128,4,128]{2,1,0:T(4,128)}), f32[128,4,128]{2,1,0:T(4,128)S(1)}, u32[]{:S(2)}, u32[]{:S(2)}) %all-to-all-start.1) | async-done | bytes 262176 | tf_op jit(solution)/shard_map/all_to_all | solution.py:611
  38.9 1.4 %shard_map.79 = (f32[128,128]{1,0:T(8,128)S(1)}, f32[512,128]{1,0:T(8,128)}) custom-call(f32[512,128]{1,0:T(8,128)S(1)} %bitcast.13, f32[104,256]{1,0:T(8,128)S(1)} %get-tuple-element.37.refs_7_.refs_1_, f32[8,256]{1,0:T(8,128)S(1)} %get-tuple-element.38.refs_2_, f32[128,256]{1,0:T(8,128)S(1)} %get-tuple-element.45.refs_3_), custom_call_target="tpu_custom_call" | custom-call | flops 100000000 | bytes 2000000 | tf_op jit(solution)/shard_map/pallas_call | solution.py:195
  40.3 6.9 %all-to-all-start.2 = ((f32[128,4,128]{2,1,0:T(4,128)}), f32[128,4,128]{2,1,0:T(4,128)S(1)}, u32[]{:S(2)}, u32[]{:S(2)}) async-start(f32[128,4,128]{2,1,0:T(4,128)} %bitcast.6), calls=%async_computation.2 | async-start | bytes 524288 | tf_op jit(solution)/shard_map/all_to_all | solution.py:611
  47.2 1.1 %shard_map.80 = (f32[4,216,256]{2,1,0:T(8,128)S(1)}, f32[32,128]{1,0:T(8,128)S(1)}, f32[32,128]{1,0:T(8,128)S(1)}, f32[32,128]{1,0:T(8,128)S(1)}, f32[32,128]{1,0:T(8,128)S(1)}) custom-call(f32[4,216,256]{2,1,0:T(8,128)S(1)} %get-tuple-element.47.refs_0_, f32[24,256]{1,0:T(8,128)S(1)} %get-tuple-element.39.refs_4_.refs_1_.refs_6_.refs_5_, ...), custom_call_target="tpu_custom_call" | custom-call | flops 50000000 | bytes 2000000 | tf_op jit(solution)/shard_map/pallas_call | solution.py:195
  48.3 0.1 collective-permute-start.4
  48.4 2.8 %collective-permute-start.5 = (f32[32,128]{1,0:T(8,128)S(1)}, f32[32,128]{1,0:T(8,128)S(1)}, u32[]{:S(2)}, u32[]{:S(2)}) collective-permute-start(f32[32,128]{1,0:T(8,128)S(1)} %get-tuple-element.51), channel_id=1, source_target_pairs={{0,8},{1,9},{2,10},{3,11},{4,12},{5,13},{6,14},{7,15},{8,0},{9,1},... | collective-permute-start | bytes 49160 | tf_op jit(solution)/shard_map/ppermute | solution.py:630
  51.2 0.0 collective-permute-start.6
  51.3 1.6 %collective-permute-start.7 = (f32[32,128]{1,0:T(8,128)S(1)}, f32[32,128]{1,0:T(8,128)S(1)}, u32[]{:S(2)}, u32[]{:S(2)}) collective-permute-start(f32[32,128]{1,0:T(8,128)S(1)} %get-tuple-element.53), channel_id=1, source_target_pairs={{0,1},{1,0},{2,3},{3,2},{4,5},{5,4},{6,7},{7,6},{8,9},{9,8},{10,11... | collective-permute-start | bytes 49160 | tf_op jit(solution)/shard_map/ppermute | solution.py:630
  52.8 2.0 %shard_map.81.refs_0_ = f32[4,216,256]{2,1,0:T(8,128)S(1)} custom-call(f32[4,216,256]{2,1,0:T(8,128)S(1)} %get-tuple-element.49.refs_0_, f32[4,216,256]{2,1,0:T(8,128)S(1)} %copy-done.1, bf16[240,216]{1,0:T(8,128)(2,1)S(1)} %copy-done.2, bf16[6,216,216]{2,1,0:T(8,128)(2,1)S(1)} %copy-done.3, s32[6,256]{1,0:T(8,128)S(1)} %copy-done.4, ...), custom_call_target="tpu_custom_call" | custom-call | flops 800000000 | bytes 2000000 | tf_op jit(solution)/shard_map/pallas_call | solution.py:195
  54.8 0.0 collective-permute-done.4.refs_1_
  54.8 0.2 collective-permute-done.6.refs_3_
  55.1 1.2 %shard_map.82 = (f32[4,216,256]{2,1,0:T(8,128)S(1)}, f32[128,256]{1,0:T(8,128)S(1)}) custom-call(f32[4,216,256]{2,1,0:T(8,128)S(1)} %shard_map.81.refs_0_, f32[32,128]{1,0:T(8,128)S(1)} %collective-permute-done.4.refs_1_, f32[32,128]{1,0:T(8,128)S(1)} %collective-permute-done.5.refs_2_, f32[32,128]{1,0:T(8,128)S(1)} %collective-permute-done.6.refs_3_, ...), custom_call_target="tpu_custom_call" | custom-call | flops 100000000 | bytes 2000000 | tf_op jit(solution)/shard_map/pallas_call | solution.py:195
  56.3 1.6 %all-to-all-done.2 = f32[128,4,128]{2,1,0:T(4,128)S(1)} async-done(((f32[128,4,128]{2,1,0:T(4,128)}), f32[128,4,128]{2,1,0:T(4,128)S(1)}, u32[]{:S(2)}, u32[]{:S(2)}) %all-to-all-start.2) | async-done | bytes 262176 | tf_op jit(solution)/shard_map/all_to_all | solution.py:611
  57.9 1.4 %shard_map.83 = (f32[128,128]{1,0:T(8,128)S(1)}, f32[512,128]{1,0:T(8,128)}) custom-call(f32[512,128]{1,0:T(8,128)S(1)} %bitcast.12, f32[104,256]{1,0:T(8,128)S(1)} %get-tuple-element.37.refs_7_.refs_1_, f32[8,256]{1,0:T(8,128)S(1)} %get-tuple-element.38.refs_2_, f32[128,256]{1,0:T(8,128)S(1)} %get-tuple-element.54.refs_3_), custom_call_target="tpu_custom_call" | custom-call | flops 100000000 | bytes 2000000 | tf_op jit(solution)/shard_map/pallas_call | solution.py:195
  59.4 7.3 %all-to-all-start.3 = ((f32[128,4,128]{2,1,0:T(4,128)}), f32[128,4,128]{2,1,0:T(4,128)S(1)}, u32[]{:S(2)}, u32[]{:S(2)}) async-start(f32[128,4,128]{2,1,0:T(4,128)} %bitcast.8), calls=%async_computation.3 | async-start | bytes 524288 | tf_op jit(solution)/shard_map/all_to_all | solution.py:611
  66.7 1.1 %shard_map.84 = (f32[4,216,256]{2,1,0:T(8,128)S(1)}, f32[32,128]{1,0:T(8,128)S(1)}, f32[32,128]{1,0:T(8,128)S(1)}, f32[32,128]{1,0:T(8,128)S(1)}, f32[32,128]{1,0:T(8,128)S(1)}) custom-call(f32[4,216,256]{2,1,0:T(8,128)S(1)} %get-tuple-element.56.refs_0_, f32[24,256]{1,0:T(8,128)S(1)} %get-tuple-element.39.refs_4_.refs_1_.refs_6_.refs_5_, ...), custom_call_target="tpu_custom_call" | custom-call | flops 50000000 | bytes 2000000 | tf_op jit(solution)/shard_map/pallas_call | solution.py:195
  67.8 0.1 collective-permute-start.8
  67.9 2.8 %collective-permute-start.9 = (f32[32,128]{1,0:T(8,128)S(1)}, f32[32,128]{1,0:T(8,128)S(1)}, u32[]{:S(2)}, u32[]{:S(2)}) collective-permute-start(f32[32,128]{1,0:T(8,128)S(1)} %get-tuple-element.60), channel_id=1, source_target_pairs={{0,8},{1,9},{2,10},{3,11},{4,12},{5,13},{6,14},{7,15},{8,0},{9,1},... | collective-permute-start | bytes 49160 | tf_op jit(solution)/shard_map/ppermute | solution.py:630
  70.7 0.0 collective-permute-start.10
  70.8 1.6 %collective-permute-start.11 = (f32[32,128]{1,0:T(8,128)S(1)}, f32[32,128]{1,0:T(8,128)S(1)}, u32[]{:S(2)}, u32[]{:S(2)}) collective-permute-start(f32[32,128]{1,0:T(8,128)S(1)} %get-tuple-element.62), channel_id=1, source_target_pairs={{0,1},{1,0},{2,3},{3,2},{4,5},{5,4},{6,7},{7,6},{8,9},{9,8},{10,11... | collective-permute-start | bytes 49160 | tf_op jit(solution)/shard_map/ppermute | solution.py:630
  72.3 2.0 %shard_map.85.refs_0_ = f32[4,216,256]{2,1,0:T(8,128)S(1)} custom-call(f32[4,216,256]{2,1,0:T(8,128)S(1)} %get-tuple-element.58.refs_0_, f32[4,216,256]{2,1,0:T(8,128)S(1)} %copy-done.1, bf16[240,216]{1,0:T(8,128)(2,1)S(1)} %copy-done.2, bf16[6,216,216]{2,1,0:T(8,128)(2,1)S(1)} %copy-done.3, s32[6,256]{1,0:T(8,128)S(1)} %copy-done.4, ...), custom_call_target="tpu_custom_call" | custom-call | flops 800000000 | bytes 2000000 | tf_op jit(solution)/shard_map/pallas_call | solution.py:195
  74.3 0.0 collective-permute-done.8.refs_1_
  74.3 0.0 collective-permute-done.9.refs_2_
  74.3 0.2 collective-permute-done.10.refs_3_
  74.5 0.7 shard_map.86.refs_3_
  75.3 2.2 %all-to-all-done.3 = f32[128,4,128]{2,1,0:T(4,128)S(1)} async-done(((f32[128,4,128]{2,1,0:T(4,128)}), f32[128,4,128]{2,1,0:T(4,128)S(1)}, u32[]{:S(2)}, u32[]{:S(2)}) %all-to-all-start.3) | async-done | bytes 262176 | tf_op jit(solution)/shard_map/all_to_all | solution.py:611
  77.4 1.8 %shard_map.87 = f32[4,216,256]{2,1,0:T(8,128)} custom-call(f32[512,128]{1,0:T(8,128)S(1)} %bitcast.11, f32[104,256]{1,0:T(8,128)S(1)} %get-tuple-element.37.refs_7_.refs_1_, f32[8,256]{1,0:T(8,128)S(1)} %get-tuple-element.38.refs_2_, f32[4,216,256]{2,1,0:T(8,128)S(1)} %shard_map.86.refs_3_, f32[24,256]{1,0:T(8,128)S(1)} %get-tuple-element.39.refs_4_.refs_1_.refs_6_.refs_5_, ...), custom_call_target="tpu_custom_call" | custom-call | flops 100000000 | bytes 2000000 | tf_op jit(solution)/shard_map/pallas_call | solution.py:195
  (15 shorter events, 0.0 us)
Async XLA Ops:
  0.0 0.7 copy-start.7
  0.7 12.0 %copy-start.5 = (s32[3,512]{1,0:T(4,128)S(1)}, s32[3,512]{1,0:T(4,128)}, u32[]{:S(2)}) copy-start(s32[3,512]{1,0:T(4,128)} %refs_1_.4) | copy-start | bytes 18436
  1.5 11.2 %copy-start.2 = (bf16[240,216]{1,0:T(8,128)(2,1)S(1)}, bf16[240,216]{1,0:T(8,128)(2,1)}, u32[]{:S(2)}) copy-start(bf16[240,216]{1,0:T(8,128)(2,1)} %constant.4.clone.refs_4_.refs_1_.refs_2_.refs_5_) | copy-start | bytes 311044
  1.5 11.2 %copy-start.4 = (s32[6,256]{1,0:T(8,128)S(1)}, s32[6,256]{1,0:T(8,128)}, u32[]{:S(2)}) copy-start(s32[6,256]{1,0:T(8,128)} %refs_4_.4) | copy-start | bytes 18436
  1.5 20.4 %all-to-all-start = ((f32[128,1,128]{2,1,0:T(1,128)}), f32[128,1,128]{2,1,0:T(1,128)S(1)}, u32[]{:S(2)}, u32[]{:S(2)}) async-start(f32[128,1,128]{2,1,0:T(1,128)} %bitcast.1), calls=%async_computation | async-start | bytes 131072 | tf_op jit(solution)/shard_map/all_to_all | solution.py:611
  12.7 0.7 copy-start.6
  13.4 1.2 %copy-start = (f32[4,216,256]{2,1,0:T(8,128)S(1)}, f32[4,216,256]{2,1,0:T(8,128)}, u32[]{:S(2)}) copy-start(f32[4,216,256]{2,1,0:T(8,128)} %refs_1_.6) | copy-start | bytes 2654212
  14.5 13.6 %copy-start.1 = (f32[4,216,256]{2,1,0:T(8,128)S(1)}, f32[4,216,256]{2,1,0:T(8,128)}, u32[]{:S(2)}) copy-start(f32[4,216,256]{2,1,0:T(8,128)} %refs_1_.6) | copy-start | bytes 2654212
  23.4 10.0 %copy-start.3 = (bf16[6,216,216]{2,1,0:T(8,128)(2,1)S(1)}, bf16[6,216,216]{2,1,0:T(8,128)(2,1)}, u32[]{:S(2)}) copy-start(bf16[6,216,216]{2,1,0:T(8,128)(2,1)} %constant.5.clone.refs_2_.refs_3_) | copy-start | bytes 1679620
  23.4 15.5 %all-to-all-start.1 = ((f32[128,4,128]{2,1,0:T(4,128)}), f32[128,4,128]{2,1,0:T(4,128)S(1)}, u32[]{:S(2)}, u32[]{:S(2)}) async-start(f32[128,4,128]{2,1,0:T(4,128)} %bitcast.4), calls=%async_computation.1 | async-start | bytes 524288 | tf_op jit(solution)/shard_map/all_to_all | solution.py:611
  28.9 6.5 %collective-permute-start = (f32[32,128]{1,0:T(8,128)S(1)}, f32[32,128]{1,0:T(8,128)S(1)}, u32[]{:S(2)}, u32[]{:S(2)}) collective-permute-start(f32[32,128]{1,0:T(8,128)S(1)} %get-tuple-element.41), channel_id=1, source_target_pairs={{0,1},{1,0},{2,3},{3,2},{4,5},{5,4},{6,7},{7,6},{8,16},{9,17},{10,... | collective-permute-start | bytes 49160 | tf_op jit(solution)/shard_map/ppermute | solution.py:630
  28.9 6.4 %collective-permute-start.1 = (f32[32,128]{1,0:T(8,128)S(1)}, f32[32,128]{1,0:T(8,128)S(1)}, u32[]{:S(2)}, u32[]{:S(2)}) collective-permute-start(f32[32,128]{1,0:T(8,128)S(1)} %get-tuple-element.42), channel_id=1, source_target_pairs={{0,8},{1,9},{2,10},{3,11},{4,12},{5,13},{6,14},{7,15},{8,0},{9,1},... | collective-permute-start | bytes 49160 | tf_op jit(solution)/shard_map/ppermute | solution.py:630
  31.7 3.8 %collective-permute-start.2 = (f32[32,128]{1,0:T(8,128)S(1)}, f32[32,128]{1,0:T(8,128)S(1)}, u32[]{:S(2)}, u32[]{:S(2)}) collective-permute-start(f32[32,128]{1,0:T(8,128)S(1)} %get-tuple-element.43), channel_id=1, source_target_pairs={{0,8},{1,2},{2,1},{3,4},{4,3},{5,6},{6,5},{7,15},{8,0},{9,10},{10,... | collective-permute-start | bytes 49160 | tf_op jit(solution)/shard_map/ppermute | solution.py:630
  31.8 3.7 %collective-permute-start.3 = (f32[32,128]{1,0:T(8,128)S(1)}, f32[32,128]{1,0:T(8,128)S(1)}, u32[]{:S(2)}, u32[]{:S(2)}) collective-permute-start(f32[32,128]{1,0:T(8,128)S(1)} %get-tuple-element.44), channel_id=1, source_target_pairs={{0,1},{1,0},{2,3},{3,2},{4,5},{5,4},{6,7},{7,6},{8,9},{9,8},{10,11... | collective-permute-start | bytes 49160 | tf_op jit(solution)/shard_map/ppermute | solution.py:630
  40.3 17.6 %all-to-all-start.2 = ((f32[128,4,128]{2,1,0:T(4,128)}), f32[128,4,128]{2,1,0:T(4,128)S(1)}, u32[]{:S(2)}, u32[]{:S(2)}) async-start(f32[128,4,128]{2,1,0:T(4,128)} %bitcast.6), calls=%async_computation.2 | async-start | bytes 524288 | tf_op jit(solution)/shard_map/all_to_all | solution.py:611
  48.3 6.5 %collective-permute-start.4 = (f32[32,128]{1,0:T(8,128)S(1)}, f32[32,128]{1,0:T(8,128)S(1)}, u32[]{:S(2)}, u32[]{:S(2)}) collective-permute-start(f32[32,128]{1,0:T(8,128)S(1)} %get-tuple-element.50), channel_id=1, source_target_pairs={{0,1},{1,0},{2,3},{3,2},{4,5},{5,4},{6,7},{7,6},{8,16},{9,17},{10,... | collective-permute-start | bytes 49160 | tf_op jit(solution)/shard_map/ppermute | solution.py:630
  48.4 6.4 %collective-permute-start.5 = (f32[32,128]{1,0:T(8,128)S(1)}, f32[32,128]{1,0:T(8,128)S(1)}, u32[]{:S(2)}, u32[]{:S(2)}) collective-permute-start(f32[32,128]{1,0:T(8,128)S(1)} %get-tuple-element.51), channel_id=1, source_target_pairs={{0,8},{1,9},{2,10},{3,11},{4,12},{5,13},{6,14},{7,15},{8,0},{9,1},... | collective-permute-start | bytes 49160 | tf_op jit(solution)/shard_map/ppermute | solution.py:630
  51.2 3.8 %collective-permute-start.6 = (f32[32,128]{1,0:T(8,128)S(1)}, f32[32,128]{1,0:T(8,128)S(1)}, u32[]{:S(2)}, u32[]{:S(2)}) collective-permute-start(f32[32,128]{1,0:T(8,128)S(1)} %get-tuple-element.52), channel_id=1, source_target_pairs={{0,8},{1,2},{2,1},{3,4},{4,3},{5,6},{6,5},{7,15},{8,0},{9,10},{10,... | collective-permute-start | bytes 49160 | tf_op jit(solution)/shard_map/ppermute | solution.py:630
  51.3 3.8 %collective-permute-start.7 = (f32[32,128]{1,0:T(8,128)S(1)}, f32[32,128]{1,0:T(8,128)S(1)}, u32[]{:S(2)}, u32[]{:S(2)}) collective-permute-start(f32[32,128]{1,0:T(8,128)S(1)} %get-tuple-element.53), channel_id=1, source_target_pairs={{0,1},{1,0},{2,3},{3,2},{4,5},{5,4},{6,7},{7,6},{8,9},{9,8},{10,11... | collective-permute-start | bytes 49160 | tf_op jit(solution)/shard_map/ppermute | solution.py:630
  59.4 18.1 %all-to-all-start.3 = ((f32[128,4,128]{2,1,0:T(4,128)}), f32[128,4,128]{2,1,0:T(4,128)S(1)}, u32[]{:S(2)}, u32[]{:S(2)}) async-start(f32[128,4,128]{2,1,0:T(4,128)} %bitcast.8), calls=%async_computation.3 | async-start | bytes 524288 | tf_op jit(solution)/shard_map/all_to_all | solution.py:611
  67.8 6.5 %collective-permute-start.8 = (f32[32,128]{1,0:T(8,128)S(1)}, f32[32,128]{1,0:T(8,128)S(1)}, u32[]{:S(2)}, u32[]{:S(2)}) collective-permute-start(f32[32,128]{1,0:T(8,128)S(1)} %get-tuple-element.59), channel_id=1, source_target_pairs={{0,1},{1,0},{2,3},{3,2},{4,5},{5,4},{6,7},{7,6},{8,16},{9,17},{10,... | collective-permute-start | bytes 49160 | tf_op jit(solution)/shard_map/ppermute | solution.py:630
  67.9 6.4 %collective-permute-start.9 = (f32[32,128]{1,0:T(8,128)S(1)}, f32[32,128]{1,0:T(8,128)S(1)}, u32[]{:S(2)}, u32[]{:S(2)}) collective-permute-start(f32[32,128]{1,0:T(8,128)S(1)} %get-tuple-element.60), channel_id=1, source_target_pairs={{0,8},{1,9},{2,10},{3,11},{4,12},{5,13},{6,14},{7,15},{8,0},{9,1},... | collective-permute-start | bytes 49160 | tf_op jit(solution)/shard_map/ppermute | solution.py:630
  70.7 3.8 %collective-permute-start.10 = (f32[32,128]{1,0:T(8,128)S(1)}, f32[32,128]{1,0:T(8,128)S(1)}, u32[]{:S(2)}, u32[]{:S(2)}) collective-permute-start(f32[32,128]{1,0:T(8,128)S(1)} %get-tuple-element.61), channel_id=1, source_target_pairs={{0,8},{1,2},{2,1},{3,4},{4,3},{5,6},{6,5},{7,15},{8,0},{9,10},{10,... | collective-permute-start | bytes 49160 | tf_op jit(solution)/shard_map/ppermute | solution.py:630
  70.8 3.8 %collective-permute-start.11 = (f32[32,128]{1,0:T(8,128)S(1)}, f32[32,128]{1,0:T(8,128)S(1)}, u32[]{:S(2)}, u32[]{:S(2)}) collective-permute-start(f32[32,128]{1,0:T(8,128)S(1)} %get-tuple-element.62), channel_id=1, source_target_pairs={{0,1},{1,0},{2,3},{3,2},{4,5},{5,4},{6,7},{7,6},{8,9},{9,8},{10,11... | collective-permute-start | bytes 49160 | tf_op jit(solution)/shard_map/ppermute | solution.py:630
